TPU v7x, 512 devices: a whole 4x4x16 slice. The times are simulated.
512 devices in a mesh: orig: 128 (over y, z, core), link: 4 (over x).
Axes of the slice: x: 4, y: 4, z: 16, core: 2. Of those that a mesh axis runs over, the one named last changes fastest.
Arguments:
- background: bfloat16 [262144, 256], P('orig'), may hold values from -6 to 6
- live_counts: int32 [2048], P('orig'), may hold values from 1 to 128
- patterns: bfloat16 [4, 4096, 128, 128], P('link', 'orig'), may hold values from -0.009765625 to 0.009765625
- pattern_ids: int32 [4, 2048, 12], P('link', 'orig'), may hold values from 0 to 31
- link_targets: int32 [4, 2048, 12], P('link', 'orig'), may hold values from 0 to 7
- counts_obs: float32 [4, 1024], P('link', 'orig'), may hold values from -6 to 6
- obs_var: float32 [4, 1024], P('link', 'orig'), may hold values from 1 to 10
Outputs:
- analysis: bfloat16 [262144, 256], P(('orig', 'link'))
All inputs are finite; a program needn't handle non-finite values. Where the computation divides by a largest or mean magnitude, that divisor is 1e-20 or more.
Results may differ from a plain program's by a relative error of at most 0.001.
Values sent between devices are 32-bit elements; how exact they have to be, the bound alone decides.
No kernel may reach another device: no remote copies, remote signals or barrier semaphores. Data moves between devices by JAX's collectives and lax.ppermute only.
A program may use at most 64 MiB of HBM per device.

v0:
```python
import jax
import jax.numpy as jnp
from jax import lax
from jax.sharding import Mesh
from jax.sharding import PartitionSpec as P

NLB = 8
NS_ITERS = 4
ORIG = ("orig_0", "orig_1", "orig_2")
ORIG_LINK = ("orig_0", "orig_1", "orig_2", "link")


def rows_for(lines, peers):
    spare = -lines.shape[0] % peers
    if not spare:
        return lines
    return jnp.concatenate([lines, jnp.zeros((spare, *lines.shape[1:]), lines.dtype)])


def from_everyone(x, axis):
    copies = jnp.broadcast_to(x, (lax.axis_size(axis), *x.shape))
    return lax.all_to_all(copies, axis, split_axis=0, concat_axis=0, tiled=True)


def in_order(blocks, dim):
    dims = list(blocks.shape[1:])
    dims[dim] *= blocks.shape[0]
    return jnp.moveaxis(blocks, 0, dim).reshape(dims)


def gather_axes(x, axes, dim):
    far, near = axes
    leading = from_everyone(x, far)
    blocks = jnp.swapaxes(from_everyone(leading, near), 0, 1)
    return in_order(blocks.reshape(-1, *x.shape), dim)


def cut_along(x, dim, peers):
    dims = x.shape
    blocks = x.reshape(*dims[:dim], peers, dims[dim] // peers, *dims[dim + 1 :])
    return jnp.moveaxis(blocks, dim, 0)


def sum_at_owner(x, axis, dim):
    blocks = cut_along(x, dim, lax.axis_size(axis))
    arrived = lax.all_to_all(blocks, axis, split_axis=0, concat_axis=0, tiled=True)
    return arrived.sum(axis=0)


def sum_by_axis(x, axes, dim):
    far, near = axes
    own = sum_at_owner(cut_along(x, dim, lax.axis_size(far)), near, dim + 1)
    return jnp.sum(lax.all_to_all(own, far, 0, 0, tiled=True), axis=0)


def nested_sum(x, axes):
    lines = x.reshape(-1, x.shape[-1])
    padded = rows_for(lines, lax.axis_size(axes[0]) * lax.axis_size(axes[1]))
    whole = gather_axes(sum_by_axis(padded, axes, 0), axes, 0)
    return lax.slice_in_dim(whole, 0, len(lines)).reshape(x.shape)


def over_copies(x, axis):
    return from_everyone(x, axis).sum(axis=0)


def together(arrays, axis):
    ravelled, at, done = (jnp.concatenate([a.reshape(-1) for a in arrays]), 0, [])
    so_far = over_copies(ravelled, axis)
    for a in arrays:
        done.append(so_far[at : at + a.size].reshape(a.shape))
        at += a.size
    return tuple(done)


def transform_of(ensemble_gram, forcing):
    members = ensemble_gram.shape[0]
    identity = jnp.eye(members, dtype=jnp.float32)
    system = identity + ensemble_gram / (members - 1.0)
    row_bound = jnp.max(jnp.sum(jnp.abs(system), axis=1))
    square_root = system / row_bound
    inverse = identity
    for sweep_index in range(NS_ITERS):
        middle = 0.5 * (
            3.0 * identity - jnp.dot(inverse, square_root, precision=lax.Precision.HIGHEST)
        )
        square_root = jnp.dot(square_root, middle, precision=lax.Precision.HIGHEST)
        inverse = jnp.dot(middle, inverse, precision=lax.Precision.HIGHEST)
    spread_weights = inverse / jnp.sqrt(row_bound)
    inner = jnp.dot(inverse, forcing, precision=lax.Precision.HIGHEST)
    mean_weights = jnp.dot(inverse, inner, precision=lax.Precision.HIGHEST) / (
        row_bound * (members - 1.0)
    )
    return spread_weights + mean_weights[:, None]


def per_device(background, live_counts, patterns, pattern_ids, link_targets, counts_obs, obs_var):
    n_link = lax.axis_size("link")
    states_dev, members = background.shape
    blocks_dev = live_counts.shape[0]
    block_rows = states_dev // blocks_dev
    tile_bank = patterns[0].astype(jnp.float32)
    stored = tile_bank.shape[0]
    link_rows = tile_bank.shape[1]
    position = jnp.arange(block_rows, dtype=jnp.int32)
    living = position[None, :] < live_counts[:, None]
    masked = background.reshape(blocks_dev, block_rows, members) * living[:, :, None].astype(
        jnp.bfloat16
    )
    block_numbers = jnp.arange(NLB, dtype=jnp.int32)
    tile_numbers = jnp.arange(stored, dtype=jnp.int32)
    target_hit = (link_targets[0][:, :, None] == block_numbers[None, None, :]).astype(jnp.float32)
    tile_hit = (pattern_ids[0][:, :, None] == tile_numbers[None, None, :]).astype(jnp.float32)
    tile_counts = jnp.einsum("btj,btp->bjp", target_hit, tile_hit)
    group_size = 4
    steps_count = blocks_dev // group_size

    def add_group(running, inputs):
        counts_part, states_part = inputs
        combined = jnp.einsum(
            "bjp,pls->bjls", counts_part, tile_bank, precision=lax.Precision.HIGHEST
        )
        return (
            running
            + jnp.einsum(
                "bjls,bsm->jlm",
                combined,
                states_part.astype(jnp.float32),
                precision=lax.Precision.HIGHEST,
            ),
            None,
        )

    start = jnp.zeros((NLB, link_rows, members), jnp.float32)
    grouped_counts = tile_counts.reshape(steps_count, group_size, NLB, stored)
    grouped_states = masked.reshape(steps_count, group_size, block_rows, members)
    total, unused = lax.scan(add_group, start, (grouped_counts, grouped_states))
    group_term = total.reshape(NLB * link_rows, members)
    whole_group = nested_sum(group_term, (("orig_0", "orig_1"), "orig_2"))
    counts_group, var_group = (
        gather_axes(counts_obs[0], (("orig_0", "orig_1"), "orig_2"), 0),
        gather_axes(obs_var[0], (("orig_0", "orig_1"), "orig_2"), 0),
    )
    group_mean = jnp.mean(whole_group, axis=1)
    group_spread = whole_group - group_mean[:, None]
    group_weights = 1.0 / var_group
    group_weighted = group_weights * (counts_group - group_mean)
    part_gram = jnp.dot(
        group_spread.T, group_spread * group_weights[:, None], precision=lax.Precision.HIGHEST
    )
    part_forcing = jnp.dot(group_spread.T, group_weighted, precision=lax.Precision.HIGHEST)
    ensemble_gram, forcing = together((part_gram, part_forcing), "link")
    transform_mat = transform_of(ensemble_gram, forcing)
    own_rows = states_dev // n_link
    first_row = lax.axis_index("link") * own_rows
    state_rows = lax.dynamic_slice_in_dim(background, first_row, own_rows, 0).astype(jnp.float32)
    live_rows = lax.dynamic_slice_in_dim(living.reshape(states_dev), first_row, own_rows, 0)
    centre = jnp.mean(state_rows, axis=1, keepdims=True)
    updated = centre + jnp.dot(state_rows - centre, transform_mat, precision=lax.Precision.HIGHEST)
    return jnp.where(live_rows[:, None], updated, state_rows).astype(jnp.bfloat16)


def solution(mesh):
    torus = Mesh(
        mesh.devices.reshape(4, 16, 2, mesh.shape["link"]), ("orig_0", "orig_1", "orig_2", "link")
    )
    return jax.shard_map(
        per_device,
        mesh=torus,
        in_specs=(
            P(ORIG, None),
            P(ORIG),
            P("link", ORIG, None, None),
            P("link", ORIG, None),
            P("link", ORIG, None),
            P("link", ORIG),
            P("link", ORIG),
        ),
        out_specs=P(ORIG_LINK, None),
        check_vma=False,
    )
```

profile of v0, /device:TPU:1, one launch (start us, length us, event | category | flops | bytes accessed | tf_op | source)
XLA Modules:
  0.0 210.6 jit_solution(2808892868382646930)
XLA Ops:
  0.0 3.3 %bitcast_convert_fusion = f32[32,128,128]{2,0,1:T(8,128)} fusion(bf16[1,32,128,128]{3,2,1,0:T(8,128)(2,1)} %param.11), kind=kLoop, calls=%fused_computation.28 | loop fusion | flops 524288 | bytes 3145728 | tf_op jit(solution)/shard_map/convert_element_type | solution.py:102
  5.2 25.1 %while.11 = (s32[]{:T(128)}, f32[8,128,256]{2,1,0:T(8,128)S(1)}, f32[4,4,8,32]{3,2,1,0:T(8,128)S(1)}, f32[32,128,128]{2,0,1:T(8,128)}, bf16[4,4,128,256]{3,2,1,0:T(8,128)(2,1)}, /*index=5*/s32[]{:T(128)}, s32[]{:T(128)}) while((s32[]{:T(128)}, f32[8,128,256]{2,1,0:T(8,128)S(1)}, f32[4,4,8,32]{3,2,1,0:T(8,128)S(1)}, ...), condition=%wide.region_2.3_spmd.clone, body=%wide.region_1.2_spmd.clone.sunk | while | flops 1812463616 | bytes 8667739 | solution.py:137
  5.2 3.4 %fusion.88 = f32[4,8,128,128]{3,1,2,0:T(8,128)S(1)} fusion(f32[32,128,128]{2,0,1:T(8,128)} %get-tuple-element.109, f32[4,4,8,32]{3,2,1,0:T(8,128)S(1)} %get-tuple-element.108, s32[]{:T(128)} %get-tuple-element.99), kind=kOutput, calls=%fused_computation.clone.1 | convolution fusion | flops 201326592 | bytes 4210692 | tf_op jit(solution)/shard_map/while/body/eval_jaxpr/bjp,pls->bjls/dot_general | solution.py:120
  8.6 2.8 %fusion.89 = f32[8,128,256]{2,1,0:T(8,128)S(1)} fusion(f32[4,8,128,128]{3,1,2,0:T(8,128)S(1)} %fusion.88, f32[8,128,256]{2,1,0:T(8,128)S(1)} %get-tuple-element.100, pred[]{:T(512)S(6)} %compare.3, bf16[4,4,128,256]{3,2,1,0:T(8,128)(2,1)} %get-tuple-element.110, s32[]{:T(128)} %get-tuple-element.99), kind=kOutput, calls=%fused_computation.5.clone.1 | convolution fusion | flops 1611137024 | bytes 4456961 | tf_op jit(solution)/shard_map/while/body/eval_jaxpr/bjls,bsm->jlm/dot_general | solution.py:125
  11.5 3.4 %fusion.88 = f32[4,8,128,128]{3,1,2,0:T(8,128)S(1)} fusion(f32[32,128,128]{2,0,1:T(8,128)} %get-tuple-element.109, f32[4,4,8,32]{3,2,1,0:T(8,128)S(1)} %get-tuple-element.108, s32[]{:T(128)} %get-tuple-element.99), kind=kOutput, calls=%fused_computation.clone.1 | convolution fusion | flops 201326592 | bytes 4210692 | tf_op jit(solution)/shard_map/while/body/eval_jaxpr/bjp,pls->bjls/dot_general | solution.py:120
  14.9 2.8 %fusion.89 = f32[8,128,256]{2,1,0:T(8,128)S(1)} fusion(f32[4,8,128,128]{3,1,2,0:T(8,128)S(1)} %fusion.88, f32[8,128,256]{2,1,0:T(8,128)S(1)} %get-tuple-element.100, pred[]{:T(512)S(6)} %compare.3, bf16[4,4,128,256]{3,2,1,0:T(8,128)(2,1)} %get-tuple-element.110, s32[]{:T(128)} %get-tuple-element.99), kind=kOutput, calls=%fused_computation.5.clone.1 | convolution fusion | flops 1611137024 | bytes 4456961 | tf_op jit(solution)/shard_map/while/body/eval_jaxpr/bjls,bsm->jlm/dot_general | solution.py:125
  17.8 3.4 %fusion.88 = f32[4,8,128,128]{3,1,2,0:T(8,128)S(1)} fusion(f32[32,128,128]{2,0,1:T(8,128)} %get-tuple-element.109, f32[4,4,8,32]{3,2,1,0:T(8,128)S(1)} %get-tuple-element.108, s32[]{:T(128)} %get-tuple-element.99), kind=kOutput, calls=%fused_computation.clone.1 | convolution fusion | flops 201326592 | bytes 4210692 | tf_op jit(solution)/shard_map/while/body/eval_jaxpr/bjp,pls->bjls/dot_general | solution.py:120
  21.2 2.8 %fusion.89 = f32[8,128,256]{2,1,0:T(8,128)S(1)} fusion(f32[4,8,128,128]{3,1,2,0:T(8,128)S(1)} %fusion.88, f32[8,128,256]{2,1,0:T(8,128)S(1)} %get-tuple-element.100, pred[]{:T(512)S(6)} %compare.3, bf16[4,4,128,256]{3,2,1,0:T(8,128)(2,1)} %get-tuple-element.110, s32[]{:T(128)} %get-tuple-element.99), kind=kOutput, calls=%fused_computation.5.clone.1 | convolution fusion | flops 1611137024 | bytes 4456961 | tf_op jit(solution)/shard_map/while/body/eval_jaxpr/bjls,bsm->jlm/dot_general | solution.py:125
  24.0 3.4 %fusion.88 = f32[4,8,128,128]{3,1,2,0:T(8,128)S(1)} fusion(f32[32,128,128]{2,0,1:T(8,128)} %get-tuple-element.109, f32[4,4,8,32]{3,2,1,0:T(8,128)S(1)} %get-tuple-element.108, s32[]{:T(128)} %get-tuple-element.99), kind=kOutput, calls=%fused_computation.clone.1 | convolution fusion | flops 201326592 | bytes 4210692 | tf_op jit(solution)/shard_map/while/body/eval_jaxpr/bjp,pls->bjls/dot_general | solution.py:120
  27.5 2.8 %fusion.89 = f32[8,128,256]{2,1,0:T(8,128)S(1)} fusion(f32[4,8,128,128]{3,1,2,0:T(8,128)S(1)} %fusion.88, f32[8,128,256]{2,1,0:T(8,128)S(1)} %get-tuple-element.100, pred[]{:T(512)S(6)} %compare.3, bf16[4,4,128,256]{3,2,1,0:T(8,128)(2,1)} %get-tuple-element.110, s32[]{:T(128)} %get-tuple-element.99), kind=kOutput, calls=%fused_computation.5.clone.1 | convolution fusion | flops 1611137024 | bytes 4456961 | tf_op jit(solution)/shard_map/while/body/eval_jaxpr/bjls,bsm->jlm/dot_general | solution.py:125
  30.4 11.1 %all_to_all.54 = f32[2,64,8,256]{3,2,1,0:T(8,128)S(1)} all-to-all(f32[2,64,8,256]{3,2,1,0:T(8,128)S(1)} %copy.50), channel_id=1, replica_groups=mesh['orig_0'=4,'orig_1'=16,'orig_2'=2,'link'=4] {'orig_2'}, dimensions={0} | all-to-all | bytes 2097152 | tf_op jit(solution)/shard_map/all_to_all | solution.py:46
  41.5 26.2 %all_to_all.55 = f32[64,1,8]{2,1,0:T(1,128)S(1)} all-to-all(f32[64,1,8]{2,1,0:T(1,128)S(1)} %broadcast_in_dim.46), channel_id=1, replica_groups=mesh['orig_0'=4,'orig_1'=16,'orig_2'=2,'link'=4] {'orig_0','orig_1'}, dimensions={0} | all-to-all | bytes 4096 | tf_op jit(solution)/shard_map/all_to_all | solution.py:22
  68.3 4.6 %all-to-all-start.6 = ((f32[64,1,8]{2,1,0:T(1,128)}), f32[64,1,8]{2,1,0:T(1,128)S(1)}, u32[]{:S(2)}, u32[]{:S(2)}) async-start(f32[64,1,8]{2,1,0:T(1,128)} %broadcast_in_dim.48), calls=%async_computation.6 | async-start | bytes 65536 | tf_op jit(solution)/shard_map/all_to_all | solution.py:22
  73.8 12.3 %all-to-all-done.6 = f32[64,1,8]{2,1,0:T(1,128)S(1)} async-done(((f32[64,1,8]{2,1,0:T(1,128)}), f32[64,1,8]{2,1,0:T(1,128)S(1)}, u32[]{:S(2)}, u32[]{:S(2)}) %all-to-all-start.6) | async-done | bytes 2080 | tf_op jit(solution)/shard_map/all_to_all | solution.py:22
  86.2 4.6 %all-to-all-start.1 = ((f32[64,8,256]{2,1,0:T(8,128)}), f32[64,8,256]{2,1,0:T(8,128)S(1)}, u32[]{:S(2)}, u32[]{:S(2)}) async-start(f32[64,8,256]{2,1,0:T(8,128)} %reduce_sum.55), calls=%async_computation.1 | async-start | bytes 1048576 | tf_op jit(solution)/shard_map/all_to_all | solution.py:53
  91.7 26.8 %all-to-all-done.1 = f32[64,8,256]{2,1,0:T(8,128)S(1)} async-done(((f32[64,8,256]{2,1,0:T(8,128)}), f32[64,8,256]{2,1,0:T(8,128)S(1)}, u32[]{:S(2)}, u32[]{:S(2)}) %all-to-all-start.1) | async-done | bytes 524320 | tf_op jit(solution)/shard_map/all_to_all | solution.py:53
  118.5 8.1 %all-to-all-start.5 = ((f32[2,1,512]{2,1,0:T(1,128)}), f32[2,1,512]{2,1,0:T(1,128)S(1)}, u32[]{:S(2)}, u32[]{:S(2)}) async-start(f32[2,1,512]{2,1,0:T(1,128)} %reshape.125), calls=%async_computation.5 | async-start | bytes 8192 | tf_op jit(solution)/shard_map/all_to_all | solution.py:22
  127.7 3.7 %all_to_all.56 = f32[2,1,512]{2,1,0:T(1,128)S(1)} all-to-all(f32[2,1,512]{2,1,0:T(1,128)S(1)} %reshape.127), channel_id=1, replica_groups=mesh['orig_0'=4,'orig_1'=16,'orig_2'=2,'link'=4] {'orig_2'}, dimensions={0} | all-to-all | bytes 8192 | tf_op jit(solution)/shard_map/all_to_all | solution.py:22
  132.2 6.6 %all-to-all-start.2 = ((f32[64,8,256]{2,1,0:T(8,128)}), f32[64,8,256]{2,1,0:T(8,128)S(1)}, u32[]{:S(2)}, u32[]{:S(2)}) async-start(f32[64,8,256]{2,1,0:T(8,128)} %broadcast_in_dim.44), calls=%async_computation.2 | async-start | bytes 1048576 | tf_op jit(solution)/shard_map/all_to_all | solution.py:22
  141.3 27.3 %all-to-all-done.2 = f32[64,8,256]{2,1,0:T(8,128)S(1)} async-done(((f32[64,8,256]{2,1,0:T(8,128)}), f32[64,8,256]{2,1,0:T(8,128)S(1)}, u32[]{:S(2)}, u32[]{:S(2)}) %all-to-all-start.2) | async-done | bytes 524320 | tf_op jit(solution)/shard_map/all_to_all | solution.py:22
  168.6 7.3 %all_to_all.57 = f32[2,64,8,256]{3,2,1,0:T(8,128)S(1)} all-to-all(f32[2,64,8,256]{3,2,1,0:T(8,128)S(1)} %broadcast_in_dim.45), channel_id=1, replica_groups=mesh['orig_0'=4,'orig_1'=16,'orig_2'=2,'link'=4] {'orig_2'}, dimensions={0} | all-to-all | bytes 2097152 | tf_op jit(solution)/shard_map/all_to_all | solution.py:22
  176.4 2.3 %fusion.20 = f32[32,2,8,128]{3,2,1,0:T(8,128)S(1)} fusion(f32[64,2,8]{2,1,0:T(2,128)S(1)} %copy.53, f32[64,2,8]{2,1,0:T(2,128)S(1)} %broadcast_multiply_fusion.1, f32[2,64,8,256]{3,2,1,0:T(8,128)S(1)} %all_to_all.57), kind=kOutput, calls=%fused_computation.17 | convolution fusion | flops 806092800 | bytes 1318912 | tf_op jit(solution)/shard_map/dot_general | solution.py:148
  181.3 4.0 %all-to-all-start.8 = ((f32[4,1,65792]{2,1,0:T(1,128)}), f32[4,1,65792]{2,1,0:T(1,128)S(1)}, u32[]{:S(2)}, u32[]{:S(2)}) async-start(f32[4,1,65792]{2,1,0:T(1,128)} %broadcast_in_dim.50), calls=%async_computation.8 | async-start | bytes 2105344 | tf_op jit(solution)/shard_map/all_to_all | solution.py:22
  185.7 14.3 %all-to-all-done.8 = f32[4,1,65792]{2,1,0:T(1,128)S(1)} async-done(((f32[4,1,65792]{2,1,0:T(1,128)}), f32[4,1,65792]{2,1,0:T(1,128)S(1)}, u32[]{:S(2)}, u32[]{:S(2)}) %all-to-all-start.8) | async-done | bytes 1052704 | tf_op jit(solution)/shard_map/all_to_all | solution.py:22
  (81 shorter events, 21.3 us)
Async XLA Ops:
  0.0 3.3 %copy-start.4 = (s32[16]{0:T(128)S(1)}, s32[16]{0:T(128)}, u32[]{:S(2)}) copy-start(s32[16]{0:T(128)} %param.10) | copy-start | bytes 196
  0.0 3.5 %copy-start.2 = (s32[1,16,12]{1,0,2:T(1,128)S(1)}, s32[1,16,12]{1,0,2:T(1,128)}, u32[]{:S(2)}) copy-start(s32[1,16,12]{1,0,2:T(1,128)} %param.13) | copy-start | bytes 2308
  0.0 3.6 %copy-start.3 = (s32[1,16,12]{1,0,2:T(1,128)S(1)}, s32[1,16,12]{1,0,2:T(1,128)}, u32[]{:S(2)}) copy-start(s32[1,16,12]{1,0,2:T(1,128)} %param.12) | copy-start | bytes 2308
  0.0 3.6 %copy-start = (bf16[2048,256]{1,0:T(8,128)(2,1)S(1)}, bf16[2048,256]{1,0:T(8,128)(2,1)}, u32[]{:S(2)}) copy-start(bf16[2048,256]{1,0:T(8,128)(2,1)} %param.9) | copy-start | bytes 3145732
  30.3 11.2 %copy-start.5 = (f32[1,8]{1,0:T(1,128)S(1)}, f32[1,8]{1,0:T(1,128)}, u32[]{:S(2)}) copy-start(f32[1,8]{1,0:T(1,128)} %param.15) | copy-start | bytes 100
  30.3 37.4 %copy-start.6 = (f32[1,8]{1,0:T(1,128)S(1)}, f32[1,8]{1,0:T(1,128)}, u32[]{:S(2)}) copy-start(f32[1,8]{1,0:T(1,128)} %param.14) | copy-start | bytes 100
  68.3 17.8 %all-to-all-start.6 = ((f32[64,1,8]{2,1,0:T(1,128)}), f32[64,1,8]{2,1,0:T(1,128)S(1)}, u32[]{:S(2)}, u32[]{:S(2)}) async-start(f32[64,1,8]{2,1,0:T(1,128)} %broadcast_in_dim.48), calls=%async_computation.6 | async-start | bytes 65536 | tf_op jit(solution)/shard_map/all_to_all | solution.py:22
  86.2 32.4 %all-to-all-start.1 = ((f32[64,8,256]{2,1,0:T(8,128)}), f32[64,8,256]{2,1,0:T(8,128)S(1)}, u32[]{:S(2)}, u32[]{:S(2)}) async-start(f32[64,8,256]{2,1,0:T(8,128)} %reduce_sum.55), calls=%async_computation.1 | async-start | bytes 1048576 | tf_op jit(solution)/shard_map/all_to_all | solution.py:53
  118.5 9.2 %all-to-all-start.5 = ((f32[2,1,512]{2,1,0:T(1,128)}), f32[2,1,512]{2,1,0:T(1,128)S(1)}, u32[]{:S(2)}, u32[]{:S(2)}) async-start(f32[2,1,512]{2,1,0:T(1,128)} %reshape.125), calls=%async_computation.5 | async-start | bytes 8192 | tf_op jit(solution)/shard_map/all_to_all | solution.py:22
  132.2 36.3 %all-to-all-start.2 = ((f32[64,8,256]{2,1,0:T(8,128)}), f32[64,8,256]{2,1,0:T(8,128)S(1)}, u32[]{:S(2)}, u32[]{:S(2)}) async-start(f32[64,8,256]{2,1,0:T(8,128)} %broadcast_in_dim.44), calls=%async_computation.2 | async-start | bytes 1048576 | tf_op jit(solution)/shard_map/all_to_all | solution.py:22
  179.8 5.7 %copy-start.1 = (bf16[2048,256]{1,0:T(8,128)(2,1)S(1)}, bf16[2048,256]{1,0:T(8,128)(2,1)}, u32[]{:S(2)}) copy-start(bf16[2048,256]{1,0:T(8,128)(2,1)} %param.9) | copy-start | bytes 3145732
  181.3 18.6 %all-to-all-start.8 = ((f32[4,1,65792]{2,1,0:T(1,128)}), f32[4,1,65792]{2,1,0:T(1,128)S(1)}, u32[]{:S(2)}, u32[]{:S(2)}) async-start(f32[4,1,65792]{2,1,0:T(1,128)} %broadcast_in_dim.50), calls=%async_computation.8 | async-start | bytes 2105344 | tf_op jit(solution)/shard_map/all_to_all | solution.py:22
where the time goes:
time: 212 us; the launch traced here: 211 us
  waiting for transfers between devices  81.7 us (39%)
  blocking collectives  48.3 us (23%)
  matrix products  35.4 us (17%)
  starting transfers between devices  27.9 us (13%)
  other arithmetic  9.49 us (4%)
  local copies, waits for them, and re-layouts  6.02 us (3%)
    all_to_all x4, waiting for transfers between devices, from_everyone(): return lax.all_to_all(copies, axis, split_axis=0, concat_axis=0, tiled=True)  54.9 us
    all_to_all x3, blocking collectives, from_everyone(): return lax.all_to_all(copies, axis, split_axis=0, concat_axis=0, tiled=True)  37.2 us
    all_to_all x1, waiting for transfers between devices, sum_by_axis(): return jnp.sum(lax.all_to_all(own, far, 0, 0, tiled=True), axis=0)  26.8 us
    all_to_all x4, starting transfers between devices, from_everyone(): return lax.all_to_all(copies, axis, split_axis=0, concat_axis=0, tiled=True)  23.3 us
    dot_general x4, matrix products, add_group(): jnp.einsum('bjp,pls->bjls', counts_part, tile_bank, precision=lax.Precisi...  13.8 us
    dot_general x4, matrix products, add_group(): jnp.einsum('bjls,bsm->jlm', combined, states_part.astype(jnp.float32), pr...  11.2 us
    all_to_all x1, blocking collectives, sum_at_owner(): lax.all_to_all(blocks, axis, split_axis=0, concat_axis=0, tiled=True)  11.1 us
    all_to_all x1, starting transfers between devices, sum_by_axis(): return jnp.sum(lax.all_to_all(own, far, 0, 0, tiled=True), axis=0)  4.63 us
  transfers between devices with their start and end apart: 5, of which 5 were waited for; matrix products, arithmetic and copies ran while one was open for 2% of the time, Pallas kernels for 0%

commit v1 on v0

v1 whole, which is shorter than its diff:
```python
import functools

import jax
import jax.numpy as jnp
from jax import lax
from jax.experimental import pallas as pl
from jax.experimental.pallas import tpu as pltpu
from jax.sharding import Mesh
from jax.sharding import PartitionSpec as P

NLB = 8
NS_ITERS = 4
F32 = jnp.float32
BF16 = jnp.bfloat16
ORIG = ("y", "zh", "zl", "c")
SLAB = ("x", "y", "zl", "c")
VMEM = pl.BlockSpec(memory_space=pltpu.VMEM)
SMEM = pl.BlockSpec(memory_space=pltpu.SMEM)
PARAMS = pltpu.CompilerParams(vmem_limit_bytes=40 * 2**20)


def halves(a):
    high = a.astype(BF16)
    return high, (a - high.astype(F32)).astype(BF16)


def dot(a, b):
    return jnp.dot(a, b, preferred_element_type=F32)


def dot3(a, b):
    (ah, al), (bh, bl) = a, b
    return dot(ah, bh) + (dot(ah, bl) + dot(al, bh))


def term_kernel(me_ref, ids_ref, targets_ref, live_ref, states_ref, tiles_ref, keep_ref, send_ref):
    blocks, slots = ids_ref.shape
    block_rows = tiles_ref.shape[2]
    keep_ref[...] = jnp.zeros_like(keep_ref)
    send_ref[...] = jnp.zeros_like(send_ref)

    def run(by_core):
        def add_block(b, carry):
            rows = pl.ds(pl.multiple_of(b * block_rows, block_rows), block_rows)
            position = lax.broadcasted_iota(jnp.int32, (block_rows, states_ref.shape[1]), 0)
            living = (position < live_ref[b]).astype(F32).astype(BF16)
            masked = states_ref[rows, :] * living
            for t in range(slots):
                product = dot(tiles_ref[ids_ref[b, t]], masked)
                target = targets_ref[b, t]
                chunk = (target // 2) * 2
                first = (target % 2) * 32
                for g in range(16):
                    q, zl, c = g // 4, (g // 2) % 2, g % 2
                    at = pl.ds(pl.multiple_of(first + q * 8, 8), 8)
                    by_core[c][chunk + zl, at, :] += product[g * 8 : g * 8 + 8]
            return carry

        lax.fori_loop(0, blocks, add_block, 0)

    @pl.when(me_ref[0] == 0)
    def _():
        run((keep_ref, send_ref))

    @pl.when(me_ref[0] == 1)
    def _():
        run((send_ref, keep_ref))


def rows_kernel(parts_ref, counts_ref, var_ref, out_ref):
    total = jnp.sum(parts_ref[...], axis=0)
    rows = total.shape[0]
    out_ref[0:rows, :] = total[:, :128]
    out_ref[rows : 2 * rows, :] = total[:, 128:]
    lane = lax.broadcasted_iota(jnp.int32, (8, 128), 1)
    tail = jnp.where(lane == 0, counts_ref[...], jnp.where(lane == 1, var_ref[...], 0.0))
    out_ref[2 * rows : 2 * rows + 8, :] = tail


def gram_kernel(parts_ref, out_ref):
    rows = (parts_ref.shape[1] - 8) // 2
    left = jnp.sum(parts_ref[:, 0:rows, :], axis=0)
    right = jnp.sum(parts_ref[:, rows : 2 * rows, :], axis=0)
    tail = parts_ref[:, 2 * rows :, :].reshape(rows, 128)
    counts, variance = tail[:, 0:1], tail[:, 1:2]
    mean = jnp.sum(left + right, axis=1, keepdims=True) * (1.0 / 256.0)
    spread = jnp.concatenate([left - mean, right - mean], axis=1)
    weights = 1.0 / variance
    forcing = jnp.sum(spread * (weights * (counts - mean)), axis=0, keepdims=True)
    gram = dot3(halves(spread.T), halves(spread * weights))
    out_ref[...] = jnp.zeros_like(out_ref)
    out_ref[0:16] = gram[:128, :128].reshape(16, 8, 128)
    out_ref[16:32] = gram[:128, 128:].reshape(16, 8, 128)
    out_ref[32:48] = gram[128:, 128:].reshape(16, 8, 128)
    out_ref[48, 0:1, :] = forcing[:, :128]
    out_ref[48, 1:2, :] = forcing[:, 128:]


def share_kernel(parts_ref, out_ref):
    total = jnp.sum(parts_ref[...], axis=0)
    out_ref[...] = jnp.broadcast_to(total[None], out_ref.shape)


def update_kernel(link_ref, live_ref, pieces_ref, states_ref, out_ref):
    members = states_ref.shape[1]
    first = pieces_ref[0:16].reshape(128, 128)
    across = pieces_ref[16:32].reshape(128, 128)
    last = pieces_ref[32:48].reshape(128, 128)
    gram = jnp.concatenate(
        [jnp.concatenate([first, across], axis=1), jnp.concatenate([across.T, last], axis=1)], axis=0
    )
    forcing = jnp.concatenate([pieces_ref[48, 0:1, :], pieces_ref[48, 1:2, :]], axis=1)
    at = lambda dim: lax.broadcasted_iota(jnp.int32, (members, members), dim)
    identity = jnp.where(at(0) == at(1), 1.0, 0.0).astype(F32)
    system = identity + gram * (1.0 / (members - 1.0))
    bound = jnp.max(jnp.sum(jnp.abs(system), axis=0, keepdims=True), axis=1, keepdims=True)
    root = system * (1.0 / bound)
    inverse = identity
    for sweep in range(NS_ITERS):
        if sweep == 0:
            middle = 1.5 * identity - 0.5 * root
            inverse = middle
        else:
            middle = 1.5 * identity - 0.5 * dot3(halves(inverse), halves(root))
        middle_halves = halves(middle)
        if sweep > 0:
            inverse = dot3(middle_halves, halves(inverse))
        if sweep < NS_ITERS - 1:
            root = dot3(halves(root), middle_halves)
    inner = dot3(halves(jnp.broadcast_to(forcing, (8, members))), halves(inverse))[0:1]
    mean_weights = jnp.sum(inverse * inner, axis=1, keepdims=True) * (1.0 / (bound * (members - 1.0)))
    transform = inverse * lax.rsqrt(bound) + mean_weights
    transform += (1.0 - jnp.sum(transform, axis=0, keepdims=True)) * (1.0 / members)
    high, low = halves(transform)
    states = states_ref[...]
    updated = dot(states, high) + dot(states, low)
    own_blocks = states.shape[0] // 128
    position = lax.broadcasted_iota(jnp.int32, (128, members), 0)
    for k in range(own_blocks):
        rows = slice(k * 128, k * 128 + 128)
        live = live_ref[link_ref[0] * own_blocks + k]
        kept = states[rows].astype(F32)
        out_ref[rows, :] = jnp.where(position < live, updated[rows], kept).astype(BF16)


def all_to_all(x, axes):
    return lax.all_to_all(x, axes, split_axis=0, concat_axis=0, tiled=True)


def per_device(background, live_counts, patterns, pattern_ids, link_targets, counts_obs, obs_var):
    states_dev, members = background.shape
    core = lax.axis_index("c").astype(jnp.int32).reshape(1)
    link = lax.axis_index("x").astype(jnp.int32).reshape(1)
    half = jax.ShapeDtypeStruct((8, 64, members), F32)
    keep, send = pl.pallas_call(
        term_kernel,
        out_shape=(half, half),
        in_specs=[SMEM, SMEM, SMEM, SMEM, VMEM, VMEM],
        out_specs=(VMEM, VMEM),
        compiler_params=PARAMS,
        name="term",
    )(core, pattern_ids[0], link_targets[0], live_counts, background, patterns[0])
    of_chip = keep + lax.ppermute(send, "c", [(0, 1), (1, 0)])
    parts = all_to_all(of_chip, ("y", "zl"))
    own = pl.pallas_call(
        rows_kernel,
        out_shape=jax.ShapeDtypeStruct((136, 128), F32),
        in_specs=[VMEM, VMEM, VMEM],
        out_specs=VMEM,
        compiler_params=PARAMS,
        name="rows",
    )(parts, counts_obs.reshape(8, 1), obs_var.reshape(8, 1))
    column = lax.all_gather(own, "zh")
    gram = pl.pallas_call(
        gram_kernel,
        out_shape=jax.ShapeDtypeStruct((64, 8, 128), F32),
        in_specs=[VMEM],
        out_specs=VMEM,
        compiler_params=PARAMS,
        name="gram",
    )(column)
    shared = pl.pallas_call(
        share_kernel,
        out_shape=jax.ShapeDtypeStruct((64, 8, 128), F32),
        in_specs=[VMEM],
        out_specs=VMEM,
        compiler_params=PARAMS,
        name="share",
    )(all_to_all(gram, SLAB))
    pieces = all_to_all(shared, SLAB)
    own_rows = states_dev // lax.axis_size("x")
    return pl.pallas_call(
        update_kernel,
        out_shape=jax.ShapeDtypeStruct((own_rows, members), BF16),
        grid_spec=pltpu.PrefetchScalarGridSpec(
            num_scalar_prefetch=2,
            grid=(1,),
            in_specs=[
                pl.BlockSpec((64, 8, 128), lambda i, link, live: (0, 0, 0)),
                pl.BlockSpec((own_rows, members), lambda i, link, live: (link[0], 0)),
            ],
            out_specs=pl.BlockSpec((own_rows, members), lambda i, link, live: (0, 0)),
        ),
        compiler_params=PARAMS,
        name="update",
    )(link, live_counts, pieces, background)


def solution(mesh):
    torus = Mesh(mesh.devices.reshape(4, 8, 2, 2, 4), ("y", "zh", "zl", "c", "x"))
    return jax.shard_map(
        per_device,
        mesh=torus,
        in_specs=(
            P(ORIG, None),
            P(ORIG),
            P("x", ORIG, None, None),
            P("x", ORIG, None),
            P("x", ORIG, None),
            P("x", ORIG),
            P("x", ORIG),
        ),
        out_specs=P((*ORIG, "x"), None),
        check_vma=False,
    )
```

time: 212 us -> 108 us (0.51)
  waiting for transfers between devices: 81.7 us -> 19.6 us
  matrix products: 35.4 us -> 0 us
  Pallas kernels: 0 us -> 13.7 us
  starting transfers between devices: 27.9 us -> 16.8 us
  other arithmetic: 9.49 us -> 0.86 us
  blocking collectives: 48.3 us -> 50.6 us
    all_to_all x5 -> x2, waiting for transfers between devices: 81.7 us -> 18.1 us  [all_to_all(): return lax.all_to_all(x, axes, split_axis=0, concat_axis=0, tiled=True)]
    dot_general x25 -> x0, matrix products: 35.4 us -> none  [the longest x4 13.8 us: add_group(): jnp.einsum('bjp,pls->bjls', counts_part, tile_bank, precision=lax.Precisi...]
    all_gather x0 -> x1, blocking collectives: none -> 28.3 us  [per_device(): column = lax.all_gather(own, 'zh')]
    all_to_all x4 -> x1, blocking collectives: 48.3 us -> 22.3 us  [all_to_all(): return lax.all_to_all(x, axes, split_axis=0, concat_axis=0, tiled=True)]
    all_to_all x5 -> x2, starting transfers between devices: 27.9 us -> 8.01 us  [all_to_all(): return lax.all_to_all(x, axes, split_axis=0, concat_axis=0, tiled=True)]
    pallas_call x0 -> x5, Pallas kernels: none -> 13.7 us  [the longest x1 8.01 us: per_device(): pl.pallas_call(term_kernel, out_shape=(half, half), in_specs=[SMEM, SMEM,...]
    ppermute x0 -> x1, starting transfers between devices: none -> 8.76 us  [per_device(): of_chip = keep + lax.ppermute(send, 'c', [(0, 1), (1, 0)])]
    unnamed x21 -> x18, local copies, waits for them, and re-layouts: 1.1 us -> 5.87 us
  transfers between devices with their start and end apart: 5 -> 3, of which waited for: 5 -> 3; matrix products, arithmetic and copies ran while one was open for 2% -> 0% of each run, Pallas kernels for 0% -> 0%
where the time goes in v1:
time: 108 us
  blocking collectives  50.6 us (47%)
  waiting for transfers between devices  19.6 us (18%)
  starting transfers between devices  16.8 us (16%)
  Pallas kernels  13.7 us (13%)
  local copies, waits for them, and re-layouts  6.04 us (6%)
    all_gather x1, blocking collectives, per_device(): column = lax.all_gather(own, 'zh')  28.3 us
    all_to_all x1, blocking collectives, all_to_all(): return lax.all_to_all(x, axes, split_axis=0, concat_axis=0, tiled=True)  22.3 us
    all_to_all x2, waiting for transfers between devices, all_to_all(): return lax.all_to_all(x, axes, split_axis=0, concat_axis=0, tiled=True)  18.1 us
    ppermute x1, starting transfers between devices, per_device(): of_chip = keep + lax.ppermute(send, 'c', [(0, 1), (1, 0)])  8.76 us
    pallas_call x1, Pallas kernels, per_device(): pl.pallas_call(term_kernel, out_shape=(half, half), in_specs=[SMEM, SMEM,...  8.01 us
    all_to_all x2, starting transfers between devices, all_to_all(): return lax.all_to_all(x, axes, split_axis=0, concat_axis=0, tiled=True)  8.01 us
    unnamed x18, local copies, waits for them, and re-layouts  5.87 us
    pallas_call x1, Pallas kernels, per_device(): pl.pallas_call(update_kernel, out_shape=jax.ShapeDtypeStruct((own_rows, m...  4.39 us
  transfers between devices with their start and end apart: 3, of which 3 were waited for; matrix products, arithmetic and copies ran while one was open for 0% of the time, Pallas kernels for 0%

profile of v1, /device:TPU:1, one launch (start us, length us, event | category | flops | bytes accessed | tf_op | source)
XLA Modules:
  0.0 107.7 jit_solution(10313480285651674026)
XLA Ops:
  0.0 0.7 copy-done.4
  0.7 0.1 copy.8
  0.8 0.6 copy-done.5
  1.4 0.1 copy.9
  1.5 0.7 copy-done.3
  2.1 1.2 %copy-done = bf16[2048,256]{1,0:T(8,128)(2,1)S(1)} copy-done((bf16[2048,256]{1,0:T(8,128)(2,1)S(1)}, bf16[2048,256]{1,0:T(8,128)(2,1)}, u32[]{:S(2)}) %copy-start) | copy-done | bytes 1048600
  3.3 1.2 %copy-done.2 = bf16[1,32,128,128]{3,2,1,0:T(8,128)(2,1)S(1)} copy-done((bf16[1,32,128,128]{3,2,1,0:T(8,128)(2,1)S(1)}, bf16[1,32,128,128]{3,2,1,0:T(8,128)(2,1)}, u32[]{:S(2)}) %copy-start.2) | copy-done | bytes 1048600
  4.6 8.0 %term.1 = (f32[8,64,256]{2,1,0:T(8,128)S(1)}, f32[8,64,256]{2,1,0:T(8,128)S(1)}) custom-call(s32[1]{0:T(128)} %bitcast.1.me_ref, s32[16,12]{1,0:T(8,128)S(1)} %bitcast.10, s32[16,12]{1,0:T(8,128)S(1)} %bitcast.11, s32[16]{0:T(128)S(1)} %copy-done.3, bf16[2048,256]{1,0:T(8,128)(2,1)S(1)} %copy-done, bf16[32,128,128]{2,1,0:T(8,128)(2,1)S(1)} %bitcast.9), custom_call_target="tpu_custom_call" | custom-call | tf_op jit(solution)/shard_map/term/pallas_call | solution.py:155
  12.6 8.8 %collective-permute-start = (f32[8,64,256]{2,1,0:T(8,128)S(1)}, f32[8,64,256]{2,1,0:T(8,128)S(1)}, u32[]{:S(2)}, u32[]{:S(2)}) collective-permute-start(f32[8,64,256]{2,1,0:T(8,128)S(1)} %get-tuple-element.8), channel_id=1, source_target_pairs={{0,4},{4,0},{1,5},{5,1},{2,6},{6,2},{3,7},{7,3},{8,12},{12,8},{9,1... | collective-permute-start | bytes 1572872 | tf_op jit(solution)/shard_map/ppermute | solution.py:163
  21.4 1.5 %collective-permute-done = f32[8,64,256]{2,1,0:T(8,128)S(1)} collective-permute-done((f32[8,64,256]{2,1,0:T(8,128)S(1)}, f32[8,64,256]{2,1,0:T(8,128)S(1)}, u32[]{:S(2)}, u32[]{:S(2)}) %collective-permute-start) | collective-permute-done | bytes 524320 | tf_op jit(solution)/shard_map/ppermute | solution.py:163
  22.9 0.9 add.3
  23.7 3.5 %all-to-all-start = ((f32[8,64,256]{2,1,0:T(8,128)}), f32[8,64,256]{2,1,0:T(8,128)S(1)}, u32[]{:S(2)}, u32[]{:S(2)}) async-start(f32[8,64,256]{2,1,0:T(8,128)} %add.3), calls=%async_computation | async-start | bytes 1048576 | tf_op jit(solution)/shard_map/all_to_all | solution.py:147
  27.3 0.6 copy-done.6
  27.9 0.1 copy.10.counts_ref
  28.0 0.7 copy-done.7
  28.6 0.1 copy.11.var_ref
  28.7 8.0 %all-to-all-done.parts_ref = f32[8,64,256]{2,1,0:T(8,128)S(1)} async-done(((f32[8,64,256]{2,1,0:T(8,128)}), f32[8,64,256]{2,1,0:T(8,128)S(1)}, u32[]{:S(2)}, u32[]{:S(2)}) %all-to-all-start) | async-done | bytes 524320 | tf_op jit(solution)/shard_map/all_to_all | solution.py:147
  36.8 28.3 %all-gather = f32[1088,128]{1,0:T(8,128)S(1)} all-gather(f32[136,128]{1,0:T(8,128)S(1)} %rows.1), channel_id=2, replica_groups=mesh['y'=4,'zh'=8,'zl'=2,'c'=2,'x'=4] {'zh'}, dimensions={0}, use_global_device_ids=true | all-gather | bytes 626688 | tf_op jit(solution)/shard_map/all_gather | solution.py:173
  65.1 0.4 gram.1
  65.5 22.3 %all_to_all.15.parts_ref = f32[64,8,128]{2,1,0:T(8,128)S(1)} all-to-all(f32[64,8,128]{2,1,0:T(8,128)S(1)} %gram.1), channel_id=1, replica_groups=mesh['y'=4,'zh'=8,'zl'=2,'c'=2,'x'=4] {'x','y','zl','c'}, dimensions={0} | all-to-all | bytes 524288 | tf_op jit(solution)/shard_map/all_to_all | solution.py:147
  87.8 0.8 share.1
  88.6 4.5 %all-to-all-start.2 = ((f32[64,8,128]{2,1,0:T(8,128)}), f32[64,8,128]{2,1,0:T(8,128)S(1)}, u32[]{:S(2)}, u32[]{:S(2)}) async-start(f32[64,8,128]{2,1,0:T(8,128)} %share.1), calls=%async_computation.2 | async-start | bytes 524288 | tf_op jit(solution)/shard_map/all_to_all | solution.py:147
  93.2 10.1 %all-to-all-done.2.pieces_ref = f32[64,8,128]{2,1,0:T(8,128)S(1)} async-done(((f32[64,8,128]{2,1,0:T(8,128)}), f32[64,8,128]{2,1,0:T(8,128)S(1)}, u32[]{:S(2)}, u32[]{:S(2)}) %all-to-all-start.2) | async-done | bytes 262176 | tf_op jit(solution)/shard_map/all_to_all | solution.py:147
  103.3 4.4 %update.1 = bf16[512,256]{1,0:T(8,128)(2,1)} custom-call(s32[1]{0:T(128)} %bitcast.link_ref, s32[16]{0:T(128)S(1)} %copy-done.3, f32[64,8,128]{2,1,0:T(8,128)S(1)} %all-to-all-done.2.pieces_ref, bf16[2048,256]{1,0:T(8,128)(2,1)S(1)} %copy-done.1), custom_call_target="tpu_custom_call" | custom-call | tf_op jit(solution)/shard_map/update/pallas_call | solution.py:192
  (10 shorter events, 0.1 us)
Async XLA Ops:
  0.0 0.7 copy-start.4
  0.7 0.7 copy-start.5
  1.5 0.7 copy-start.3
  2.1 1.2 %copy-start = (bf16[2048,256]{1,0:T(8,128)(2,1)S(1)}, bf16[2048,256]{1,0:T(8,128)(2,1)}, u32[]{:S(2)}) copy-start(bf16[2048,256]{1,0:T(8,128)(2,1)} %states_ref.3) | copy-start | bytes 3145732
  3.3 1.2 %copy-start.2 = (bf16[1,32,128,128]{3,2,1,0:T(8,128)(2,1)S(1)}, bf16[1,32,128,128]{3,2,1,0:T(8,128)(2,1)}, u32[]{:S(2)}) copy-start(bf16[1,32,128,128]{3,2,1,0:T(8,128)(2,1)} %param.9) | copy-start | bytes 3145732
  12.6 10.3 %collective-permute-start = (f32[8,64,256]{2,1,0:T(8,128)S(1)}, f32[8,64,256]{2,1,0:T(8,128)S(1)}, u32[]{:S(2)}, u32[]{:S(2)}) collective-permute-start(f32[8,64,256]{2,1,0:T(8,128)S(1)} %get-tuple-element.8), channel_id=1, source_target_pairs={{0,4},{4,0},{1,5},{5,1},{2,6},{6,2},{3,7},{7,3},{8,12},{12,8},{9,1... | collective-permute-start | bytes 1572872 | tf_op jit(solution)/shard_map/ppermute | solution.py:163
  23.7 13.0 %all-to-all-start = ((f32[8,64,256]{2,1,0:T(8,128)}), f32[8,64,256]{2,1,0:T(8,128)S(1)}, u32[]{:S(2)}, u32[]{:S(2)}) async-start(f32[8,64,256]{2,1,0:T(8,128)} %add.3), calls=%async_computation | async-start | bytes 1048576 | tf_op jit(solution)/shard_map/all_to_all | solution.py:147
  27.2 0.7 copy-start.6
  28.0 0.7 copy-start.7
  65.1 38.2 %copy-start.1 = (bf16[2048,256]{1,0:T(8,128)(2,1)S(1)}, bf16[2048,256]{1,0:T(8,128)(2,1)}, u32[]{:S(2)}) copy-start(bf16[2048,256]{1,0:T(8,128)(2,1)} %states_ref.3) | copy-start | bytes 3145732
  88.6 14.6 %all-to-all-start.2 = ((f32[64,8,128]{2,1,0:T(8,128)}), f32[64,8,128]{2,1,0:T(8,128)S(1)}, u32[]{:S(2)}, u32[]{:S(2)}) async-start(f32[64,8,128]{2,1,0:T(8,128)} %share.1), calls=%async_computation.2 | async-start | bytes 524288 | tf_op jit(solution)/shard_map/all_to_all | solution.py:147

commit v2 on v1

--- a/solution.py
+++ b/solution.py
@@ -1,5 +1,3 @@
-import functools
-
 import jax
 import jax.numpy as jnp
 from jax import lax
@@ -67,33 +65,29 @@
         run((send_ref, keep_ref))
 
 
-def rows_kernel(parts_ref, counts_ref, var_ref, out_ref):
+def rows_kernel(parts_ref, out_ref):
     total = jnp.sum(parts_ref[...], axis=0)
-    rows = total.shape[0]
-    out_ref[0:rows, :] = total[:, :128]
-    out_ref[rows : 2 * rows, :] = total[:, 128:]
-    lane = lax.broadcasted_iota(jnp.int32, (8, 128), 1)
-    tail = jnp.where(lane == 0, counts_ref[...], jnp.where(lane == 1, var_ref[...], 0.0))
-    out_ref[2 * rows : 2 * rows + 8, :] = tail
-
-
-def gram_kernel(parts_ref, out_ref):
-    rows = (parts_ref.shape[1] - 8) // 2
-    left = jnp.sum(parts_ref[:, 0:rows, :], axis=0)
-    right = jnp.sum(parts_ref[:, rows : 2 * rows, :], axis=0)
-    tail = parts_ref[:, 2 * rows :, :].reshape(rows, 128)
-    counts, variance = tail[:, 0:1], tail[:, 1:2]
-    mean = jnp.sum(left + right, axis=1, keepdims=True) * (1.0 / 256.0)
-    spread = jnp.concatenate([left - mean, right - mean], axis=1)
-    weights = 1.0 / variance
-    forcing = jnp.sum(spread * (weights * (counts - mean)), axis=0, keepdims=True)
+    out_ref[...] = total.reshape(out_ref.shape)
+
+
+def as_column(ref):
+    count = ref.shape[1]
+    at = lambda dim: lax.broadcasted_iota(jnp.int32, (count, count), dim)
+    return jnp.sum(jnp.where(at(0) == at(1), ref[...], 0.0), axis=1, keepdims=True)
+
+
+def gram_kernel(parts_ref, counts_ref, var_ref, out_ref):
+    total = jnp.sum(parts_ref[...], axis=0)
+    mean = jnp.mean(total, axis=1, keepdims=True)
+    spread = total - mean
+    weights = 1.0 / as_column(var_ref)
+    forcing = jnp.sum(spread * (weights * (as_column(counts_ref) - mean)), axis=0, keepdims=True)
     gram = dot3(halves(spread.T), halves(spread * weights))
-    out_ref[...] = jnp.zeros_like(out_ref)
+    out_ref[49:] = jnp.zeros((15, 8, 128), F32)
     out_ref[0:16] = gram[:128, :128].reshape(16, 8, 128)
     out_ref[16:32] = gram[:128, 128:].reshape(16, 8, 128)
     out_ref[32:48] = gram[128:, 128:].reshape(16, 8, 128)
-    out_ref[48, 0:1, :] = forcing[:, :128]
-    out_ref[48, 1:2, :] = forcing[:, 128:]
+    out_ref[48] = jnp.concatenate([forcing[:, :128], forcing[:, 128:], jnp.zeros((6, 128), F32)], axis=0)
 
 
 def share_kernel(parts_ref, out_ref):
@@ -147,6 +141,17 @@
     return lax.all_to_all(x, axes, split_axis=0, concat_axis=0, tiled=True)
 
 
+def local(kernel, shape, operands):
+    return pl.pallas_call(
+        kernel,
+        out_shape=jax.ShapeDtypeStruct(shape, F32),
+        in_specs=[VMEM] * operands,
+        out_specs=VMEM,
+        compiler_params=PARAMS,
+        name=kernel.__name__,
+    )
+
+
 def per_device(background, live_counts, patterns, pattern_ids, link_targets, counts_obs, obs_var):
     states_dev, members = background.shape
     core = lax.axis_index("c").astype(jnp.int32).reshape(1)
@@ -162,31 +167,11 @@
     )(core, pattern_ids[0], link_targets[0], live_counts, background, patterns[0])
     of_chip = keep + lax.ppermute(send, "c", [(0, 1), (1, 0)])
     parts = all_to_all(of_chip, ("y", "zl"))
-    own = pl.pallas_call(
-        rows_kernel,
-        out_shape=jax.ShapeDtypeStruct((136, 128), F32),
-        in_specs=[VMEM, VMEM, VMEM],
-        out_specs=VMEM,
-        compiler_params=PARAMS,
-        name="rows",
-    )(parts, counts_obs.reshape(8, 1), obs_var.reshape(8, 1))
-    column = lax.all_gather(own, "zh")
-    gram = pl.pallas_call(
-        gram_kernel,
-        out_shape=jax.ShapeDtypeStruct((64, 8, 128), F32),
-        in_specs=[VMEM],
-        out_specs=VMEM,
-        compiler_params=PARAMS,
-        name="gram",
-    )(column)
-    shared = pl.pallas_call(
-        share_kernel,
-        out_shape=jax.ShapeDtypeStruct((64, 8, 128), F32),
-        in_specs=[VMEM],
-        out_specs=VMEM,
-        compiler_params=PARAMS,
-        name="share",
-    )(all_to_all(gram, SLAB))
+    rows = local(rows_kernel, (8, 8, members), 1)(parts)
+    own = all_to_all(rows, "zh")
+    gram = local(gram_kernel, (64, 8, 128), 3)(own, counts_obs, obs_var)
+    plane = local(share_kernel, (8, 8, 128), 1)(all_to_all(gram, SLAB))
+    shared = local(share_kernel, (64, 8, 128), 1)(all_to_all(plane, "zh"))
     pieces = all_to_all(shared, SLAB)
     own_rows = states_dev // lax.axis_size("x")
     return pl.pallas_call(

time: 108 us -> 113 us (1.046)
  blocking collectives: 50.6 us -> 68.1 us
  waiting for transfers between devices: 19.6 us -> 11.6 us
  starting transfers between devices: 16.8 us -> 14.4 us
  local copies, waits for them, and re-layouts: 6.04 us -> 4.58 us
    all_to_all x1 -> x4, blocking collectives: 22.3 us -> 68.1 us  [all_to_all(): return lax.all_to_all(x, axes, split_axis=0, concat_axis=0, tiled=True)]
    all_gather x1 -> x0, blocking collectives: 28.3 us -> none  [per_device(): column = lax.all_gather(own, 'zh')]
    all_to_all x2 -> x1, waiting for transfers between devices: 18.1 us -> 10.1 us  [all_to_all(): return lax.all_to_all(x, axes, split_axis=0, concat_axis=0, tiled=True)]
    all_to_all x2 -> x1, starting transfers between devices: 8.01 us -> 5.62 us  [all_to_all(): return lax.all_to_all(x, axes, split_axis=0, concat_axis=0, tiled=True)]
    unnamed x18, local copies, waits for them, and re-layouts: 5.87 us -> 4.58 us
  transfers between devices with their start and end apart: 3 -> 2, of which waited for: 3 -> 2; matrix products, arithmetic and copies ran while one was open for 0% -> 0% of each run, Pallas kernels for 0% -> 0%
where the time goes in v2:
time: 113 us; the launch traced here: 112 us
  blocking collectives  68.1 us (60%)
  starting transfers between devices  14.4 us (13%)
  Pallas kernels  13.6 us (12%)
  waiting for transfers between devices  11.6 us (10%)
  local copies, waits for them, and re-layouts  4.58 us (4%)
    all_to_all x4, blocking collectives, all_to_all(): return lax.all_to_all(x, axes, split_axis=0, concat_axis=0, tiled=True)  68.1 us
    all_to_all x1, waiting for transfers between devices, all_to_all(): return lax.all_to_all(x, axes, split_axis=0, concat_axis=0, tiled=True)  10.1 us
    ppermute x1, starting transfers between devices, per_device(): of_chip = keep + lax.ppermute(send, 'c', [(0, 1), (1, 0)])  8.76 us
    pallas_call x1, Pallas kernels, per_device(): pl.pallas_call(term_kernel, out_shape=(half, half), in_specs=[SMEM, SMEM,...  8.01 us
    all_to_all x1, starting transfers between devices, all_to_all(): return lax.all_to_all(x, axes, split_axis=0, concat_axis=0, tiled=True)  5.62 us
    unnamed x18, local copies, waits for them, and re-layouts  4.58 us
    pallas_call x1, Pallas kernels, per_device(): pl.pallas_call(update_kernel, out_shape=jax.ShapeDtypeStruct((own_rows, m...  4.39 us
  transfers between devices with their start and end apart: 2, of which 2 were waited for; matrix products, arithmetic and copies ran while one was open for 0% of the time, Pallas kernels for 0%

profile of v2, /device:TPU:1, one launch (start us, length us, event | category | flops | bytes accessed | tf_op | source)
XLA Modules:
  0.0 112.5 jit_solution(10563403251215972725)
XLA Ops:
  0.0 0.7 copy-done.6
  0.7 0.1 copy.8
  0.8 0.6 copy-done.7
  1.4 0.1 copy.9
  1.5 0.7 copy-done.3
  2.1 1.2 %copy-done = bf16[2048,256]{1,0:T(8,128)(2,1)S(1)} copy-done((bf16[2048,256]{1,0:T(8,128)(2,1)S(1)}, bf16[2048,256]{1,0:T(8,128)(2,1)}, u32[]{:S(2)}) %copy-start) | copy-done | bytes 1048600
  3.3 1.2 %copy-done.2 = bf16[1,32,128,128]{3,2,1,0:T(8,128)(2,1)S(1)} copy-done((bf16[1,32,128,128]{3,2,1,0:T(8,128)(2,1)S(1)}, bf16[1,32,128,128]{3,2,1,0:T(8,128)(2,1)}, u32[]{:S(2)}) %copy-start.2) | copy-done | bytes 1048600
  4.6 8.0 %term.1 = (f32[8,64,256]{2,1,0:T(8,128)S(1)}, f32[8,64,256]{2,1,0:T(8,128)S(1)}) custom-call(s32[1]{0:T(128)} %bitcast.1.me_ref, s32[16,12]{1,0:T(8,128)S(1)} %bitcast.6, s32[16,12]{1,0:T(8,128)S(1)} %bitcast.7, s32[16]{0:T(128)S(1)} %copy-done.3, bf16[2048,256]{1,0:T(8,128)(2,1)S(1)} %copy-done, bf16[32,128,128]{2,1,0:T(8,128)(2,1)S(1)} %bitcast.5), custom_call_target="tpu_custom_call" | custom-call | tf_op jit(solution)/shard_map/term/pallas_call | solution.py:160
  12.6 8.8 %collective-permute-start = (f32[8,64,256]{2,1,0:T(8,128)S(1)}, f32[8,64,256]{2,1,0:T(8,128)S(1)}, u32[]{:S(2)}, u32[]{:S(2)}) collective-permute-start(f32[8,64,256]{2,1,0:T(8,128)S(1)} %get-tuple-element.8), channel_id=1, source_target_pairs={{0,4},{4,0},{1,5},{5,1},{2,6},{6,2},{3,7},{7,3},{8,12},{12,8},{9,1... | collective-permute-start | bytes 1572872 | tf_op jit(solution)/shard_map/ppermute | solution.py:168
  21.4 1.5 %collective-permute-done = f32[8,64,256]{2,1,0:T(8,128)S(1)} collective-permute-done((f32[8,64,256]{2,1,0:T(8,128)S(1)}, f32[8,64,256]{2,1,0:T(8,128)S(1)}, u32[]{:S(2)}, u32[]{:S(2)}) %collective-permute-start) | collective-permute-done | bytes 524320 | tf_op jit(solution)/shard_map/ppermute | solution.py:168
  22.9 0.1 add.3
  23.0 12.2 %all_to_all.25.parts_ref = f32[8,64,256]{2,1,0:T(8,128)S(1)} all-to-all(f32[8,64,256]{2,1,0:T(8,128)S(1)} %add.3), channel_id=1, replica_groups=mesh['y'=4,'zh'=8,'zl'=2,'c'=2,'x'=4] {'y','zl'}, dimensions={0} | all-to-all | bytes 1048576 | tf_op jit(solution)/shard_map/all_to_all | solution.py:141
  35.3 0.0 copy-start.4
  35.3 0.0 copy-start.5
  35.3 23.0 %all_to_all.26.parts_ref = f32[8,8,256]{2,1,0:T(8,128)S(1)} all-to-all(f32[8,8,256]{2,1,0:T(8,128)S(1)} %rows_kernel.1), channel_id=1, replica_groups=mesh['y'=4,'zh'=8,'zl'=2,'c'=2,'x'=4] {'zh'}, dimensions={0} | all-to-all | bytes 131072 | tf_op jit(solution)/shard_map/all_to_all | solution.py:141
  58.3 0.0 copy-done.4
  58.3 0.4 gram_kernel.1
  58.7 18.7 %all_to_all.27.parts_ref = f32[64,8,128]{2,1,0:T(8,128)S(1)} all-to-all(f32[64,8,128]{2,1,0:T(8,128)S(1)} %gram_kernel.1), channel_id=1, replica_groups=mesh['y'=4,'zh'=8,'zl'=2,'c'=2,'x'=4] {'x','y','zl','c'}, dimensions={0} | all-to-all | bytes 524288 | tf_op jit(solution)/shard_map/all_to_all | solution.py:141
  77.4 0.1 share_kernel.2
  77.5 14.2 %all_to_all.28.parts_ref = f32[8,8,128]{2,1,0:T(8,128)S(1)} all-to-all(f32[8,8,128]{2,1,0:T(8,128)S(1)} %share_kernel.2), channel_id=1, replica_groups=mesh['y'=4,'zh'=8,'zl'=2,'c'=2,'x'=4] {'zh'}, dimensions={0} | all-to-all | bytes 65536 | tf_op jit(solution)/shard_map/all_to_all | solution.py:141
  91.6 0.7 share_kernel.3
  92.4 5.6 %all-to-all-start.4 = ((f32[64,8,128]{2,1,0:T(8,128)}), f32[64,8,128]{2,1,0:T(8,128)S(1)}, u32[]{:S(2)}, u32[]{:S(2)}) async-start(f32[64,8,128]{2,1,0:T(8,128)} %share_kernel.3), calls=%async_computation.4 | async-start | bytes 524288 | tf_op jit(solution)/shard_map/all_to_all | solution.py:141
  98.0 10.1 %all-to-all-done.4.pieces_ref = f32[64,8,128]{2,1,0:T(8,128)S(1)} async-done(((f32[64,8,128]{2,1,0:T(8,128)}), f32[64,8,128]{2,1,0:T(8,128)S(1)}, u32[]{:S(2)}, u32[]{:S(2)}) %all-to-all-start.4) | async-done | bytes 262176 | tf_op jit(solution)/shard_map/all_to_all | solution.py:141
  108.1 4.4 %update.1 = bf16[512,256]{1,0:T(8,128)(2,1)} custom-call(s32[1]{0:T(128)} %bitcast.link_ref, s32[16]{0:T(128)S(1)} %copy-done.3, f32[64,8,128]{2,1,0:T(8,128)S(1)} %all-to-all-done.4.pieces_ref, bf16[2048,256]{1,0:T(8,128)(2,1)S(1)} %copy-done.1), custom_call_target="tpu_custom_call" | custom-call | tf_op jit(solution)/shard_map/update/pallas_call | solution.py:177
  (9 shorter events, 0.0 us)
Async XLA Ops:
  0.0 0.7 copy-start.6
  0.7 0.7 copy-start.7
  1.5 0.7 copy-start.3
  2.1 1.2 %copy-start = (bf16[2048,256]{1,0:T(8,128)(2,1)S(1)}, bf16[2048,256]{1,0:T(8,128)(2,1)}, u32[]{:S(2)}) copy-start(bf16[2048,256]{1,0:T(8,128)(2,1)} %states_ref.3) | copy-start | bytes 3145732
  3.3 1.2 %copy-start.2 = (bf16[1,32,128,128]{3,2,1,0:T(8,128)(2,1)S(1)}, bf16[1,32,128,128]{3,2,1,0:T(8,128)(2,1)}, u32[]{:S(2)}) copy-start(bf16[1,32,128,128]{3,2,1,0:T(8,128)(2,1)} %param.9) | copy-start | bytes 3145732
  12.6 10.3 %collective-permute-start = (f32[8,64,256]{2,1,0:T(8,128)S(1)}, f32[8,64,256]{2,1,0:T(8,128)S(1)}, u32[]{:S(2)}, u32[]{:S(2)}) collective-permute-start(f32[8,64,256]{2,1,0:T(8,128)S(1)} %get-tuple-element.8), channel_id=1, source_target_pairs={{0,4},{4,0},{1,5},{5,1},{2,6},{6,2},{3,7},{7,3},{8,12},{12,8},{9,1... | collective-permute-start | bytes 1572872 | tf_op jit(solution)/shard_map/ppermute | solution.py:168
  35.3 23.0 %copy-start.4 = (f32[1,8]{1,0:T(1,128)S(1)}, f32[1,8]{1,0:T(1,128)}, u32[]{:S(2)}) copy-start(f32[1,8]{1,0:T(1,128)} %counts_ref.1) | copy-start | bytes 100
  35.3 23.0 %copy-start.5 = (f32[1,8]{1,0:T(1,128)S(1)}, f32[1,8]{1,0:T(1,128)}, u32[]{:S(2)}) copy-start(f32[1,8]{1,0:T(1,128)} %var_ref.1) | copy-start | bytes 100
  58.3 49.8 %copy-start.1 = (bf16[2048,256]{1,0:T(8,128)(2,1)S(1)}, bf16[2048,256]{1,0:T(8,128)(2,1)}, u32[]{:S(2)}) copy-start(bf16[2048,256]{1,0:T(8,128)(2,1)} %states_ref.3) | copy-start | bytes 3145732
  92.4 15.7 %all-to-all-start.4 = ((f32[64,8,128]{2,1,0:T(8,128)}), f32[64,8,128]{2,1,0:T(8,128)S(1)}, u32[]{:S(2)}, u32[]{:S(2)}) async-start(f32[64,8,128]{2,1,0:T(8,128)} %share_kernel.3), calls=%async_computation.4 | async-start | bytes 524288 | tf_op jit(solution)/shard_map/all_to_all | solution.py:141

commit v3 on v2

v3 whole, which is shorter than its diff:
```python
import jax
import jax.numpy as jnp
from jax import lax
from jax.experimental import pallas as pl
from jax.experimental.pallas import tpu as pltpu
from jax.sharding import Mesh
from jax.sharding import PartitionSpec as P

NLB = 8
NS_ITERS = 4
F32 = jnp.float32
BF16 = jnp.bfloat16
ORIG = ("y", "zh", "zl", "c")
SLAB = ("x", "y", "zl", "c")
VMEM = pl.BlockSpec(memory_space=pltpu.VMEM)
SMEM = pl.BlockSpec(memory_space=pltpu.SMEM)
HBM = pl.BlockSpec(memory_space=pltpu.HBM)
DEPTH = 8
WHOLE = pltpu.CompilerParams(vmem_limit_bytes=58 * 2**20)
PARAMS = pltpu.CompilerParams(vmem_limit_bytes=40 * 2**20)


def halves(a):
    high = a.astype(BF16)
    return high, (a - high.astype(F32)).astype(BF16)


def dot(a, b):
    return jnp.dot(a, b, preferred_element_type=F32)


def dot3(a, b):
    (ah, al), (bh, bl) = a, b
    return dot(ah, bh) + (dot(ah, bl) + dot(al, bh))


def term_kernel(
    core_ref, ids_hbm, targets_hbm, live_hbm, states_hbm, tiles_hbm, keep_ref, send_ref,
    ids_ref, targets_ref, live_ref, states_ref, tiles_ref, list_ref, sems,
):
    slots, _, blocks = ids_ref.shape
    stored, link_rows, block_rows = tiles_ref.shape
    states_dev, members = states_hbm.shape
    steps = list_ref.shape[0] // DEPTH
    empty = blocks * stored
    copies = [
        pltpu.make_async_copy(there, here, sems.at[i])
        for i, (there, here) in enumerate(
            (
                (ids_hbm, ids_ref),
                (targets_hbm, targets_ref),
                (live_hbm, live_ref),
                (states_hbm, states_ref.at[pl.ds(0, states_dev)]),
                (tiles_hbm, tiles_ref),
            )
        )
    ]
    for copy in copies:
        copy.start()
    for k in range(steps * DEPTH):
        list_ref[k] = empty
    keep_ref[...] = jnp.zeros_like(keep_ref)
    send_ref[...] = jnp.zeros_like(send_ref)
    states_ref[states_dev:, :] = jnp.zeros((block_rows, members), BF16)
    copies[0].wait()
    copies[1].wait()

    def bump(words, target):
        one = jnp.left_shift(jnp.int32(1), (target & 3) * 8)
        return words[0] + jnp.where(target < 4, one, 0), words[1] + jnp.where(target < 4, 0, one)

    def count(b, words):
        for t in range(slots):
            words = bump(words, targets_ref[t, 0, b])
        return words

    def put(b, words):
        for t in range(slots):
            target = targets_ref[t, 0, b]
            at = jnp.right_shift(jnp.where(target < 4, words[0], words[1]), (target & 3) * 8) & 255
            list_ref[at] = target * 1024 + (b * stored + ids_ref[t, 0, b])
            words = bump(words, target)
        return words

    none = jnp.int32(0)
    counted = lax.fori_loop(0, blocks, count, (none, none))
    first_step, starts = none, [none, none]
    for j in range(NLB):
        entries = jnp.right_shift(counted[j // 4], 8 * (j % 4)) & 255
        starts[j // 4] += jnp.left_shift(first_step * DEPTH, 8 * (j % 4))
        first_step += jnp.right_shift(entries + DEPTH - 1, DEPTH.bit_length() - 1)
    lax.fori_loop(0, blocks, put, tuple(starts))

    copies[2].wait()
    copies[3].wait()
    position = lax.broadcasted_iota(jnp.int32, (block_rows, members), 0)
    for b in range(blocks):
        rows = slice(b * block_rows, (b + 1) * block_rows)
        living = (position < live_ref[b]).astype(F32).astype(BF16)
        states_ref[rows, :] = states_ref[rows, :] * living
    copies[4].wait()

    def run(by_core):
        def step(i, carry):
            codes = [list_ref[i * DEPTH + k] for k in range(DEPTH)]
            tiles, states = [], []
            for code in codes:
                first = pl.multiple_of((jnp.right_shift(code, 5) & 31) * block_rows, block_rows)
                tiles.append(tiles_ref[code & 31])
                states.append(states_ref[pl.ds(first, block_rows), :])
            product = dot(jnp.concatenate(tiles, axis=1), jnp.concatenate(states, axis=0))
            target = jnp.right_shift(codes[0], 10)
            chunk = jnp.right_shift(target, 1) * 2
            for g in range(16):
                q, zl, c = g // 4, (g // 2) % 2, g % 2
                at = pl.ds(pl.multiple_of((target & 1) * 32 + q * 8, 8), 8)
                by_core[c][chunk + zl, at, :] += product[g * 8 : g * 8 + 8]
            return carry

        lax.fori_loop(0, steps, step, 0, unroll=steps)

    @pl.when(core_ref[0] == 0)
    def _():
        run((keep_ref, send_ref))

    @pl.when(core_ref[0] == 1)
    def _():
        run((send_ref, keep_ref))


def term(core, ids, targets, live, states, tiles):
    slots, _, blocks = ids.shape
    states_dev, members = states.shape
    steps = (slots * blocks + NLB * (DEPTH - 1)) // DEPTH
    half = jax.ShapeDtypeStruct((8, 64, members), F32)
    return pl.pallas_call(
        term_kernel,
        out_shape=(half, half),
        in_specs=[SMEM] + [HBM] * 5,
        out_specs=(VMEM, VMEM),
        scratch_shapes=[
            pltpu.SMEM(ids.shape, jnp.int32),
            pltpu.SMEM(ids.shape, jnp.int32),
            pltpu.SMEM(live.shape, jnp.int32),
            pltpu.VMEM((states_dev + tiles.shape[2], members), BF16),
            pltpu.VMEM(tiles.shape, BF16),
            pltpu.SMEM((steps * DEPTH,), jnp.int32),
            pltpu.SemaphoreType.DMA((5,)),
        ],
        compiler_params=WHOLE,
        name="term",
    )(core, ids, targets, live, states, tiles)


def as_column(ref):
    count = ref.shape[1]
    at = lambda dim: lax.broadcasted_iota(jnp.int32, (count, count), dim)
    return jnp.sum(jnp.where(at(0) == at(1), ref[...], 0.0), axis=1, keepdims=True)


def rows_kernel(parts_ref, counts_ref, var_ref, out_ref):
    total = jnp.sum(parts_ref[...], axis=0)
    rows = total.shape[0]
    out_ref[0:rows, :] = total[:, :128]
    out_ref[rows : 2 * rows, :] = total[:, 128:]
    lane = lax.broadcasted_iota(jnp.int32, (8, 128), 1)
    counts, variance = as_column(counts_ref), as_column(var_ref)
    out_ref[2 * rows : 2 * rows + 8, :] = jnp.where(lane == 0, counts, jnp.where(lane == 1, variance, 0.0))


def gram_kernel(parts_ref, out_ref):
    rows = (parts_ref.shape[1] - 8) // 2
    left = jnp.sum(parts_ref[:, 0:rows, :], axis=0)
    right = jnp.sum(parts_ref[:, rows : 2 * rows, :], axis=0)
    tail = parts_ref[:, 2 * rows :, :].reshape(rows, 128)
    counts, variance = tail[:, 0:1], tail[:, 1:2]
    mean = jnp.sum(left + right, axis=1, keepdims=True) * (1.0 / 256.0)
    spread = jnp.concatenate([left - mean, right - mean], axis=1)
    weights = 1.0 / variance
    forcing = jnp.sum(spread * (weights * (counts - mean)), axis=0, keepdims=True)
    gram = dot3(halves(spread.T), halves(spread * weights))
    out_ref[...] = jnp.zeros_like(out_ref)
    out_ref[0:16] = gram[:128, :128].reshape(16, 8, 128)
    out_ref[16:32] = gram[:128, 128:].reshape(16, 8, 128)
    out_ref[32:48] = gram[128:, 128:].reshape(16, 8, 128)
    out_ref[48, 0:1, :] = forcing[:, :128]
    out_ref[48, 1:2, :] = forcing[:, 128:]


def share_kernel(parts_ref, out_ref):
    total = jnp.sum(parts_ref[...], axis=0)
    out_ref[...] = jnp.broadcast_to(total[None], out_ref.shape)


def update_kernel(link_ref, live_ref, pieces_ref, states_hbm, out_ref, states_ref, sem):
    own_rows, members = states_ref.shape
    own = pl.ds(pl.multiple_of(link_ref[0] * own_rows, own_rows), own_rows)
    copy = pltpu.make_async_copy(states_hbm.at[own], states_ref, sem)
    copy.start()
    first = pieces_ref[0:16].reshape(128, 128)
    across = pieces_ref[16:32].reshape(128, 128)
    last = pieces_ref[32:48].reshape(128, 128)
    gram = jnp.concatenate(
        [jnp.concatenate([first, across], axis=1), jnp.concatenate([across.T, last], axis=1)], axis=0
    )
    forcing = jnp.concatenate([pieces_ref[48, 0:1, :], pieces_ref[48, 1:2, :]], axis=1)
    at = lambda dim: lax.broadcasted_iota(jnp.int32, (members, members), dim)
    identity = jnp.where(at(0) == at(1), 1.0, 0.0).astype(F32)
    system = identity + gram * (1.0 / (members - 1.0))
    bound = jnp.max(jnp.sum(jnp.abs(system), axis=0, keepdims=True), axis=1, keepdims=True)
    root = system * (1.0 / bound)
    inverse = identity
    for sweep in range(NS_ITERS):
        if sweep == 0:
            middle = 1.5 * identity - 0.5 * root
            inverse = middle
        else:
            middle = 1.5 * identity - 0.5 * dot3(halves(inverse), halves(root))
        middle_halves = halves(middle)
        if sweep > 0:
            inverse = dot3(middle_halves, halves(inverse))
        if sweep < NS_ITERS - 1:
            root = dot3(halves(root), middle_halves)
    inner = dot3(halves(jnp.broadcast_to(forcing, (8, members))), halves(inverse))[0:1]
    mean_weights = jnp.sum(inverse * inner, axis=1, keepdims=True) * (1.0 / (bound * (members - 1.0)))
    transform = inverse * lax.rsqrt(bound) + mean_weights
    transform += (1.0 - jnp.sum(transform, axis=0, keepdims=True)) * (1.0 / members)
    high, low = halves(transform)
    copy.wait()
    own_blocks = own_rows // 128
    position = lax.broadcasted_iota(jnp.int32, (128, members), 0)
    for k in range(own_blocks):
        rows = slice(k * 128, k * 128 + 128)
        states = states_ref[rows, :]
        updated = dot(states, high) + dot(states, low)
        live = live_ref[link_ref[0] * own_blocks + k]
        out_ref[rows, :] = jnp.where(position < live, updated, states.astype(F32)).astype(BF16)


def all_to_all(x, axes):
    return lax.all_to_all(x, axes, split_axis=0, concat_axis=0, tiled=True)


def local(kernel, shape, operands):
    return pl.pallas_call(
        kernel,
        out_shape=jax.ShapeDtypeStruct(shape, F32),
        in_specs=[VMEM] * operands,
        out_specs=VMEM,
        compiler_params=PARAMS,
        name=kernel.__name__,
    )


def per_device(background, live_counts, patterns, pattern_ids, link_targets, counts_obs, obs_var):
    states_dev, members = background.shape
    core = lax.axis_index("c").astype(jnp.int32).reshape(1)
    link = lax.axis_index("x").astype(jnp.int32).reshape(1)
    ids, targets = (jnp.transpose(a, (2, 0, 1)) for a in (pattern_ids, link_targets))
    keep, send = term(core, ids, targets, live_counts, background, patterns[0])
    of_chip = keep + lax.ppermute(send, "c", [(0, 1), (1, 0)])
    parts = all_to_all(of_chip, ("y", "zl"))
    own = local(rows_kernel, (136, 128), 3)(parts, counts_obs, obs_var)
    column = lax.all_gather(own, "zh")
    gram = local(gram_kernel, (64, 8, 128), 1)(column)
    shared = local(share_kernel, (64, 8, 128), 1)(all_to_all(gram, SLAB))
    pieces = all_to_all(shared, SLAB)
    own_rows = states_dev // lax.axis_size("x")
    return pl.pallas_call(
        update_kernel,
        out_shape=jax.ShapeDtypeStruct((own_rows, members), BF16),
        in_specs=[SMEM, SMEM, VMEM, HBM],
        out_specs=VMEM,
        scratch_shapes=[pltpu.VMEM((own_rows, members), BF16), pltpu.SemaphoreType.DMA],
        compiler_params=PARAMS,
        name="update",
    )(link, live_counts, pieces, background)


def solution(mesh):
    torus = Mesh(mesh.devices.reshape(4, 8, 2, 2, 4), ("y", "zh", "zl", "c", "x"))
    return jax.shard_map(
        per_device,
        mesh=torus,
        in_specs=(
            P(ORIG, None),
            P(ORIG),
            P("x", ORIG, None, None),
            P("x", ORIG, None),
            P("x", ORIG, None),
            P("x", ORIG),
            P("x", ORIG),
        ),
        out_specs=P((*ORIG, "x"), None),
        check_vma=False,
    )
```

time: 113 us -> 102 us (0.903)
  blocking collectives: 68.1 us -> 63.2 us
  local copies, waits for them, and re-layouts: 4.58 us -> 0.02 us
  Pallas kernels: 13.6 us -> 12.1 us
    all_to_all x4 -> x2, blocking collectives: 68.1 us -> 34.4 us  [all_to_all(): return lax.all_to_all(x, axes, split_axis=0, concat_axis=0, tiled=True)]
    all_gather x0 -> x1, blocking collectives: none -> 28.9 us  [per_device(): column = lax.all_gather(own, 'zh')]
    unnamed x18 -> x8, local copies, waits for them, and re-layouts: 4.58 us -> 0.02 us
    pallas_call x5 -> x4, Pallas kernels: 9.23 us -> 7.61 us  [the longest x1 6.34 us: term(): pl.pallas_call(term_kernel, out_shape=(half, half), in_specs=[SMEM] + [HB...]
where the time goes in v3:
time: 102 us
  blocking collectives  63.2 us (62%)
  starting transfers between devices  13.3 us (13%)
  Pallas kernels  12.1 us (12%)
  waiting for transfers between devices  11.8 us (12%)
  other arithmetic  1.11 us (1%)
    all_to_all x2, blocking collectives, all_to_all(): return lax.all_to_all(x, axes, split_axis=0, concat_axis=0, tiled=True)  34.4 us
    all_gather x1, blocking collectives, per_device(): column = lax.all_gather(own, 'zh')  28.9 us
    all_to_all x1, waiting for transfers between devices, all_to_all(): return lax.all_to_all(x, axes, split_axis=0, concat_axis=0, tiled=True)  10.1 us
    ppermute x1, starting transfers between devices, per_device(): of_chip = keep + lax.ppermute(send, 'c', [(0, 1), (1, 0)])  8.78 us
    pallas_call x1, Pallas kernels, term(): pl.pallas_call(term_kernel, out_shape=(half, half), in_specs=[SMEM] + [HB...  6.34 us
    all_to_all x1, starting transfers between devices, all_to_all(): return lax.all_to_all(x, axes, split_axis=0, concat_axis=0, tiled=True)  4.52 us
    pallas_call x1, Pallas kernels, per_device(): pl.pallas_call(update_kernel, out_shape=jax.ShapeDtypeStruct((own_rows, m...  4.45 us
  transfers between devices with their start and end apart: 2, of which 2 were waited for; matrix products, arithmetic and copies ran while one was open for 0% of the time, Pallas kernels for 0%

profile of v3, /device:TPU:1, one launch (start us, length us, event | category | flops | bytes accessed | tf_op | source)
XLA Modules:
  0.0 101.6 jit_solution(4861675529274245681)
XLA Ops:
  0.0 6.3 %term.1 = (f32[8,64,256]{2,1,0:T(8,128)}, f32[8,64,256]{2,1,0:T(8,128)}) custom-call(s32[1]{0:T(128)} %bitcast.1.core_ref, s32[12,1,16]{2,1,0:T(1,128)} %bitcast.8, s32[12,1,16]{2,1,0:T(1,128)} %bitcast.9, s32[16]{0:T(128)} %live_ref.1, bf16[2048,256]{1,0:T(8,128)(2,1)} %states_hbm.3, bf16[32,128,128]{2,1,0:T(8,128)(2,1)} %bitcast.7), custom_call_target="tpu_custom_call" | custom-call | tf_op jit(solution)/shard_map/term/pallas_call | solution.py:136
  6.3 8.8 %collective-permute-start = (f32[8,64,256]{2,1,0:T(8,128)}, f32[8,64,256]{2,1,0:T(8,128)S(1)}, u32[]{:S(2)}, u32[]{:S(2)}) collective-permute-start(f32[8,64,256]{2,1,0:T(8,128)} %get-tuple-element.8), channel_id=1, source_target_pairs={{0,4},{4,0},{1,5},{5,1},{2,6},{6,2},{3,7},{7,3},{8,12},{12,8},{9,1... | collective-permute-start | bytes 1572872 | tf_op jit(solution)/shard_map/ppermute | solution.py:261
  15.1 1.7 %collective-permute-done = f32[8,64,256]{2,1,0:T(8,128)S(1)} collective-permute-done((f32[8,64,256]{2,1,0:T(8,128)}, f32[8,64,256]{2,1,0:T(8,128)S(1)}, u32[]{:S(2)}, u32[]{:S(2)}) %collective-permute-start) | collective-permute-done | bytes 524320 | tf_op jit(solution)/shard_map/ppermute | solution.py:261
  16.9 1.1 %add.3 = f32[8,64,256]{2,1,0:T(8,128)S(1)} add(f32[8,64,256]{2,1,0:T(8,128)} %get-tuple-element.7, f32[8,64,256]{2,1,0:T(8,128)S(1)} %collective-permute-done) | non-fusion elementwise | flops 131072 | bytes 1572864 | tf_op jit(solution)/shard_map/add | solution.py:261
  18.0 0.0 copy-start.2
  18.0 0.0 copy-start.3
  18.0 12.2 %all_to_all.15.parts_ref = f32[8,64,256]{2,1,0:T(8,128)S(1)} all-to-all(f32[8,64,256]{2,1,0:T(8,128)S(1)} %add.3), channel_id=1, replica_groups=mesh['y'=4,'zh'=8,'zl'=2,'c'=2,'x'=4] {'y','zl'}, dimensions={0} | all-to-all | bytes 1048576 | tf_op jit(solution)/shard_map/all_to_all | solution.py:241
  30.3 0.0 copy-done.2
  30.3 0.0 copy-done.3
  30.3 0.1 rows_kernel.1
  30.3 28.9 %all-gather = f32[1088,128]{1,0:T(8,128)S(1)} all-gather(f32[136,128]{1,0:T(8,128)S(1)} %rows_kernel.1), channel_id=2, replica_groups=mesh['y'=4,'zh'=8,'zl'=2,'c'=2,'x'=4] {'zh'}, dimensions={0}, use_global_device_ids=true | all-gather | bytes 626688 | tf_op jit(solution)/shard_map/all_gather | solution.py:264
  59.2 0.0 copy-start
  59.2 0.4 gram_kernel.1
  59.6 22.1 %all_to_all.16.parts_ref = f32[64,8,128]{2,1,0:T(8,128)S(1)} all-to-all(f32[64,8,128]{2,1,0:T(8,128)S(1)} %gram_kernel.1), channel_id=1, replica_groups=mesh['y'=4,'zh'=8,'zl'=2,'c'=2,'x'=4] {'x','y','zl','c'}, dimensions={0} | all-to-all | bytes 524288 | tf_op jit(solution)/shard_map/all_to_all | solution.py:241
  81.7 0.8 share_kernel.1
  82.5 4.5 %all-to-all-start.2 = ((f32[64,8,128]{2,1,0:T(8,128)}), f32[64,8,128]{2,1,0:T(8,128)S(1)}, u32[]{:S(2)}, u32[]{:S(2)}) async-start(f32[64,8,128]{2,1,0:T(8,128)} %share_kernel.1), calls=%async_computation.2 | async-start | bytes 524288 | tf_op jit(solution)/shard_map/all_to_all | solution.py:241
  87.1 0.0 copy-start.1
  87.1 10.1 %all-to-all-done.2.pieces_ref = f32[64,8,128]{2,1,0:T(8,128)S(1)} async-done(((f32[64,8,128]{2,1,0:T(8,128)}), f32[64,8,128]{2,1,0:T(8,128)S(1)}, u32[]{:S(2)}, u32[]{:S(2)}) %all-to-all-start.2) | async-done | bytes 262176 | tf_op jit(solution)/shard_map/all_to_all | solution.py:241
  97.2 0.0 copy-done
  97.2 0.0 copy-done.1
  97.2 4.4 %update.1 = bf16[512,256]{1,0:T(8,128)(2,1)} custom-call(s32[1]{0:T(128)} %bitcast.link_ref, s32[16]{0:T(128)S(1)} %copy-done.1, f32[64,8,128]{2,1,0:T(8,128)S(1)} %all-to-all-done.2.pieces_ref, bf16[2048,256]{1,0:T(8,128)(2,1)S(1)} %copy-done), custom_call_target="tpu_custom_call" | custom-call | tf_op jit(solution)/shard_map/update/pallas_call | solution.py:269
Async XLA Ops:
  6.3 10.5 %collective-permute-start = (f32[8,64,256]{2,1,0:T(8,128)}, f32[8,64,256]{2,1,0:T(8,128)S(1)}, u32[]{:S(2)}, u32[]{:S(2)}) collective-permute-start(f32[8,64,256]{2,1,0:T(8,128)} %get-tuple-element.8), channel_id=1, source_target_pairs={{0,4},{4,0},{1,5},{5,1},{2,6},{6,2},{3,7},{7,3},{8,12},{12,8},{9,1... | collective-permute-start | bytes 1572872 | tf_op jit(solution)/shard_map/ppermute | solution.py:261
  18.0 12.3 %copy-start.2 = (f32[1,8]{1,0:T(1,128)S(1)}, f32[1,8]{1,0:T(1,128)}, u32[]{:S(2)}) copy-start(f32[1,8]{1,0:T(1,128)} %counts_ref.1) | copy-start | bytes 100
  18.0 12.3 %copy-start.3 = (f32[1,8]{1,0:T(1,128)S(1)}, f32[1,8]{1,0:T(1,128)}, u32[]{:S(2)}) copy-start(f32[1,8]{1,0:T(1,128)} %var_ref.1) | copy-start | bytes 100
  59.2 38.0 %copy-start = (bf16[2048,256]{1,0:T(8,128)(2,1)S(1)}, bf16[2048,256]{1,0:T(8,128)(2,1)}, u32[]{:S(2)}) copy-start(bf16[2048,256]{1,0:T(8,128)(2,1)} %states_hbm.3) | copy-start | bytes 3145732
  82.5 14.6 %all-to-all-start.2 = ((f32[64,8,128]{2,1,0:T(8,128)}), f32[64,8,128]{2,1,0:T(8,128)S(1)}, u32[]{:S(2)}, u32[]{:S(2)}) async-start(f32[64,8,128]{2,1,0:T(8,128)} %share_kernel.1), calls=%async_computation.2 | async-start | bytes 524288 | tf_op jit(solution)/shard_map/all_to_all | solution.py:241
  87.1 10.1 %copy-start.1 = (s32[16]{0:T(128)S(1)}, s32[16]{0:T(128)}, u32[]{:S(2)}) copy-start(s32[16]{0:T(128)} %live_ref.1) | copy-start | bytes 196

commit v4 on v3

--- a/solution.py
+++ b/solution.py
@@ -10,7 +10,7 @@
 NS_ITERS = 4
 F32 = jnp.float32
 BF16 = jnp.bfloat16
-ORIG = ("y", "zh", "zl", "c")
+ORIG = ("y", "zq", "zp", "zl", "c")
 SLAB = ("x", "y", "zl", "c")
 VMEM = pl.BlockSpec(memory_space=pltpu.VMEM)
 SMEM = pl.BlockSpec(memory_space=pltpu.SMEM)
@@ -158,33 +158,41 @@
     return jnp.sum(jnp.where(at(0) == at(1), ref[...], 0.0), axis=1, keepdims=True)
 
 
-def rows_kernel(parts_ref, counts_ref, var_ref, out_ref):
+def rows_kernel(pair_ref, parts_ref, counts_ref, var_ref, out_ref):
     total = jnp.sum(parts_ref[...], axis=0)
     rows = total.shape[0]
     out_ref[0:rows, :] = total[:, :128]
     out_ref[rows : 2 * rows, :] = total[:, 128:]
-    lane = lax.broadcasted_iota(jnp.int32, (8, 128), 1)
+    lane = lax.broadcasted_iota(jnp.int32, (8, 128), 1) - 2 * pair_ref[0]
     counts, variance = as_column(counts_ref), as_column(var_ref)
     out_ref[2 * rows : 2 * rows + 8, :] = jnp.where(lane == 0, counts, jnp.where(lane == 1, variance, 0.0))
 
 
-def gram_kernel(parts_ref, out_ref):
+def gram_kernel(core_ref, parts_ref, out_ref):
     rows = (parts_ref.shape[1] - 8) // 2
-    left = jnp.sum(parts_ref[:, 0:rows, :], axis=0)
-    right = jnp.sum(parts_ref[:, rows : 2 * rows, :], axis=0)
-    tail = parts_ref[:, 2 * rows :, :].reshape(rows, 128)
-    counts, variance = tail[:, 0:1], tail[:, 1:2]
+    quads = parts_ref.shape[0] // 2
+
+    def both(first, count):
+        return jnp.concatenate(
+            [sum(parts_ref[2 * k + c, first : first + count, :] for k in range(quads)) for c in range(2)], axis=0
+        )
+
+    left, right = both(0, rows), both(rows, rows)
+    tails = [parts_ref[2 * k + c, 2 * rows : 2 * rows + 8, :] for c in range(2) for k in range(quads)]
+    column = lambda at: jnp.concatenate([t[:, 2 * p + at : 2 * p + at + 1] for t in tails for p in range(2)], axis=0)
+    counts, variance = column(0), column(1)
     mean = jnp.sum(left + right, axis=1, keepdims=True) * (1.0 / 256.0)
-    spread = jnp.concatenate([left - mean, right - mean], axis=1)
+    left, right = left - mean, right - mean
     weights = 1.0 / variance
-    forcing = jnp.sum(spread * (weights * (counts - mean)), axis=0, keepdims=True)
-    gram = dot3(halves(spread.T), halves(spread * weights))
-    out_ref[...] = jnp.zeros_like(out_ref)
-    out_ref[0:16] = gram[:128, :128].reshape(16, 8, 128)
-    out_ref[16:32] = gram[:128, 128:].reshape(16, 8, 128)
-    out_ref[32:48] = gram[128:, 128:].reshape(16, 8, 128)
-    out_ref[48, 0:1, :] = forcing[:, :128]
-    out_ref[48, 1:2, :] = forcing[:, 128:]
+    weighted = weights * (counts - mean)
+    mine = core_ref[0] == 0
+    own = jnp.where(mine, left, right)
+    half = jnp.where(mine, left[:, :64], left[:, 64:])
+    out_ref[0:16] = dot3(halves(own.T), halves(own * weights)).reshape(16, 8, 128)
+    out_ref[16:24] = dot3(halves(half.T), halves(right * weights)).reshape(8, 8, 128)
+    forcing = [jnp.sum(part * weighted, axis=0, keepdims=True) for part in (left, right)]
+    out_ref[24] = jnp.concatenate([*forcing, jnp.zeros((6, 128), F32)], axis=0)
+    out_ref[25:] = jnp.zeros((out_ref.shape[0] - 25, 8, 128), F32)
 
 
 def share_kernel(parts_ref, out_ref):
@@ -197,13 +205,14 @@
     own = pl.ds(pl.multiple_of(link_ref[0] * own_rows, own_rows), own_rows)
     copy = pltpu.make_async_copy(states_hbm.at[own], states_ref, sem)
     copy.start()
-    first = pieces_ref[0:16].reshape(128, 128)
-    across = pieces_ref[16:32].reshape(128, 128)
-    last = pieces_ref[32:48].reshape(128, 128)
+    by_core = pieces_ref[...].reshape(pieces_ref.shape[0] // 2, 2, 8, 128)
+    first = by_core[0:16, 0].reshape(128, 128)
+    last = by_core[0:16, 1].reshape(128, 128)
+    across = jnp.concatenate([by_core[16:24, c].reshape(64, 128) for c in range(2)], axis=0)
     gram = jnp.concatenate(
         [jnp.concatenate([first, across], axis=1), jnp.concatenate([across.T, last], axis=1)], axis=0
     )
-    forcing = jnp.concatenate([pieces_ref[48, 0:1, :], pieces_ref[48, 1:2, :]], axis=1)
+    forcing = jnp.concatenate([by_core[24, 0, 0:1], by_core[24, 0, 1:2]], axis=1)
     at = lambda dim: lax.broadcasted_iota(jnp.int32, (members, members), dim)
     identity = jnp.where(at(0) == at(1), 1.0, 0.0).astype(F32)
     system = identity + gram * (1.0 / (members - 1.0))
@@ -241,11 +250,11 @@
     return lax.all_to_all(x, axes, split_axis=0, concat_axis=0, tiled=True)
 
 
-def local(kernel, shape, operands):
+def local(kernel, shape, operands, scalars=0):
     return pl.pallas_call(
         kernel,
         out_shape=jax.ShapeDtypeStruct(shape, F32),
-        in_specs=[VMEM] * operands,
+        in_specs=[SMEM] * scalars + [VMEM] * operands,
         out_specs=VMEM,
         compiler_params=PARAMS,
         name=kernel.__name__,
@@ -254,16 +263,16 @@
 
 def per_device(background, live_counts, patterns, pattern_ids, link_targets, counts_obs, obs_var):
     states_dev, members = background.shape
-    core = lax.axis_index("c").astype(jnp.int32).reshape(1)
-    link = lax.axis_index("x").astype(jnp.int32).reshape(1)
+    core, link, pair = (lax.axis_index(axis).astype(jnp.int32).reshape(1) for axis in ("c", "x", "zp"))
     ids, targets = (jnp.transpose(a, (2, 0, 1)) for a in (pattern_ids, link_targets))
     keep, send = term(core, ids, targets, live_counts, background, patterns[0])
     of_chip = keep + lax.ppermute(send, "c", [(0, 1), (1, 0)])
     parts = all_to_all(of_chip, ("y", "zl"))
-    own = local(rows_kernel, (136, 128), 3)(parts, counts_obs, obs_var)
-    column = lax.all_gather(own, "zh")
-    gram = local(gram_kernel, (64, 8, 128), 1)(column)
-    shared = local(share_kernel, (64, 8, 128), 1)(all_to_all(gram, SLAB))
+    own = local(rows_kernel, (136, 128), 3, 1)(pair, parts, counts_obs, obs_var)
+    own += lax.ppermute(own, "zp", [(0, 1), (1, 0)])
+    column = lax.all_gather(own, ("zq", "c"))
+    gram = local(gram_kernel, (32, 8, 128), 1, 1)(core, column)
+    shared = local(share_kernel, (64, 8, 128), 1)(all_to_all(gram, ("x", "y", "zl")))
     pieces = all_to_all(shared, SLAB)
     own_rows = states_dev // lax.axis_size("x")
     return pl.pallas_call(
@@ -278,7 +287,7 @@
 
 
 def solution(mesh):
-    torus = Mesh(mesh.devices.reshape(4, 8, 2, 2, 4), ("y", "zh", "zl", "c", "x"))
+    torus = Mesh(mesh.devices.reshape(4, 4, 2, 2, 2, 4), ("y", "zq", "zp", "zl", "c", "x"))
     return jax.shard_map(
         per_device,
         mesh=torus,

time: 102 us -> 101 us (level)
  blocking collectives: 63.2 us -> 40.6 us
  waiting for transfers between devices: 11.8 us -> 26 us
  starting transfers between devices: 13.3 us -> 19.8 us
    all_to_all x2 -> x1, blocking collectives: 34.4 us -> 12.2 us  [all_to_all(): return lax.all_to_all(x, axes, split_axis=0, concat_axis=0, tiled=True)]
    all_to_all x1 -> x2, waiting for transfers between devices: 10.1 us -> 19.5 us  [all_to_all(): return lax.all_to_all(x, axes, split_axis=0, concat_axis=0, tiled=True)]
    ppermute x0 -> x1, waiting for transfers between devices: none -> 4.77 us  [per_device(): own += lax.ppermute(own, 'zp', [(0, 1), (1, 0)])]
    all_to_all x1 -> x2, starting transfers between devices: 4.52 us -> 9.11 us  [all_to_all(): return lax.all_to_all(x, axes, split_axis=0, concat_axis=0, tiled=True)]
    ppermute x0 -> x1, starting transfers between devices: none -> 1.91 us  [per_device(): own += lax.ppermute(own, 'zp', [(0, 1), (1, 0)])]
  transfers between devices with their start and end apart: 2 -> 4, of which waited for: 2 -> 4; matrix products, arithmetic and copies ran while one was open for 0% -> 0% of each run, Pallas kernels for 0% -> 0%
where the time goes in v4:
time: 101 us
  blocking collectives  40.6 us (40%)
  waiting for transfers between devices  26 us (26%)
  starting transfers between devices  19.8 us (20%)
  Pallas kernels  12.1 us (12%)
  other arithmetic  1.9 us (2%)
    all_gather x1, blocking collectives, per_device(): column = lax.all_gather(own, ('zq', 'c'))  28.4 us
    all_to_all x2, waiting for transfers between devices, all_to_all(): return lax.all_to_all(x, axes, split_axis=0, concat_axis=0, tiled=True)  19.5 us
    all_to_all x1, blocking collectives, all_to_all(): return lax.all_to_all(x, axes, split_axis=0, concat_axis=0, tiled=True)  12.2 us
    all_to_all x2, starting transfers between devices, all_to_all(): return lax.all_to_all(x, axes, split_axis=0, concat_axis=0, tiled=True)  9.11 us
    ppermute x1, starting transfers between devices, per_device(): of_chip = keep + lax.ppermute(send, 'c', [(0, 1), (1, 0)])  8.78 us
    pallas_call x1, Pallas kernels, term(): pl.pallas_call(term_kernel, out_shape=(half, half), in_specs=[SMEM] + [HB...  6.35 us
    ppermute x1, waiting for transfers between devices, per_device(): own += lax.ppermute(own, 'zp', [(0, 1), (1, 0)])  4.77 us
    pallas_call x1, Pallas kernels, per_device(): pl.pallas_call(update_kernel, out_shape=jax.ShapeDtypeStruct((own_rows, m...  4.45 us
  transfers between devices with their start and end apart: 4, of which 4 were waited for; matrix products, arithmetic and copies ran while one was open for 0% of the time, Pallas kernels for 0%

profile of v4, /device:TPU:1, one launch (start us, length us, event | category | flops | bytes accessed | tf_op | source)
XLA Modules:
  0.0 100.5 jit_solution(7122308382116569670)
XLA Ops:
  0.0 6.3 %term.1 = (f32[8,64,256]{2,1,0:T(8,128)}, f32[8,64,256]{2,1,0:T(8,128)}) custom-call(s32[1]{0:T(128)} %bitcast.1.core_ref, s32[12,1,16]{2,1,0:T(1,128)} %bitcast.9, s32[12,1,16]{2,1,0:T(1,128)} %bitcast.10, s32[16]{0:T(128)} %live_ref.1, bf16[2048,256]{1,0:T(8,128)(2,1)} %states_hbm.3, bf16[32,128,128]{2,1,0:T(8,128)(2,1)} %bitcast.8), custom_call_target="tpu_custom_call" | custom-call | tf_op jit(solution)/shard_map/term/pallas_call | solution.py:136
  6.4 8.8 %collective-permute-start = (f32[8,64,256]{2,1,0:T(8,128)}, f32[8,64,256]{2,1,0:T(8,128)S(1)}, u32[]{:S(2)}, u32[]{:S(2)}) collective-permute-start(f32[8,64,256]{2,1,0:T(8,128)} %get-tuple-element.8), channel_id=1, source_target_pairs={{0,4},{4,0},{1,5},{5,1},{2,6},{6,2},{3,7},{7,3},{8,12},{12,8},{9,1... | collective-permute-start | bytes 1572872 | tf_op jit(solution)/shard_map/ppermute | solution.py:269
  15.1 1.7 %collective-permute-done = f32[8,64,256]{2,1,0:T(8,128)S(1)} collective-permute-done((f32[8,64,256]{2,1,0:T(8,128)}, f32[8,64,256]{2,1,0:T(8,128)S(1)}, u32[]{:S(2)}, u32[]{:S(2)}) %collective-permute-start) | collective-permute-done | bytes 524320 | tf_op jit(solution)/shard_map/ppermute | solution.py:269
  16.9 1.9 %add.6 = f32[8,64,256]{2,1,0:T(8,128)} add(f32[8,64,256]{2,1,0:T(8,128)} %get-tuple-element.7, f32[8,64,256]{2,1,0:T(8,128)S(1)} %collective-permute-done) | non-fusion elementwise | flops 131072 | bytes 1572864 | tf_op jit(solution)/shard_map/add | solution.py:269
  18.8 3.5 %all-to-all-start = ((f32[8,64,256]{2,1,0:T(8,128)}), f32[8,64,256]{2,1,0:T(8,128)S(1)}, u32[]{:S(2)}, u32[]{:S(2)}) async-start(f32[8,64,256]{2,1,0:T(8,128)} %add.6), calls=%async_computation | async-start | bytes 1048576 | tf_op jit(solution)/shard_map/all_to_all | solution.py:250
  22.3 0.0 copy-start.2
  22.3 0.0 copy-start.3
  22.3 9.4 %all-to-all-done.parts_ref = f32[8,64,256]{2,1,0:T(8,128)S(1)} async-done(((f32[8,64,256]{2,1,0:T(8,128)}), f32[8,64,256]{2,1,0:T(8,128)S(1)}, u32[]{:S(2)}, u32[]{:S(2)}) %all-to-all-start) | async-done | bytes 524320 | tf_op jit(solution)/shard_map/all_to_all | solution.py:250
  31.7 0.0 copy-done.2
  31.7 0.0 copy-done.3
  31.7 0.1 rows_kernel.1
  31.8 1.9 %collective-permute-start.1 = (f32[136,128]{1,0:T(8,128)S(1)}, f32[136,128]{1,0:T(8,128)S(1)}, u32[]{:S(2)}, u32[]{:S(2)}) collective-permute-start(f32[136,128]{1,0:T(8,128)S(1)} %rows_kernel.1), channel_id=1, source_target_pairs={{0,16},{16,0},{1,17},{17,1},{2,18},{18,2},{3,19},{19,3},{4,20},{20... | collective-permute-start | bytes 208904 | tf_op jit(solution)/shard_map/ppermute | solution.py:272
  33.8 4.8 %collective-permute-done.1 = f32[136,128]{1,0:T(8,128)S(1)} collective-permute-done((f32[136,128]{1,0:T(8,128)S(1)}, f32[136,128]{1,0:T(8,128)S(1)}, u32[]{:S(2)}, u32[]{:S(2)}) %collective-permute-start.1) | collective-permute-done | bytes 69664 | tf_op jit(solution)/shard_map/ppermute | solution.py:272
  38.5 28.4 %all-gather = f32[1088,128]{1,0:T(8,128)S(1)} all-gather(f32[136,128]{1,0:T(8,128)S(1)} %add.7), channel_id=2, replica_groups=mesh['y'=4,'zq'=4,'zp'=2,'zl'=2,'c'=2,'x'=4] {'zq','c'}, dimensions={0}, use_global_device_ids=true | all-gather | bytes 626688 | tf_op jit(solution)/shard_map/all_gather | solution.py:273
  66.9 0.0 copy-start
  66.9 0.4 gram_kernel.1
  67.3 12.2 %all_to_all.15.parts_ref = f32[32,8,128]{2,1,0:T(8,128)S(1)} all-to-all(f32[32,8,128]{2,1,0:T(8,128)S(1)} %gram_kernel.1), channel_id=1, replica_groups=mesh['y'=4,'zq'=4,'zp'=2,'zl'=2,'c'=2,'x'=4] {'x','y','zl'}, dimensions={0} | all-to-all | bytes 262144 | tf_op jit(solution)/shard_map/all_to_all | solution.py:250
  79.6 0.8 share_kernel.1
  80.3 5.6 %all-to-all-start.2 = ((f32[64,8,128]{2,1,0:T(8,128)}), f32[64,8,128]{2,1,0:T(8,128)S(1)}, u32[]{:S(2)}, u32[]{:S(2)}) async-start(f32[64,8,128]{2,1,0:T(8,128)} %share_kernel.1), calls=%async_computation.2 | async-start | bytes 524288 | tf_op jit(solution)/shard_map/all_to_all | solution.py:250
  86.0 0.0 copy-start.1
  86.0 10.1 %all-to-all-done.2.pieces_ref = f32[64,8,128]{2,1,0:T(8,128)S(1)} async-done(((f32[64,8,128]{2,1,0:T(8,128)}), f32[64,8,128]{2,1,0:T(8,128)S(1)}, u32[]{:S(2)}, u32[]{:S(2)}) %all-to-all-start.2) | async-done | bytes 262176 | tf_op jit(solution)/shard_map/all_to_all | solution.py:250
  96.1 0.0 copy-done
  96.1 0.0 copy-done.1
  96.1 4.4 %update.1 = bf16[512,256]{1,0:T(8,128)(2,1)} custom-call(s32[1]{0:T(128)} %bitcast.link_ref, s32[16]{0:T(128)S(1)} %copy-done.1, f32[64,8,128]{2,1,0:T(8,128)S(1)} %all-to-all-done.2.pieces_ref, bf16[2048,256]{1,0:T(8,128)(2,1)S(1)} %copy-done), custom_call_target="tpu_custom_call" | custom-call | tf_op jit(solution)/shard_map/update/pallas_call | solution.py:278
  (1 shorter events, 0.0 us)
Async XLA Ops:
  6.4 10.5 %collective-permute-start = (f32[8,64,256]{2,1,0:T(8,128)}, f32[8,64,256]{2,1,0:T(8,128)S(1)}, u32[]{:S(2)}, u32[]{:S(2)}) collective-permute-start(f32[8,64,256]{2,1,0:T(8,128)} %get-tuple-element.8), channel_id=1, source_target_pairs={{0,4},{4,0},{1,5},{5,1},{2,6},{6,2},{3,7},{7,3},{8,12},{12,8},{9,1... | collective-permute-start | bytes 1572872 | tf_op jit(solution)/shard_map/ppermute | solution.py:269
  18.8 13.0 %all-to-all-start = ((f32[8,64,256]{2,1,0:T(8,128)}), f32[8,64,256]{2,1,0:T(8,128)S(1)}, u32[]{:S(2)}, u32[]{:S(2)}) async-start(f32[8,64,256]{2,1,0:T(8,128)} %add.6), calls=%async_computation | async-start | bytes 1048576 | tf_op jit(solution)/shard_map/all_to_all | solution.py:250
  22.3 9.5 %copy-start.2 = (f32[1,8]{1,0:T(1,128)S(1)}, f32[1,8]{1,0:T(1,128)}, u32[]{:S(2)}) copy-start(f32[1,8]{1,0:T(1,128)} %counts_ref.1) | copy-start | bytes 100
  22.3 9.5 %copy-start.3 = (f32[1,8]{1,0:T(1,128)S(1)}, f32[1,8]{1,0:T(1,128)}, u32[]{:S(2)}) copy-start(f32[1,8]{1,0:T(1,128)} %var_ref.1) | copy-start | bytes 100
  31.8 6.7 %collective-permute-start.1 = (f32[136,128]{1,0:T(8,128)S(1)}, f32[136,128]{1,0:T(8,128)S(1)}, u32[]{:S(2)}, u32[]{:S(2)}) collective-permute-start(f32[136,128]{1,0:T(8,128)S(1)} %rows_kernel.1), channel_id=1, source_target_pairs={{0,16},{16,0},{1,17},{17,1},{2,18},{18,2},{3,19},{19,3},{4,20},{20... | collective-permute-start | bytes 208904 | tf_op jit(solution)/shard_map/ppermute | solution.py:272
  66.9 29.1 %copy-start = (bf16[2048,256]{1,0:T(8,128)(2,1)S(1)}, bf16[2048,256]{1,0:T(8,128)(2,1)}, u32[]{:S(2)}) copy-start(bf16[2048,256]{1,0:T(8,128)(2,1)} %states_hbm.3) | copy-start | bytes 3145732
  80.3 15.7 %all-to-all-start.2 = ((f32[64,8,128]{2,1,0:T(8,128)}), f32[64,8,128]{2,1,0:T(8,128)S(1)}, u32[]{:S(2)}, u32[]{:S(2)}) async-start(f32[64,8,128]{2,1,0:T(8,128)} %share_kernel.1), calls=%async_computation.2 | async-start | bytes 524288 | tf_op jit(solution)/shard_map/all_to_all | solution.py:250
  86.0 10.1 %copy-start.1 = (s32[16]{0:T(128)S(1)}, s32[16]{0:T(128)}, u32[]{:S(2)}) copy-start(s32[16]{0:T(128)} %live_ref.1) | copy-start | bytes 196

commit v5 on v4

--- a/solution.py
+++ b/solution.py
@@ -34,8 +34,20 @@
     return dot(ah, bh) + (dot(ah, bl) + dot(al, bh))
 
 
+def link_of(place_ref):
+    return place_ref[0] & 3
+
+
+def core_of(place_ref):
+    return jnp.right_shift(place_ref[0], 2) & 1
+
+
+def pair_of(place_ref):
+    return jnp.right_shift(place_ref[0], 4) & 1
+
+
 def term_kernel(
-    core_ref, ids_hbm, targets_hbm, live_hbm, states_hbm, tiles_hbm, keep_ref, send_ref,
+    place_ref, ids_hbm, targets_hbm, live_hbm, states_hbm, tiles_hbm, keep_ref, send_ref,
     ids_ref, targets_ref, live_ref, states_ref, tiles_ref, list_ref, sems,
 ):
     slots, _, blocks = ids_ref.shape
@@ -119,16 +131,16 @@
 
         lax.fori_loop(0, steps, step, 0, unroll=steps)
 
-    @pl.when(core_ref[0] == 0)
+    @pl.when(core_of(place_ref) == 0)
     def _():
         run((keep_ref, send_ref))
 
-    @pl.when(core_ref[0] == 1)
+    @pl.when(core_of(place_ref) == 1)
     def _():
         run((send_ref, keep_ref))
 
 
-def term(core, ids, targets, live, states, tiles):
+def term(place, ids, targets, live, states, tiles):
     slots, _, blocks = ids.shape
     states_dev, members = states.shape
     steps = (slots * blocks + NLB * (DEPTH - 1)) // DEPTH
@@ -149,7 +161,7 @@
         ],
         compiler_params=WHOLE,
         name="term",
-    )(core, ids, targets, live, states, tiles)
+    )(place, ids, targets, live, states, tiles)
 
 
 def as_column(ref):
@@ -158,34 +170,42 @@
     return jnp.sum(jnp.where(at(0) == at(1), ref[...], 0.0), axis=1, keepdims=True)
 
 
-def rows_kernel(pair_ref, parts_ref, counts_ref, var_ref, out_ref):
+def add_kernel(a_ref, b_ref, out_ref):
+    out_ref[...] = a_ref[...] + b_ref[...]
+
+
+def rows_kernel(place_ref, parts_ref, counts_ref, var_ref, keep_ref, send_ref):
     total = jnp.sum(parts_ref[...], axis=0)
-    rows = total.shape[0]
-    out_ref[0:rows, :] = total[:, :128]
-    out_ref[rows : 2 * rows, :] = total[:, 128:]
-    lane = lax.broadcasted_iota(jnp.int32, (8, 128), 1) - 2 * pair_ref[0]
+    rows, members = total.shape
+    by_pair = total.reshape(rows // 16, 2, 8, members)
+    first, second = (by_pair[:, p].reshape(rows // 2, members) for p in range(2))
+    mine = pair_of(place_ref) == 0
+    lane = lax.broadcasted_iota(jnp.int32, (8, 128), 1)
     counts, variance = as_column(counts_ref), as_column(var_ref)
-    out_ref[2 * rows : 2 * rows + 8, :] = jnp.where(lane == 0, counts, jnp.where(lane == 1, variance, 0.0))
-
-
-def gram_kernel(core_ref, parts_ref, out_ref):
+    tail = jnp.where(lane == 0, counts, jnp.where(lane == 1, variance, 0.0))
+    for ref, at, below in ((keep_ref, mine, tail), (send_ref, jnp.logical_not(mine), jnp.zeros_like(tail))):
+        chosen = jnp.where(at, first, second)
+        ref[0 : rows // 2, :] = chosen[:, :128]
+        ref[rows // 2 : rows, :] = chosen[:, 128:]
+        ref[rows:, :] = below
+
+
+def gram_kernel(place_ref, parts_ref, out_ref):
     rows = (parts_ref.shape[1] - 8) // 2
-    quads = parts_ref.shape[0] // 2
-
-    def both(first, count):
-        return jnp.concatenate(
-            [sum(parts_ref[2 * k + c, first : first + count, :] for k in range(quads)) for c in range(2)], axis=0
-        )
-
-    left, right = both(0, rows), both(rows, rows)
-    tails = [parts_ref[2 * k + c, 2 * rows : 2 * rows + 8, :] for c in range(2) for k in range(quads)]
-    column = lambda at: jnp.concatenate([t[:, 2 * p + at : 2 * p + at + 1] for t in tails for p in range(2)], axis=0)
-    counts, variance = column(0), column(1)
+    quads = parts_ref.shape[0] // 4
+    groups = [[(2 * k + p) * 2 + c for k in range(quads)] for c in range(2) for p in range(2)]
+
+    def whole(first):
+        return jnp.concatenate([sum(parts_ref[m, first : first + rows, :] for m in g) for g in groups], axis=0)
+
+    left, right = whole(0), whole(rows)
+    tails = jnp.concatenate([parts_ref[m, 2 * rows :, :] for g in groups for m in g], axis=0)
+    counts, variance = tails[:, 0:1], tails[:, 1:2]
     mean = jnp.sum(left + right, axis=1, keepdims=True) * (1.0 / 256.0)
     left, right = left - mean, right - mean
     weights = 1.0 / variance
     weighted = weights * (counts - mean)
-    mine = core_ref[0] == 0
+    mine = core_of(place_ref) == 0
     own = jnp.where(mine, left, right)
     half = jnp.where(mine, left[:, :64], left[:, 64:])
     out_ref[0:16] = dot3(halves(own.T), halves(own * weights)).reshape(16, 8, 128)
@@ -200,9 +220,9 @@
     out_ref[...] = jnp.broadcast_to(total[None], out_ref.shape)
 
 
-def update_kernel(link_ref, live_ref, pieces_ref, states_hbm, out_ref, states_ref, sem):
+def update_kernel(place_ref, live_ref, pieces_ref, states_hbm, out_ref, states_ref, sem):
     own_rows, members = states_ref.shape
-    own = pl.ds(pl.multiple_of(link_ref[0] * own_rows, own_rows), own_rows)
+    own = pl.ds(pl.multiple_of(link_of(place_ref) * own_rows, own_rows), own_rows)
     copy = pltpu.make_async_copy(states_hbm.at[own], states_ref, sem)
     copy.start()
     by_core = pieces_ref[...].reshape(pieces_ref.shape[0] // 2, 2, 8, 128)
@@ -242,7 +262,7 @@
         rows = slice(k * 128, k * 128 + 128)
         states = states_ref[rows, :]
         updated = dot(states, high) + dot(states, low)
-        live = live_ref[link_ref[0] * own_blocks + k]
+        live = live_ref[link_of(place_ref) * own_blocks + k]
         out_ref[rows, :] = jnp.where(position < live, updated, states.astype(F32)).astype(BF16)
 
 
@@ -263,15 +283,22 @@
 
 def per_device(background, live_counts, patterns, pattern_ids, link_targets, counts_obs, obs_var):
     states_dev, members = background.shape
-    core, link, pair = (lax.axis_index(axis).astype(jnp.int32).reshape(1) for axis in ("c", "x", "zp"))
+    place = lax.axis_index(("zp", "zl", "c", "x")).astype(jnp.int32).reshape(1)
     ids, targets = (jnp.transpose(a, (2, 0, 1)) for a in (pattern_ids, link_targets))
-    keep, send = term(core, ids, targets, live_counts, background, patterns[0])
-    of_chip = keep + lax.ppermute(send, "c", [(0, 1), (1, 0)])
+    keep, send = term(place, ids, targets, live_counts, background, patterns[0])
+    of_chip = local(add_kernel, keep.shape, 2)(keep, lax.ppermute(send, "c", [(0, 1), (1, 0)]))
     parts = all_to_all(of_chip, ("y", "zl"))
-    own = local(rows_kernel, (136, 128), 3, 1)(pair, parts, counts_obs, obs_var)
-    own += lax.ppermute(own, "zp", [(0, 1), (1, 0)])
-    column = lax.all_gather(own, ("zq", "c"))
-    gram = local(gram_kernel, (32, 8, 128), 1, 1)(core, column)
+    own, other = pl.pallas_call(
+        rows_kernel,
+        out_shape=(jax.ShapeDtypeStruct((72, 128), F32),) * 2,
+        in_specs=[SMEM, VMEM, VMEM, VMEM],
+        out_specs=(VMEM, VMEM),
+        compiler_params=PARAMS,
+        name="rows",
+    )(place, parts, counts_obs, obs_var)
+    own += lax.ppermute(other, "zp", [(0, 1), (1, 0)])
+    column = lax.all_gather(own, ("zq", "zp", "c"))
+    gram = local(gram_kernel, (32, 8, 128), 1, 1)(place, column)
     shared = local(share_kernel, (64, 8, 128), 1)(all_to_all(gram, ("x", "y", "zl")))
     pieces = all_to_all(shared, SLAB)
     own_rows = states_dev // lax.axis_size("x")
@@ -283,7 +310,7 @@
         scratch_shapes=[pltpu.VMEM((own_rows, members), BF16), pltpu.SemaphoreType.DMA],
         compiler_params=PARAMS,
         name="update",
-    )(link, live_counts, pieces, background)
+    )(place, live_counts, pieces, background)
 
 
 def solution(mesh):

time: 101 us -> 97.3 us (0.963)
  blocking collectives: 40.6 us -> 67.9 us
  waiting for transfers between devices: 26 us -> 5.79 us
  starting transfers between devices: 19.8 us -> 10.7 us
  other arithmetic: 1.9 us -> 0.01 us
  local copies, waits for them, and re-layouts: 0.02 us -> 1.06 us
    all_to_all x1 -> x3, blocking collectives: 12.2 us -> 42 us  [all_to_all(): return lax.all_to_all(x, axes, split_axis=0, concat_axis=0, tiled=True)]
    all_to_all x2 -> x0, waiting for transfers between devices: 19.5 us -> none  [all_to_all(): return lax.all_to_all(x, axes, split_axis=0, concat_axis=0, tiled=True)]
    all_to_all x2 -> x0, starting transfers between devices: 9.11 us -> none  [all_to_all(): return lax.all_to_all(x, axes, split_axis=0, concat_axis=0, tiled=True)]
    all_gather x1, blocking collectives: 28.4 us -> 26 us  [per_device(): column = lax.all_gather(own, ('zq', 'zp', 'c'))]
    add x2 -> x1, other arithmetic: 1.9 us -> 0.01 us  [per_device(): own += lax.ppermute(other, 'zp', [(0, 1), (1, 0)])]
    unnamed x8 -> x10, local copies, waits for them, and re-layouts: 0.02 us -> 1.06 us
  transfers between devices with their start and end apart: 4 -> 2, of which waited for: 4 -> 2; matrix products, arithmetic and copies ran while one was open for 0% -> 0% of each run, Pallas kernels for 0% -> 0%
where the time goes in v5:
time: 97.3 us; the launch traced here: 96.9 us
  blocking collectives  67.9 us (70%)
  Pallas kernels  11.4 us (12%)
  starting transfers between devices  10.7 us (11%)
  waiting for transfers between devices  5.79 us (6%)
  local copies, waits for them, and re-layouts  1.06 us (1%)
    all_to_all x3, blocking collectives, all_to_all(): return lax.all_to_all(x, axes, split_axis=0, concat_axis=0, tiled=True)  42 us
    all_gather x1, blocking collectives, per_device(): column = lax.all_gather(own, ('zq', 'zp', 'c'))  26 us
    ppermute x1, starting transfers between devices, per_device(): lax.ppermute(send, 'c', [(0, 1), (1, 0)])  8.78 us
    pallas_call x1, Pallas kernels, term(): pl.pallas_call(term_kernel, out_shape=(half, half), in_specs=[SMEM] + [HB...  6.34 us
    pallas_call x1, Pallas kernels, per_device(): pl.pallas_call(update_kernel, out_shape=jax.ShapeDtypeStruct((own_rows, m...  4.45 us
    ppermute x1, waiting for transfers between devices, per_device(): own += lax.ppermute(other, 'zp', [(0, 1), (1, 0)])  4.07 us
  transfers between devices with their start and end apart: 2, of which 2 were waited for; matrix products, arithmetic and copies ran while one was open for 0% of the time, Pallas kernels for 0%

profile of v5, /device:TPU:1, one launch (start us, length us, event | category | flops | bytes accessed | tf_op | source)
XLA Modules:
  0.0 96.9 jit_solution(18101993404102611829)
XLA Ops:
  0.0 6.3 %term.1 = (f32[8,64,256]{2,1,0:T(8,128)}, f32[8,64,256]{2,1,0:T(8,128)}) custom-call(s32[1]{0:T(128)} %bitcast.place_ref, s32[12,1,16]{2,1,0:T(1,128)} %bitcast.7, s32[12,1,16]{2,1,0:T(1,128)} %bitcast.8, s32[16]{0:T(128)} %live_ref.1, bf16[2048,256]{1,0:T(8,128)(2,1)} %states_hbm.3, bf16[32,128,128]{2,1,0:T(8,128)(2,1)} %bitcast.6), custom_call_target="tpu_custom_call" | custom-call | tf_op jit(solution)/shard_map/term/pallas_call | solution.py:148
  6.4 8.8 %collective-permute-start = (f32[8,64,256]{2,1,0:T(8,128)}, f32[8,64,256]{2,1,0:T(8,128)S(1)}, u32[]{:S(2)}, u32[]{:S(2)}) collective-permute-start(f32[8,64,256]{2,1,0:T(8,128)} %get-tuple-element.10), channel_id=1, source_target_pairs={{0,4},{4,0},{1,5},{5,1},{2,6},{6,2},{3,7},{7,3},{8,12},{12,8},{9,1... | collective-permute-start | bytes 1572872 | tf_op jit(solution)/shard_map/ppermute | solution.py:289
  15.1 1.7 %collective-permute-done.b_ref = f32[8,64,256]{2,1,0:T(8,128)S(1)} collective-permute-done((f32[8,64,256]{2,1,0:T(8,128)}, f32[8,64,256]{2,1,0:T(8,128)S(1)}, u32[]{:S(2)}, u32[]{:S(2)}) %collective-permute-start) | collective-permute-done | bytes 524320 | tf_op jit(solution)/shard_map/ppermute | solution.py:289
  16.9 0.0 copy-start.1
  16.9 1.0 %copy-done.1 = f32[8,64,256]{2,1,0:T(8,128)S(1)} copy-done((f32[8,64,256]{2,1,0:T(8,128)S(1)}, f32[8,64,256]{2,1,0:T(8,128)}, u32[]{:S(2)}) %copy-start.1) | copy-done | bytes 524312
  17.9 0.1 add_kernel.1
  18.0 0.0 copy-start.3
  18.0 0.0 copy-start.4
  18.0 12.2 %all_to_all.15.parts_ref = f32[8,64,256]{2,1,0:T(8,128)S(1)} all-to-all(f32[8,64,256]{2,1,0:T(8,128)S(1)} %add_kernel.1), channel_id=1, replica_groups=mesh['y'=4,'zq'=4,'zp'=2,'zl'=2,'c'=2,'x'=4] {'y','zl'}, dimensions={0} | all-to-all | bytes 1048576 | tf_op jit(solution)/shard_map/all_to_all | solution.py:270
  30.2 0.0 copy-done.3
  30.2 0.0 copy-done.4
  30.2 0.1 rows.1
  30.3 1.9 %collective-permute-start.1 = (f32[72,128]{1,0:T(8,128)S(1)}, f32[72,128]{1,0:T(8,128)S(1)}, u32[]{:S(2)}, u32[]{:S(2)}) collective-permute-start(f32[72,128]{1,0:T(8,128)S(1)} %get-tuple-element.12), channel_id=1, source_target_pairs={{0,16},{16,0},{1,17},{17,1},{2,18},{18,2},{3,19},{19,3},{4,20},{20... | collective-permute-start | bytes 110600 | tf_op jit(solution)/shard_map/ppermute | solution.py:299
  32.2 4.1 %collective-permute-done.1 = f32[72,128]{1,0:T(8,128)S(1)} collective-permute-done((f32[72,128]{1,0:T(8,128)S(1)}, f32[72,128]{1,0:T(8,128)S(1)}, u32[]{:S(2)}, u32[]{:S(2)}) %collective-permute-start.1) | collective-permute-done | bytes 36896 | tf_op jit(solution)/shard_map/ppermute | solution.py:299
  36.3 26.0 %all-gather = f32[1152,128]{1,0:T(8,128)S(1)} all-gather(f32[72,128]{1,0:T(8,128)S(1)} %add.15), channel_id=2, replica_groups=mesh['y'=4,'zq'=4,'zp'=2,'zl'=2,'c'=2,'x'=4] {'zq','zp','c'}, dimensions={0}, use_global_device_ids=true | all-gather | bytes 626688 | tf_op jit(solution)/shard_map/all_gather | solution.py:300
  62.3 0.0 copy-start
  62.3 0.4 gram_kernel.1
  62.7 14.5 %all_to_all.16.parts_ref = f32[32,8,128]{2,1,0:T(8,128)S(1)} all-to-all(f32[32,8,128]{2,1,0:T(8,128)S(1)} %gram_kernel.1), channel_id=1, replica_groups=mesh['y'=4,'zq'=4,'zp'=2,'zl'=2,'c'=2,'x'=4] {'x','y','zl'}, dimensions={0} | all-to-all | bytes 262144 | tf_op jit(solution)/shard_map/all_to_all | solution.py:270
  77.2 0.1 share_kernel.1
  77.3 0.0 copy-start.2
  77.3 15.2 %all_to_all.17.pieces_ref = f32[64,8,128]{2,1,0:T(8,128)S(1)} all-to-all(f32[64,8,128]{2,1,0:T(8,128)S(1)} %share_kernel.1), channel_id=1, replica_groups=mesh['y'=4,'zq'=4,'zp'=2,'zl'=2,'c'=2,'x'=4] {'x','y','zl','c'}, dimensions={0} | all-to-all | bytes 524288 | tf_op jit(solution)/shard_map/all_to_all | solution.py:270
  92.5 0.0 copy-done
  92.5 0.0 copy-done.2
  92.5 4.4 %update.1 = bf16[512,256]{1,0:T(8,128)(2,1)} custom-call(s32[1]{0:T(128)} %bitcast.place_ref, s32[16]{0:T(128)S(1)} %copy-done.2, f32[64,8,128]{2,1,0:T(8,128)S(1)} %all_to_all.17.pieces_ref, bf16[2048,256]{1,0:T(8,128)(2,1)S(1)} %copy-done), custom_call_target="tpu_custom_call" | custom-call | tf_op jit(solution)/shard_map/update/pallas_call | solution.py:305
  (1 shorter events, 0.0 us)
Async XLA Ops:
  6.4 10.5 %collective-permute-start = (f32[8,64,256]{2,1,0:T(8,128)}, f32[8,64,256]{2,1,0:T(8,128)S(1)}, u32[]{:S(2)}, u32[]{:S(2)}) collective-permute-start(f32[8,64,256]{2,1,0:T(8,128)} %get-tuple-element.10), channel_id=1, source_target_pairs={{0,4},{4,0},{1,5},{5,1},{2,6},{6,2},{3,7},{7,3},{8,12},{12,8},{9,1... | collective-permute-start | bytes 1572872 | tf_op jit(solution)/shard_map/ppermute | solution.py:289
  16.9 1.0 %copy-start.1 = (f32[8,64,256]{2,1,0:T(8,128)S(1)}, f32[8,64,256]{2,1,0:T(8,128)}, u32[]{:S(2)}) copy-start(f32[8,64,256]{2,1,0:T(8,128)} %get-tuple-element.9.a_ref) | copy-start | bytes 1572868
  18.0 12.3 %copy-start.3 = (f32[1,8]{1,0:T(1,128)S(1)}, f32[1,8]{1,0:T(1,128)}, u32[]{:S(2)}) copy-start(f32[1,8]{1,0:T(1,128)} %counts_ref.1) | copy-start | bytes 100
  18.0 12.3 %copy-start.4 = (f32[1,8]{1,0:T(1,128)S(1)}, f32[1,8]{1,0:T(1,128)}, u32[]{:S(2)}) copy-start(f32[1,8]{1,0:T(1,128)} %var_ref.1) | copy-start | bytes 100
  30.3 6.0 %collective-permute-start.1 = (f32[72,128]{1,0:T(8,128)S(1)}, f32[72,128]{1,0:T(8,128)S(1)}, u32[]{:S(2)}, u32[]{:S(2)}) collective-permute-start(f32[72,128]{1,0:T(8,128)S(1)} %get-tuple-element.12), channel_id=1, source_target_pairs={{0,16},{16,0},{1,17},{17,1},{2,18},{18,2},{3,19},{19,3},{4,20},{20... | collective-permute-start | bytes 110600 | tf_op jit(solution)/shard_map/ppermute | solution.py:299
  62.3 30.2 %copy-start = (bf16[2048,256]{1,0:T(8,128)(2,1)S(1)}, bf16[2048,256]{1,0:T(8,128)(2,1)}, u32[]{:S(2)}) copy-start(bf16[2048,256]{1,0:T(8,128)(2,1)} %states_hbm.3) | copy-start | bytes 3145732
  77.3 15.2 %copy-start.2 = (s32[16]{0:T(128)S(1)}, s32[16]{0:T(128)}, u32[]{:S(2)}) copy-start(s32[16]{0:T(128)} %live_ref.1) | copy-start | bytes 196

commit v6 on v5

--- a/solution.py
+++ b/solution.py
@@ -48,7 +48,7 @@
 
 def term_kernel(
     place_ref, ids_hbm, targets_hbm, live_hbm, states_hbm, tiles_hbm, keep_ref, send_ref,
-    ids_ref, targets_ref, live_ref, states_ref, tiles_ref, list_ref, sems,
+    ids_ref, targets_ref, live_ref, states_ref, tiles_ref, spread_ref, next_ref, list_ref, sems,
 ):
     slots, _, blocks = ids_ref.shape
     stored, link_rows, block_rows = tiles_ref.shape
@@ -64,6 +64,7 @@
                 (live_hbm, live_ref),
                 (states_hbm, states_ref.at[pl.ds(0, states_dev)]),
                 (tiles_hbm, tiles_ref),
+                (targets_hbm, spread_ref),
             )
         )
     ]
@@ -74,34 +75,25 @@
     keep_ref[...] = jnp.zeros_like(keep_ref)
     send_ref[...] = jnp.zeros_like(send_ref)
     states_ref[states_dev:, :] = jnp.zeros((block_rows, members), BF16)
+    copies[5].wait()
+    spread = spread_ref[...]
+    first_step = jnp.int32(0)
+    for j in range(NLB):
+        entries = jnp.sum(jnp.where(spread == j, 1.0, 0.0)).astype(jnp.int32)
+        next_ref[j] = first_step * DEPTH
+        first_step += jnp.right_shift(entries + DEPTH - 1, DEPTH.bit_length() - 1)
     copies[0].wait()
     copies[1].wait()
 
-    def bump(words, target):
-        one = jnp.left_shift(jnp.int32(1), (target & 3) * 8)
-        return words[0] + jnp.where(target < 4, one, 0), words[1] + jnp.where(target < 4, 0, one)
-
-    def count(b, words):
-        for t in range(slots):
-            words = bump(words, targets_ref[t, 0, b])
-        return words
-
-    def put(b, words):
+    def put(b, carry):
         for t in range(slots):
             target = targets_ref[t, 0, b]
-            at = jnp.right_shift(jnp.where(target < 4, words[0], words[1]), (target & 3) * 8) & 255
+            at = next_ref[target]
             list_ref[at] = target * 1024 + (b * stored + ids_ref[t, 0, b])
-            words = bump(words, target)
-        return words
-
-    none = jnp.int32(0)
-    counted = lax.fori_loop(0, blocks, count, (none, none))
-    first_step, starts = none, [none, none]
-    for j in range(NLB):
-        entries = jnp.right_shift(counted[j // 4], 8 * (j % 4)) & 255
-        starts[j // 4] += jnp.left_shift(first_step * DEPTH, 8 * (j % 4))
-        first_step += jnp.right_shift(entries + DEPTH - 1, DEPTH.bit_length() - 1)
-    lax.fori_loop(0, blocks, put, tuple(starts))
+            next_ref[target] = at + 1
+        return carry
+
+    lax.fori_loop(0, blocks, put, 0, unroll=4)
 
     copies[2].wait()
     copies[3].wait()
@@ -156,8 +148,10 @@
             pltpu.SMEM(live.shape, jnp.int32),
             pltpu.VMEM((states_dev + tiles.shape[2], members), BF16),
             pltpu.VMEM(tiles.shape, BF16),
+            pltpu.VMEM(ids.shape, jnp.int32),
+            pltpu.SMEM((NLB,), jnp.int32),
             pltpu.SMEM((steps * DEPTH,), jnp.int32),
-            pltpu.SemaphoreType.DMA((5,)),
+            pltpu.SemaphoreType.DMA((6,)),
         ],
         compiler_params=WHOLE,
         name="term",
@@ -168,6 +162,10 @@
     count = ref.shape[1]
     at = lambda dim: lax.broadcasted_iota(jnp.int32, (count, count), dim)
     return jnp.sum(jnp.where(at(0) == at(1), ref[...], 0.0), axis=1, keepdims=True)
+
+
+def copy_kernel(a_ref, out_ref):
+    out_ref[...] = a_ref[...]
 
 
 def add_kernel(a_ref, b_ref, out_ref):
@@ -234,7 +232,9 @@
     )
     forcing = jnp.concatenate([by_core[24, 0, 0:1], by_core[24, 0, 1:2]], axis=1)
     at = lambda dim: lax.broadcasted_iota(jnp.int32, (members, members), dim)
-    identity = jnp.where(at(0) == at(1), 1.0, 0.0).astype(F32)
+    diagonal = at(0) == at(1)
+    identity = jnp.where(diagonal, 1.0, 0.0).astype(F32)
+    forcing = jnp.sum(jnp.where(diagonal, forcing, 0.0), axis=1, keepdims=True)
     system = identity + gram * (1.0 / (members - 1.0))
     bound = jnp.max(jnp.sum(jnp.abs(system), axis=0, keepdims=True), axis=1, keepdims=True)
     root = system * (1.0 / bound)
@@ -250,7 +250,7 @@
             inverse = dot3(middle_halves, halves(inverse))
         if sweep < NS_ITERS - 1:
             root = dot3(halves(root), middle_halves)
-    inner = dot3(halves(jnp.broadcast_to(forcing, (8, members))), halves(inverse))[0:1]
+    inner = jnp.sum(inverse * forcing, axis=0, keepdims=True)
     mean_weights = jnp.sum(inverse * inner, axis=1, keepdims=True) * (1.0 / (bound * (members - 1.0)))
     transform = inverse * lax.rsqrt(bound) + mean_weights
     transform += (1.0 - jnp.sum(transform, axis=0, keepdims=True)) * (1.0 / members)
@@ -286,7 +286,8 @@
     place = lax.axis_index(("zp", "zl", "c", "x")).astype(jnp.int32).reshape(1)
     ids, targets = (jnp.transpose(a, (2, 0, 1)) for a in (pattern_ids, link_targets))
     keep, send = term(place, ids, targets, live_counts, background, patterns[0])
-    of_chip = local(add_kernel, keep.shape, 2)(keep, lax.ppermute(send, "c", [(0, 1), (1, 0)]))
+    received = lax.ppermute(send, "c", [(0, 1), (1, 0)])
+    of_chip = local(add_kernel, keep.shape, 2)(local(copy_kernel, keep.shape, 1)(keep), received)
     parts = all_to_all(of_chip, ("y", "zl"))
     own, other = pl.pallas_call(
         rows_kernel,

time: 97.3 us -> 95.8 us (0.985)
  waiting for transfers between devices: 5.79 us -> 4.71 us
    ppermute x1, waiting for transfers between devices: 1.73 us -> 0.64 us  [per_device(): received = lax.ppermute(send, 'c', [(0, 1), (1, 0)])]
where the time goes in v6:
time: 95.8 us; the launch traced here: 95.5 us
  blocking collectives  67.9 us (71%)
  Pallas kernels  11 us (11%)
  starting transfers between devices  10.7 us (11%)
  waiting for transfers between devices  4.71 us (5%)
  local copies, waits for them, and re-layouts  1.06 us (1%)
    all_to_all x3, blocking collectives, all_to_all(): return lax.all_to_all(x, axes, split_axis=0, concat_axis=0, tiled=True)  42 us
    all_gather x1, blocking collectives, per_device(): column = lax.all_gather(own, ('zq', 'zp', 'c'))  26 us
    ppermute x1, starting transfers between devices, per_device(): received = lax.ppermute(send, 'c', [(0, 1), (1, 0)])  8.79 us
    pallas_call x1, Pallas kernels, term(): pl.pallas_call(term_kernel, out_shape=(half, half), in_specs=[SMEM] + [HB...  6.12 us
    pallas_call x1, Pallas kernels, per_device(): pl.pallas_call(update_kernel, out_shape=jax.ShapeDtypeStruct((own_rows, m...  4.25 us
    ppermute x1, waiting for transfers between devices, per_device(): own += lax.ppermute(other, 'zp', [(0, 1), (1, 0)])  4.07 us
  transfers between devices with their start and end apart: 2, of which 2 were waited for; matrix products, arithmetic and copies ran while one was open for 0% of the time, Pallas kernels for 0%

profile of v6, /device:TPU:1, one launch (start us, length us, event | category | flops | bytes accessed | tf_op | source)
XLA Modules:
  0.0 95.5 jit_solution(15308526831923348060)
XLA Ops:
  0.0 6.1 %term.1 = (f32[8,64,256]{2,1,0:T(8,128)}, f32[8,64,256]{2,1,0:T(8,128)}) custom-call(s32[1]{0:T(128)} %bitcast.place_ref, s32[12,1,16]{2,1,0:T(1,128)} %bitcast.7, s32[12,1,16]{2,1,0:T(1,128)} %bitcast.8, s32[16]{0:T(128)} %live_ref.1, bf16[2048,256]{1,0:T(8,128)(2,1)} %states_hbm.3, bf16[32,128,128]{2,1,0:T(8,128)(2,1)} %bitcast.6), custom_call_target="tpu_custom_call" | custom-call | tf_op jit(solution)/shard_map/term/pallas_call | solution.py:140
  6.1 8.8 %collective-permute-start = (f32[8,64,256]{2,1,0:T(8,128)}, f32[8,64,256]{2,1,0:T(8,128)S(1)}, u32[]{:S(2)}, u32[]{:S(2)}) collective-permute-start(f32[8,64,256]{2,1,0:T(8,128)} %get-tuple-element.10), channel_id=1, source_target_pairs={{0,4},{4,0},{1,5},{5,1},{2,6},{6,2},{3,7},{7,3},{8,12},{12,8},{9,1... | collective-permute-start | bytes 1572872 | tf_op jit(solution)/shard_map/ppermute | solution.py:289
  14.9 0.0 copy-start.1
  14.9 1.0 %copy-done.1 = f32[8,64,256]{2,1,0:T(8,128)S(1)} copy-done((f32[8,64,256]{2,1,0:T(8,128)S(1)}, f32[8,64,256]{2,1,0:T(8,128)}, u32[]{:S(2)}) %copy-start.1) | copy-done | bytes 524312
  16.0 0.6 collective-permute-done.b_ref
  16.6 0.1 add_kernel.1
  16.7 0.0 copy-start.3
  16.7 0.0 copy-start.4
  16.7 12.2 %all_to_all.15.parts_ref = f32[8,64,256]{2,1,0:T(8,128)S(1)} all-to-all(f32[8,64,256]{2,1,0:T(8,128)S(1)} %add_kernel.1), channel_id=1, replica_groups=mesh['y'=4,'zq'=4,'zp'=2,'zl'=2,'c'=2,'x'=4] {'y','zl'}, dimensions={0} | all-to-all | bytes 1048576 | tf_op jit(solution)/shard_map/all_to_all | solution.py:270
  29.0 0.0 copy-done.3
  29.0 0.0 copy-done.4
  29.0 0.1 rows.1
  29.1 1.9 %collective-permute-start.1 = (f32[72,128]{1,0:T(8,128)S(1)}, f32[72,128]{1,0:T(8,128)S(1)}, u32[]{:S(2)}, u32[]{:S(2)}) collective-permute-start(f32[72,128]{1,0:T(8,128)S(1)} %get-tuple-element.12), channel_id=1, source_target_pairs={{0,16},{16,0},{1,17},{17,1},{2,18},{18,2},{3,19},{19,3},{4,20},{20... | collective-permute-start | bytes 110600 | tf_op jit(solution)/shard_map/ppermute | solution.py:300
  31.0 4.1 %collective-permute-done.1 = f32[72,128]{1,0:T(8,128)S(1)} collective-permute-done((f32[72,128]{1,0:T(8,128)S(1)}, f32[72,128]{1,0:T(8,128)S(1)}, u32[]{:S(2)}, u32[]{:S(2)}) %collective-permute-start.1) | collective-permute-done | bytes 36896 | tf_op jit(solution)/shard_map/ppermute | solution.py:300
  35.1 26.0 %all-gather = f32[1152,128]{1,0:T(8,128)S(1)} all-gather(f32[72,128]{1,0:T(8,128)S(1)} %add.15), channel_id=2, replica_groups=mesh['y'=4,'zq'=4,'zp'=2,'zl'=2,'c'=2,'x'=4] {'zq','zp','c'}, dimensions={0}, use_global_device_ids=true | all-gather | bytes 626688 | tf_op jit(solution)/shard_map/all_gather | solution.py:301
  61.0 0.0 copy-start
  61.0 0.4 gram_kernel.1
  61.4 14.5 %all_to_all.16.parts_ref = f32[32,8,128]{2,1,0:T(8,128)S(1)} all-to-all(f32[32,8,128]{2,1,0:T(8,128)S(1)} %gram_kernel.1), channel_id=1, replica_groups=mesh['y'=4,'zq'=4,'zp'=2,'zl'=2,'c'=2,'x'=4] {'x','y','zl'}, dimensions={0} | all-to-all | bytes 262144 | tf_op jit(solution)/shard_map/all_to_all | solution.py:270
  76.0 0.1 share_kernel.1
  76.0 0.0 copy-start.2
  76.0 15.2 %all_to_all.17.pieces_ref = f32[64,8,128]{2,1,0:T(8,128)S(1)} all-to-all(f32[64,8,128]{2,1,0:T(8,128)S(1)} %share_kernel.1), channel_id=1, replica_groups=mesh['y'=4,'zq'=4,'zp'=2,'zl'=2,'c'=2,'x'=4] {'x','y','zl','c'}, dimensions={0} | all-to-all | bytes 524288 | tf_op jit(solution)/shard_map/all_to_all | solution.py:270
  91.2 0.0 copy-done
  91.2 0.0 copy-done.2
  91.2 4.2 %update.1 = bf16[512,256]{1,0:T(8,128)(2,1)} custom-call(s32[1]{0:T(128)} %bitcast.place_ref, s32[16]{0:T(128)S(1)} %copy-done.2, f32[64,8,128]{2,1,0:T(8,128)S(1)} %all_to_all.17.pieces_ref, bf16[2048,256]{1,0:T(8,128)(2,1)S(1)} %copy-done), custom_call_target="tpu_custom_call" | custom-call | tf_op jit(solution)/shard_map/update/pallas_call | solution.py:306
  (2 shorter events, 0.0 us)
Async XLA Ops:
  6.1 10.5 %collective-permute-start = (f32[8,64,256]{2,1,0:T(8,128)}, f32[8,64,256]{2,1,0:T(8,128)S(1)}, u32[]{:S(2)}, u32[]{:S(2)}) collective-permute-start(f32[8,64,256]{2,1,0:T(8,128)} %get-tuple-element.10), channel_id=1, source_target_pairs={{0,4},{4,0},{1,5},{5,1},{2,6},{6,2},{3,7},{7,3},{8,12},{12,8},{9,1... | collective-permute-start | bytes 1572872 | tf_op jit(solution)/shard_map/ppermute | solution.py:289
  14.9 1.0 %copy-start.1 = (f32[8,64,256]{2,1,0:T(8,128)S(1)}, f32[8,64,256]{2,1,0:T(8,128)}, u32[]{:S(2)}) copy-start(f32[8,64,256]{2,1,0:T(8,128)} %get-tuple-element.9.a_ref) | copy-start | bytes 1572868
  16.7 12.3 %copy-start.3 = (f32[1,8]{1,0:T(1,128)S(1)}, f32[1,8]{1,0:T(1,128)}, u32[]{:S(2)}) copy-start(f32[1,8]{1,0:T(1,128)} %counts_ref.1) | copy-start | bytes 100
  16.7 12.3 %copy-start.4 = (f32[1,8]{1,0:T(1,128)S(1)}, f32[1,8]{1,0:T(1,128)}, u32[]{:S(2)}) copy-start(f32[1,8]{1,0:T(1,128)} %var_ref.1) | copy-start | bytes 100
  29.1 6.0 %collective-permute-start.1 = (f32[72,128]{1,0:T(8,128)S(1)}, f32[72,128]{1,0:T(8,128)S(1)}, u32[]{:S(2)}, u32[]{:S(2)}) collective-permute-start(f32[72,128]{1,0:T(8,128)S(1)} %get-tuple-element.12), channel_id=1, source_target_pairs={{0,16},{16,0},{1,17},{17,1},{2,18},{18,2},{3,19},{19,3},{4,20},{20... | collective-permute-start | bytes 110600 | tf_op jit(solution)/shard_map/ppermute | solution.py:300
  61.0 30.2 %copy-start = (bf16[2048,256]{1,0:T(8,128)(2,1)S(1)}, bf16[2048,256]{1,0:T(8,128)(2,1)}, u32[]{:S(2)}) copy-start(bf16[2048,256]{1,0:T(8,128)(2,1)} %states_hbm.3) | copy-start | bytes 3145732
  76.0 15.2 %copy-start.2 = (s32[16]{0:T(128)S(1)}, s32[16]{0:T(128)}, u32[]{:S(2)}) copy-start(s32[16]{0:T(128)} %live_ref.1) | copy-start | bytes 196

commit v7 on v6

--- a/solution.py
+++ b/solution.py
@@ -48,13 +48,14 @@
 
 def term_kernel(
     place_ref, ids_hbm, targets_hbm, live_hbm, states_hbm, tiles_hbm, keep_ref, send_ref,
-    ids_ref, targets_ref, live_ref, states_ref, tiles_ref, spread_ref, next_ref, list_ref, sems,
+    ids_ref, targets_ref, live_ref, states_ref, tiles_ref, order_ref, list_ref, sems,
 ):
     slots, _, blocks = ids_ref.shape
     stored, link_rows, block_rows = tiles_ref.shape
     states_dev, members = states_hbm.shape
-    steps = list_ref.shape[0] // DEPTH
-    empty = blocks * stored
+    entries = slots * blocks
+    steps = (entries + NLB * (DEPTH - 1)) // DEPTH
+    empty = float(blocks * stored)
     copies = [
         pltpu.make_async_copy(there, here, sems.at[i])
         for i, (there, here) in enumerate(
@@ -64,36 +65,36 @@
                 (live_hbm, live_ref),
                 (states_hbm, states_ref.at[pl.ds(0, states_dev)]),
                 (tiles_hbm, tiles_ref),
-                (targets_hbm, spread_ref),
             )
         )
     ]
     for copy in copies:
         copy.start()
-    for k in range(steps * DEPTH):
-        list_ref[k] = empty
     keep_ref[...] = jnp.zeros_like(keep_ref)
     send_ref[...] = jnp.zeros_like(send_ref)
     states_ref[states_dev:, :] = jnp.zeros((block_rows, members), BF16)
-    copies[5].wait()
-    spread = spread_ref[...]
-    first_step = jnp.int32(0)
-    for j in range(NLB):
-        entries = jnp.sum(jnp.where(spread == j, 1.0, 0.0)).astype(jnp.int32)
-        next_ref[j] = first_step * DEPTH
-        first_step += jnp.right_shift(entries + DEPTH - 1, DEPTH.bit_length() - 1)
+    iota = lambda shape, dim: lax.broadcasted_iota(jnp.int32, shape, dim)
+    square = (entries, entries)
+    diagonal = iota(square, 0) == iota(square, 1)
+    before = jnp.where(iota(square, 0) < iota(square, 1), 1.0, 0.0).astype(BF16)
+    column = lambda row: jnp.sum(jnp.where(diagonal, row, 0.0), axis=1, keepdims=True)
+    row = lambda a: jnp.concatenate([a[t] for t in range(slots)], axis=1).astype(F32)
     copies[0].wait()
     copies[1].wait()
-
-    def put(b, carry):
-        for t in range(slots):
-            target = targets_ref[t, 0, b]
-            at = next_ref[target]
-            list_ref[at] = target * 1024 + (b * stored + ids_ref[t, 0, b])
-            next_ref[target] = at + 1
-        return carry
-
-    lax.fori_loop(0, blocks, put, 0, unroll=4)
+    target = row(targets_ref[...])
+    code = target * 1024.0 + row(iota(ids_ref.shape, 2) * stored + ids_ref[...])
+    hits = jnp.where(iota((NLB, entries), 0).astype(F32) == target, 1.0, 0.0)
+    rank = dot(hits.astype(BF16), before)
+    needed = jnp.floor((jnp.sum(hits, axis=1, keepdims=True) + (DEPTH - 1)) * (1.0 / DEPTH)) * DEPTH
+    starts = [jnp.zeros((1, 1), F32)]
+    for j in range(NLB - 1):
+        starts.append(starts[j] + needed[j : j + 1])
+    places = jnp.sum(hits * (rank + jnp.concatenate(starts, axis=0)), axis=0, keepdims=True)
+    put = column(places) == iota((entries, order_ref.shape[1]), 1).astype(F32)
+    order = empty + jnp.sum(jnp.where(put, column(code) - empty, 0.0), axis=0, keepdims=True)
+    order_ref[...] = order.astype(jnp.int32)
+    ordered = pltpu.make_async_copy(order_ref, list_ref, sems.at[5])
+    ordered.start()
 
     copies[2].wait()
     copies[3].wait()
@@ -103,10 +104,11 @@
         living = (position < live_ref[b]).astype(F32).astype(BF16)
         states_ref[rows, :] = states_ref[rows, :] * living
     copies[4].wait()
+    ordered.wait()
 
     def run(by_core):
         def step(i, carry):
-            codes = [list_ref[i * DEPTH + k] for k in range(DEPTH)]
+            codes = [list_ref[0, i * DEPTH + k] for k in range(DEPTH)]
             tiles, states = [], []
             for code in codes:
                 first = pl.multiple_of((jnp.right_shift(code, 5) & 31) * block_rows, block_rows)
@@ -135,7 +137,7 @@
 def term(place, ids, targets, live, states, tiles):
     slots, _, blocks = ids.shape
     states_dev, members = states.shape
-    steps = (slots * blocks + NLB * (DEPTH - 1)) // DEPTH
+    places = -(-(slots * blocks + NLB * (DEPTH - 1)) // 128) * 128
     half = jax.ShapeDtypeStruct((8, 64, members), F32)
     return pl.pallas_call(
         term_kernel,
@@ -143,14 +145,13 @@
         in_specs=[SMEM] + [HBM] * 5,
         out_specs=(VMEM, VMEM),
         scratch_shapes=[
-            pltpu.SMEM(ids.shape, jnp.int32),
-            pltpu.SMEM(ids.shape, jnp.int32),
+            pltpu.VMEM(ids.shape, jnp.int32),
+            pltpu.VMEM(ids.shape, jnp.int32),
             pltpu.SMEM(live.shape, jnp.int32),
             pltpu.VMEM((states_dev + tiles.shape[2], members), BF16),
             pltpu.VMEM(tiles.shape, BF16),
-            pltpu.VMEM(ids.shape, jnp.int32),
-            pltpu.SMEM((NLB,), jnp.int32),
-            pltpu.SMEM((steps * DEPTH,), jnp.int32),
+            pltpu.VMEM((1, places), jnp.int32),
+            pltpu.SMEM((1, places), jnp.int32),
             pltpu.SemaphoreType.DMA((6,)),
         ],
         compiler_params=WHOLE,
@@ -218,11 +219,15 @@
     out_ref[...] = jnp.broadcast_to(total[None], out_ref.shape)
 
 
-def update_kernel(place_ref, live_ref, pieces_ref, states_hbm, out_ref, states_ref, sem):
+def update_kernel(place_ref, live_hbm, pieces_ref, states_hbm, out_ref, states_ref, live_ref, sems):
     own_rows, members = states_ref.shape
     own = pl.ds(pl.multiple_of(link_of(place_ref) * own_rows, own_rows), own_rows)
-    copy = pltpu.make_async_copy(states_hbm.at[own], states_ref, sem)
-    copy.start()
+    copies = (
+        pltpu.make_async_copy(states_hbm.at[own], states_ref, sems.at[0]),
+        pltpu.make_async_copy(live_hbm, live_ref, sems.at[1]),
+    )
+    for copy in copies:
+        copy.start()
     by_core = pieces_ref[...].reshape(pieces_ref.shape[0] // 2, 2, 8, 128)
     first = by_core[0:16, 0].reshape(128, 128)
     last = by_core[0:16, 1].reshape(128, 128)
@@ -255,7 +260,8 @@
     transform = inverse * lax.rsqrt(bound) + mean_weights
     transform += (1.0 - jnp.sum(transform, axis=0, keepdims=True)) * (1.0 / members)
     high, low = halves(transform)
-    copy.wait()
+    for copy in copies:
+        copy.wait()
     own_blocks = own_rows // 128
     position = lax.broadcasted_iota(jnp.int32, (128, members), 0)
     for k in range(own_blocks):
@@ -306,9 +312,13 @@
     return pl.pallas_call(
         update_kernel,
         out_shape=jax.ShapeDtypeStruct((own_rows, members), BF16),
-        in_specs=[SMEM, SMEM, VMEM, HBM],
+        in_specs=[SMEM, HBM, VMEM, HBM],
         out_specs=VMEM,
-        scratch_shapes=[pltpu.VMEM((own_rows, members), BF16), pltpu.SemaphoreType.DMA],
+        scratch_shapes=[
+            pltpu.VMEM((own_rows, members), BF16),
+            pltpu.SMEM(live_counts.shape, jnp.int32),
+            pltpu.SemaphoreType.DMA((2,)),
+        ],
         compiler_params=PARAMS,
         name="update",
     )(place, live_counts, pieces, background)

time: 95.8 us -> 94.3 us (0.984)
  Pallas kernels: 11 us -> 9.48 us
    pallas_call x1, Pallas kernels: 6.12 us -> 5.14 us  [term(): pl.pallas_call(term_kernel, out_shape=(half, half), in_specs=[SMEM] + [HB...]
where the time goes in v7:
time: 94.3 us; the launch traced here: 94 us
  blocking collectives  67.9 us (72%)
  starting transfers between devices  10.7 us (11%)
  Pallas kernels  9.48 us (10%)
  waiting for transfers between devices  4.71 us (5%)
  local copies, waits for them, and re-layouts  1.06 us (1%)
    all_to_all x3, blocking collectives, all_to_all(): return lax.all_to_all(x, axes, split_axis=0, concat_axis=0, tiled=True)  42 us
    all_gather x1, blocking collectives, per_device(): column = lax.all_gather(own, ('zq', 'zp', 'c'))  26 us
    ppermute x1, starting transfers between devices, per_device(): received = lax.ppermute(send, 'c', [(0, 1), (1, 0)])  8.79 us
    pallas_call x1, Pallas kernels, term(): pl.pallas_call(term_kernel, out_shape=(half, half), in_specs=[SMEM] + [HB...  5.14 us
    ppermute x1, waiting for transfers between devices, per_device(): own += lax.ppermute(other, 'zp', [(0, 1), (1, 0)])  4.07 us
    pallas_call x1, Pallas kernels, per_device(): pl.pallas_call(update_kernel, out_shape=jax.ShapeDtypeStruct((own_rows, m...  3.72 us
    ppermute x1, starting transfers between devices, per_device(): own += lax.ppermute(other, 'zp', [(0, 1), (1, 0)])  1.91 us
  transfers between devices with their start and end apart: 2, of which 2 were waited for; matrix products, arithmetic and copies ran while one was open for 0% of the time, Pallas kernels for 0%

profile of v7, /device:TPU:1, one launch (start us, length us, event | category | flops | bytes accessed | tf_op | source)
XLA Modules:
  0.0 94.0 jit_solution(140834343672909857)
XLA Ops:
  0.0 5.1 %term.1 = (f32[8,64,256]{2,1,0:T(8,128)}, f32[8,64,256]{2,1,0:T(8,128)}) custom-call(s32[1]{0:T(128)} %bitcast.place_ref, s32[12,1,16]{2,1,0:T(1,128)} %bitcast.7, s32[12,1,16]{2,1,0:T(1,128)} %bitcast.8, s32[16]{0:T(128)} %live_hbm.3, bf16[2048,256]{1,0:T(8,128)(2,1)} %states_hbm.3, bf16[32,128,128]{2,1,0:T(8,128)(2,1)} %bitcast.6), custom_call_target="tpu_custom_call" | custom-call | tf_op jit(solution)/shard_map/term/pallas_call | solution.py:142
  5.1 8.8 %collective-permute-start = (f32[8,64,256]{2,1,0:T(8,128)}, f32[8,64,256]{2,1,0:T(8,128)S(1)}, u32[]{:S(2)}, u32[]{:S(2)}) collective-permute-start(f32[8,64,256]{2,1,0:T(8,128)} %get-tuple-element.10), channel_id=1, source_target_pairs={{0,4},{4,0},{1,5},{5,1},{2,6},{6,2},{3,7},{7,3},{8,12},{12,8},{9,1... | collective-permute-start | bytes 1572872 | tf_op jit(solution)/shard_map/ppermute | solution.py:295
  13.9 0.0 copy-start.1
  14.0 1.0 %copy-done.1 = f32[8,64,256]{2,1,0:T(8,128)S(1)} copy-done((f32[8,64,256]{2,1,0:T(8,128)S(1)}, f32[8,64,256]{2,1,0:T(8,128)}, u32[]{:S(2)}) %copy-start.1) | copy-done | bytes 524312
  15.0 0.6 collective-permute-done.b_ref
  15.7 0.1 add_kernel.1
  15.7 0.0 copy-start.3
  15.7 0.0 copy-start.4
  15.7 12.2 %all_to_all.15.parts_ref = f32[8,64,256]{2,1,0:T(8,128)S(1)} all-to-all(f32[8,64,256]{2,1,0:T(8,128)S(1)} %add_kernel.1), channel_id=1, replica_groups=mesh['y'=4,'zq'=4,'zp'=2,'zl'=2,'c'=2,'x'=4] {'y','zl'}, dimensions={0} | all-to-all | bytes 1048576 | tf_op jit(solution)/shard_map/all_to_all | solution.py:276
  28.0 0.0 copy-done.3
  28.0 0.0 copy-done.4
  28.0 0.1 rows.1
  28.1 1.9 %collective-permute-start.1 = (f32[72,128]{1,0:T(8,128)S(1)}, f32[72,128]{1,0:T(8,128)S(1)}, u32[]{:S(2)}, u32[]{:S(2)}) collective-permute-start(f32[72,128]{1,0:T(8,128)S(1)} %get-tuple-element.12), channel_id=1, source_target_pairs={{0,16},{16,0},{1,17},{17,1},{2,18},{18,2},{3,19},{19,3},{4,20},{20... | collective-permute-start | bytes 110600 | tf_op jit(solution)/shard_map/ppermute | solution.py:306
  30.0 4.1 %collective-permute-done.1 = f32[72,128]{1,0:T(8,128)S(1)} collective-permute-done((f32[72,128]{1,0:T(8,128)S(1)}, f32[72,128]{1,0:T(8,128)S(1)}, u32[]{:S(2)}, u32[]{:S(2)}) %collective-permute-start.1) | collective-permute-done | bytes 36896 | tf_op jit(solution)/shard_map/ppermute | solution.py:306
  34.1 26.0 %all-gather = f32[1152,128]{1,0:T(8,128)S(1)} all-gather(f32[72,128]{1,0:T(8,128)S(1)} %add.15), channel_id=2, replica_groups=mesh['y'=4,'zq'=4,'zp'=2,'zl'=2,'c'=2,'x'=4] {'zq','zp','c'}, dimensions={0}, use_global_device_ids=true | all-gather | bytes 626688 | tf_op jit(solution)/shard_map/all_gather | solution.py:307
  60.0 0.0 copy-start
  60.1 0.4 gram_kernel.1
  60.5 14.5 %all_to_all.16.parts_ref = f32[32,8,128]{2,1,0:T(8,128)S(1)} all-to-all(f32[32,8,128]{2,1,0:T(8,128)S(1)} %gram_kernel.1), channel_id=1, replica_groups=mesh['y'=4,'zq'=4,'zp'=2,'zl'=2,'c'=2,'x'=4] {'x','y','zl'}, dimensions={0} | all-to-all | bytes 262144 | tf_op jit(solution)/shard_map/all_to_all | solution.py:276
  75.0 0.1 share_kernel.1
  75.0 0.0 copy-start.2
  75.0 15.2 %all_to_all.17.pieces_ref = f32[64,8,128]{2,1,0:T(8,128)S(1)} all-to-all(f32[64,8,128]{2,1,0:T(8,128)S(1)} %share_kernel.1), channel_id=1, replica_groups=mesh['y'=4,'zq'=4,'zp'=2,'zl'=2,'c'=2,'x'=4] {'x','y','zl','c'}, dimensions={0} | all-to-all | bytes 524288 | tf_op jit(solution)/shard_map/all_to_all | solution.py:276
  90.2 0.0 copy-done
  90.2 0.0 copy-done.2
  90.3 3.7 %update.1 = bf16[512,256]{1,0:T(8,128)(2,1)} custom-call(s32[1]{0:T(128)} %bitcast.place_ref, s32[16]{0:T(128)S(1)} %copy-done.2, f32[64,8,128]{2,1,0:T(8,128)S(1)} %all_to_all.17.pieces_ref, bf16[2048,256]{1,0:T(8,128)(2,1)S(1)} %copy-done), custom_call_target="tpu_custom_call" | custom-call | tf_op jit(solution)/shard_map/update/pallas_call | solution.py:312
  (2 shorter events, 0.0 us)
Async XLA Ops:
  5.1 10.5 %collective-permute-start = (f32[8,64,256]{2,1,0:T(8,128)}, f32[8,64,256]{2,1,0:T(8,128)S(1)}, u32[]{:S(2)}, u32[]{:S(2)}) collective-permute-start(f32[8,64,256]{2,1,0:T(8,128)} %get-tuple-element.10), channel_id=1, source_target_pairs={{0,4},{4,0},{1,5},{5,1},{2,6},{6,2},{3,7},{7,3},{8,12},{12,8},{9,1... | collective-permute-start | bytes 1572872 | tf_op jit(solution)/shard_map/ppermute | solution.py:295
  13.9 1.0 %copy-start.1 = (f32[8,64,256]{2,1,0:T(8,128)S(1)}, f32[8,64,256]{2,1,0:T(8,128)}, u32[]{:S(2)}) copy-start(f32[8,64,256]{2,1,0:T(8,128)} %get-tuple-element.9.a_ref) | copy-start | bytes 1572868
  15.7 12.3 %copy-start.3 = (f32[1,8]{1,0:T(1,128)S(1)}, f32[1,8]{1,0:T(1,128)}, u32[]{:S(2)}) copy-start(f32[1,8]{1,0:T(1,128)} %counts_ref.1) | copy-start | bytes 100
  15.7 12.3 %copy-start.4 = (f32[1,8]{1,0:T(1,128)S(1)}, f32[1,8]{1,0:T(1,128)}, u32[]{:S(2)}) copy-start(f32[1,8]{1,0:T(1,128)} %var_ref.1) | copy-start | bytes 100
  28.1 6.0 %collective-permute-start.1 = (f32[72,128]{1,0:T(8,128)S(1)}, f32[72,128]{1,0:T(8,128)S(1)}, u32[]{:S(2)}, u32[]{:S(2)}) collective-permute-start(f32[72,128]{1,0:T(8,128)S(1)} %get-tuple-element.12), channel_id=1, source_target_pairs={{0,16},{16,0},{1,17},{17,1},{2,18},{18,2},{3,19},{19,3},{4,20},{20... | collective-permute-start | bytes 110600 | tf_op jit(solution)/shard_map/ppermute | solution.py:306
  60.0 30.2 %copy-start = (bf16[2048,256]{1,0:T(8,128)(2,1)S(1)}, bf16[2048,256]{1,0:T(8,128)(2,1)}, u32[]{:S(2)}) copy-start(bf16[2048,256]{1,0:T(8,128)(2,1)} %states_hbm.3) | copy-start | bytes 3145732
  75.0 15.2 %copy-start.2 = (s32[16]{0:T(128)S(1)}, s32[16]{0:T(128)}, u32[]{:S(2)}) copy-start(s32[16]{0:T(128)} %live_hbm.3) | copy-start | bytes 196

commit v8 on v7

--- a/solution.py
+++ b/solution.py
@@ -40,6 +40,10 @@
 
 def core_of(place_ref):
     return jnp.right_shift(place_ref[0], 2) & 1
+
+
+def side_of(place_ref):
+    return jnp.right_shift(place_ref[0], 3) & 1
 
 
 def pair_of(place_ref):
@@ -106,6 +110,8 @@
     copies[4].wait()
     ordered.wait()
 
+    pair = pair_of(place_ref)
+
     def run(by_core):
         def step(i, carry):
             codes = [list_ref[0, i * DEPTH + k] for k in range(DEPTH)]
@@ -118,9 +124,9 @@
             target = jnp.right_shift(codes[0], 10)
             chunk = jnp.right_shift(target, 1) * 2
             for g in range(16):
-                q, zl, c = g // 4, (g // 2) % 2, g % 2
-                at = pl.ds(pl.multiple_of((target & 1) * 32 + q * 8, 8), 8)
-                by_core[c][chunk + zl, at, :] += product[g * 8 : g * 8 + 8]
+                h, p, l, c = g // 8, (g // 4) % 2, (g // 2) % 2, g % 2
+                at = pl.ds(pl.multiple_of((target & 1) * 32 + h * 16 + l * 8, 8), 8)
+                by_core[c][chunk + (p ^ pair), at, :] += product[g * 8 : g * 8 + 8]
             return carry
 
         lax.fori_loop(0, steps, step, 0, unroll=steps)
@@ -178,7 +184,7 @@
     rows, members = total.shape
     by_pair = total.reshape(rows // 16, 2, 8, members)
     first, second = (by_pair[:, p].reshape(rows // 2, members) for p in range(2))
-    mine = pair_of(place_ref) == 0
+    mine = side_of(place_ref) == 0
     lane = lax.broadcasted_iota(jnp.int32, (8, 128), 1)
     counts, variance = as_column(counts_ref), as_column(var_ref)
     tail = jnp.where(lane == 0, counts, jnp.where(lane == 1, variance, 0.0))
@@ -198,7 +204,11 @@
         return jnp.concatenate([sum(parts_ref[m, first : first + rows, :] for m in g) for g in groups], axis=0)
 
     left, right = whole(0), whole(rows)
-    tails = jnp.concatenate([parts_ref[m, 2 * rows :, :] for g in groups for m in g], axis=0)
+    tail = lambda g: jnp.concatenate([parts_ref[m, 2 * rows :, :] for m in g], axis=0)
+    straight = side_of(place_ref) == 0
+    tails = jnp.concatenate(
+        [jnp.where(straight, tail(groups[k]), tail(groups[k ^ 1])) for k in range(len(groups))], axis=0
+    )
     counts, variance = tails[:, 0:1], tails[:, 1:2]
     mean = jnp.sum(left + right, axis=1, keepdims=True) * (1.0 / 256.0)
     left, right = left - mean, right - mean
@@ -303,7 +313,7 @@
         compiler_params=PARAMS,
         name="rows",
     )(place, parts, counts_obs, obs_var)
-    own += lax.ppermute(other, "zp", [(0, 1), (1, 0)])
+    own += lax.ppermute(other, ("zq", "zp", "zl"), [(z, (z + (1 if z % 2 else -1)) % 16) for z in range(16)])
     column = lax.all_gather(own, ("zq", "zp", "c"))
     gram = local(gram_kernel, (32, 8, 128), 1, 1)(place, column)
     shared = local(share_kernel, (64, 8, 128), 1)(all_to_all(gram, ("x", "y", "zl")))

time: 94.3 us -> 94.4 us (level)
  starting transfers between devices: 10.7 us -> 16 us
  waiting for transfers between devices: 4.71 us -> 1.98 us
  blocking collectives: 67.9 us -> 65.3 us
    ppermute x1, starting transfers between devices: 1.91 us -> 7.25 us  [per_device(): lax.ppermute(other, ('zq', 'zp', 'zl'), [(z, (z + (1 if z % 2 else -1)) %...]
    all_gather x1, blocking collectives: 26 us -> 23.2 us  [per_device(): column = lax.all_gather(own, ('zq', 'zp', 'c'))]
    ppermute x1, waiting for transfers between devices: 4.07 us -> 1.33 us  [per_device(): lax.ppermute(other, ('zq', 'zp', 'zl'), [(z, (z + (1 if z % 2 else -1)) %...]
where the time goes in v8:
time: 94.4 us; the launch traced here: 94.1 us
  blocking collectives  65.3 us (69%)
  starting transfers between devices  16 us (17%)
  Pallas kernels  9.58 us (10%)
  waiting for transfers between devices  1.98 us (2%)
  local copies, waits for them, and re-layouts  1.06 us (1%)
    all_to_all x3, blocking collectives, all_to_all(): return lax.all_to_all(x, axes, split_axis=0, concat_axis=0, tiled=True)  42.1 us
    all_gather x1, blocking collectives, per_device(): column = lax.all_gather(own, ('zq', 'zp', 'c'))  23.2 us
    ppermute x1, starting transfers between devices, per_device(): received = lax.ppermute(send, 'c', [(0, 1), (1, 0)])  8.78 us
    ppermute x1, starting transfers between devices, per_device(): lax.ppermute(other, ('zq', 'zp', 'zl'), [(z, (z + (1 if z % 2 else -1)) %...  7.25 us
    pallas_call x1, Pallas kernels, term(): pl.pallas_call(term_kernel, out_shape=(half, half), in_specs=[SMEM] + [HB...  5.24 us
    pallas_call x1, Pallas kernels, per_device(): pl.pallas_call(update_kernel, out_shape=jax.ShapeDtypeStruct((own_rows, m...  3.72 us
  transfers between devices with their start and end apart: 2, of which 2 were waited for; matrix products, arithmetic and copies ran while one was open for 0% of the time, Pallas kernels for 0%

profile of v8, /device:TPU:1, one launch (start us, length us, event | category | flops | bytes accessed | tf_op | source)
XLA Modules:
  0.0 94.1 jit_solution(14291710997692314308)
XLA Ops:
  0.0 5.2 %term.1 = (f32[8,64,256]{2,1,0:T(8,128)}, f32[8,64,256]{2,1,0:T(8,128)}) custom-call(s32[1]{0:T(128)} %bitcast.place_ref, s32[12,1,16]{2,1,0:T(1,128)} %bitcast.7, s32[12,1,16]{2,1,0:T(1,128)} %bitcast.8, s32[16]{0:T(128)} %live_hbm.3, bf16[2048,256]{1,0:T(8,128)(2,1)} %states_hbm.3, bf16[32,128,128]{2,1,0:T(8,128)(2,1)} %bitcast.6), custom_call_target="tpu_custom_call" | custom-call | tf_op jit(solution)/shard_map/term/pallas_call | solution.py:148
  5.2 8.8 %collective-permute-start = (f32[8,64,256]{2,1,0:T(8,128)}, f32[8,64,256]{2,1,0:T(8,128)S(1)}, u32[]{:S(2)}, u32[]{:S(2)}) collective-permute-start(f32[8,64,256]{2,1,0:T(8,128)} %get-tuple-element.10), channel_id=1, source_target_pairs={{0,4},{4,0},{1,5},{5,1},{2,6},{6,2},{3,7},{7,3},{8,12},{12,8},{9,1... | collective-permute-start | bytes 1572872 | tf_op jit(solution)/shard_map/ppermute | solution.py:305
  14.0 0.0 copy-start.1
  14.0 1.0 %copy-done.1 = f32[8,64,256]{2,1,0:T(8,128)S(1)} copy-done((f32[8,64,256]{2,1,0:T(8,128)S(1)}, f32[8,64,256]{2,1,0:T(8,128)}, u32[]{:S(2)}) %copy-start.1) | copy-done | bytes 524312
  15.1 0.6 collective-permute-done.b_ref
  15.8 0.1 add_kernel.1
  15.8 0.0 copy-start.3
  15.8 0.0 copy-start.4
  15.8 12.2 %all_to_all.15.parts_ref = f32[8,64,256]{2,1,0:T(8,128)S(1)} all-to-all(f32[8,64,256]{2,1,0:T(8,128)S(1)} %add_kernel.1), channel_id=1, replica_groups=mesh['y'=4,'zq'=4,'zp'=2,'zl'=2,'c'=2,'x'=4] {'y','zl'}, dimensions={0} | all-to-all | bytes 1048576 | tf_op jit(solution)/shard_map/all_to_all | solution.py:286
  28.1 0.0 copy-done.3
  28.1 0.0 copy-done.4
  28.1 0.1 rows.1
  28.2 7.2 %collective-permute-start.1 = (f32[72,128]{1,0:T(8,128)S(1)}, f32[72,128]{1,0:T(8,128)S(1)}, u32[]{:S(2)}, u32[]{:S(2)}) collective-permute-start(f32[72,128]{1,0:T(8,128)S(1)} %get-tuple-element.12), channel_id=1, source_target_pairs={{0,120},{8,16},{16,8},{24,32},{32,24},{40,48},{48,40},{56,64},{64,... | collective-permute-start | bytes 110600 | tf_op jit(solution)/shard_map/ppermute | solution.py:316
  35.4 1.3 %collective-permute-done.1 = f32[72,128]{1,0:T(8,128)S(1)} collective-permute-done((f32[72,128]{1,0:T(8,128)S(1)}, f32[72,128]{1,0:T(8,128)S(1)}, u32[]{:S(2)}, u32[]{:S(2)}) %collective-permute-start.1) | collective-permute-done | bytes 36896 | tf_op jit(solution)/shard_map/ppermute | solution.py:316
  36.8 23.2 %all-gather = f32[1152,128]{1,0:T(8,128)S(1)} all-gather(f32[72,128]{1,0:T(8,128)S(1)} %add.15), channel_id=2, replica_groups=mesh['y'=4,'zq'=4,'zp'=2,'zl'=2,'c'=2,'x'=4] {'zq','zp','c'}, dimensions={0}, use_global_device_ids=true | all-gather | bytes 626688 | tf_op jit(solution)/shard_map/all_gather | solution.py:317
  60.0 0.0 copy-start
  60.0 0.4 gram_kernel.1
  60.4 14.7 %all_to_all.16.parts_ref = f32[32,8,128]{2,1,0:T(8,128)S(1)} all-to-all(f32[32,8,128]{2,1,0:T(8,128)S(1)} %gram_kernel.1), channel_id=1, replica_groups=mesh['y'=4,'zq'=4,'zp'=2,'zl'=2,'c'=2,'x'=4] {'x','y','zl'}, dimensions={0} | all-to-all | bytes 262144 | tf_op jit(solution)/shard_map/all_to_all | solution.py:286
  75.1 0.1 share_kernel.1
  75.1 0.0 copy-start.2
  75.1 15.2 %all_to_all.17.pieces_ref = f32[64,8,128]{2,1,0:T(8,128)S(1)} all-to-all(f32[64,8,128]{2,1,0:T(8,128)S(1)} %share_kernel.1), channel_id=1, replica_groups=mesh['y'=4,'zq'=4,'zp'=2,'zl'=2,'c'=2,'x'=4] {'x','y','zl','c'}, dimensions={0} | all-to-all | bytes 524288 | tf_op jit(solution)/shard_map/all_to_all | solution.py:286
  90.3 0.0 copy-done
  90.4 0.0 copy-done.2
  90.4 3.7 %update.1 = bf16[512,256]{1,0:T(8,128)(2,1)} custom-call(s32[1]{0:T(128)} %bitcast.place_ref, s32[16]{0:T(128)S(1)} %copy-done.2, f32[64,8,128]{2,1,0:T(8,128)S(1)} %all_to_all.17.pieces_ref, bf16[2048,256]{1,0:T(8,128)(2,1)S(1)} %copy-done), custom_call_target="tpu_custom_call" | custom-call | tf_op jit(solution)/shard_map/update/pallas_call | solution.py:322
  (2 shorter events, 0.0 us)
Async XLA Ops:
  5.2 10.5 %collective-permute-start = (f32[8,64,256]{2,1,0:T(8,128)}, f32[8,64,256]{2,1,0:T(8,128)S(1)}, u32[]{:S(2)}, u32[]{:S(2)}) collective-permute-start(f32[8,64,256]{2,1,0:T(8,128)} %get-tuple-element.10), channel_id=1, source_target_pairs={{0,4},{4,0},{1,5},{5,1},{2,6},{6,2},{3,7},{7,3},{8,12},{12,8},{9,1... | collective-permute-start | bytes 1572872 | tf_op jit(solution)/shard_map/ppermute | solution.py:305
  14.0 1.0 %copy-start.1 = (f32[8,64,256]{2,1,0:T(8,128)S(1)}, f32[8,64,256]{2,1,0:T(8,128)}, u32[]{:S(2)}) copy-start(f32[8,64,256]{2,1,0:T(8,128)} %get-tuple-element.9.a_ref) | copy-start | bytes 1572868
  15.8 12.3 %copy-start.3 = (f32[1,8]{1,0:T(1,128)S(1)}, f32[1,8]{1,0:T(1,128)}, u32[]{:S(2)}) copy-start(f32[1,8]{1,0:T(1,128)} %counts_ref.1) | copy-start | bytes 100
  15.8 12.3 %copy-start.4 = (f32[1,8]{1,0:T(1,128)S(1)}, f32[1,8]{1,0:T(1,128)}, u32[]{:S(2)}) copy-start(f32[1,8]{1,0:T(1,128)} %var_ref.1) | copy-start | bytes 100
  28.2 8.6 %collective-permute-start.1 = (f32[72,128]{1,0:T(8,128)S(1)}, f32[72,128]{1,0:T(8,128)S(1)}, u32[]{:S(2)}, u32[]{:S(2)}) collective-permute-start(f32[72,128]{1,0:T(8,128)S(1)} %get-tuple-element.12), channel_id=1, source_target_pairs={{0,120},{8,16},{16,8},{24,32},{32,24},{40,48},{48,40},{56,64},{64,... | collective-permute-start | bytes 110600 | tf_op jit(solution)/shard_map/ppermute | solution.py:316
  60.0 30.4 %copy-start = (bf16[2048,256]{1,0:T(8,128)(2,1)S(1)}, bf16[2048,256]{1,0:T(8,128)(2,1)}, u32[]{:S(2)}) copy-start(bf16[2048,256]{1,0:T(8,128)(2,1)} %states_hbm.3) | copy-start | bytes 3145732
  75.1 15.2 %copy-start.2 = (s32[16]{0:T(128)S(1)}, s32[16]{0:T(128)}, u32[]{:S(2)}) copy-start(s32[16]{0:T(128)} %live_hbm.3) | copy-start | bytes 196

commit v9 on v8

--- a/solution.py
+++ b/solution.py
@@ -29,9 +29,13 @@
     return jnp.dot(a, b, preferred_element_type=F32)
 
 
-def dot3(a, b):
+def dot3(a, b, dot=dot):
     (ah, al), (bh, bl) = a, b
     return dot(ah, bh) + (dot(ah, bl) + dot(al, bh))
+
+
+def over_rows(a, b):
+    return lax.dot_general(a, b, (((0,), (0,)), ((), ())), preferred_element_type=F32)
 
 
 def link_of(place_ref):
@@ -217,8 +221,8 @@
     mine = core_of(place_ref) == 0
     own = jnp.where(mine, left, right)
     half = jnp.where(mine, left[:, :64], left[:, 64:])
-    out_ref[0:16] = dot3(halves(own.T), halves(own * weights)).reshape(16, 8, 128)
-    out_ref[16:24] = dot3(halves(half.T), halves(right * weights)).reshape(8, 8, 128)
+    out_ref[0:16] = dot3(halves(own), halves(own * weights), over_rows).reshape(16, 8, 128)
+    out_ref[16:24] = dot3(halves(half), halves(right * weights), over_rows).reshape(8, 8, 128)
     forcing = [jnp.sum(part * weighted, axis=0, keepdims=True) for part in (left, right)]
     out_ref[24] = jnp.concatenate([*forcing, jnp.zeros((6, 128), F32)], axis=0)
     out_ref[25:] = jnp.zeros((out_ref.shape[0] - 25, 8, 128), F32)

time: 94.4 us -> 94.4 us (level)
  no operation moved by 1% of the time
where the time goes in v9:
time: 94.4 us; the launch traced here: 94.1 us
  blocking collectives  65.3 us (69%)
  starting transfers between devices  16 us (17%)
  Pallas kernels  9.57 us (10%)
  waiting for transfers between devices  1.98 us (2%)
  local copies, waits for them, and re-layouts  1.06 us (1%)
    all_to_all x3, blocking collectives, all_to_all(): return lax.all_to_all(x, axes, split_axis=0, concat_axis=0, tiled=True)  42.1 us
    all_gather x1, blocking collectives, per_device(): column = lax.all_gather(own, ('zq', 'zp', 'c'))  23.2 us
    ppermute x1, starting transfers between devices, per_device(): received = lax.ppermute(send, 'c', [(0, 1), (1, 0)])  8.78 us
    ppermute x1, starting transfers between devices, per_device(): lax.ppermute(other, ('zq', 'zp', 'zl'), [(z, (z + (1 if z % 2 else -1)) %...  7.25 us
    pallas_call x1, Pallas kernels, term(): pl.pallas_call(term_kernel, out_shape=(half, half), in_specs=[SMEM] + [HB...  5.24 us
    pallas_call x1, Pallas kernels, per_device(): pl.pallas_call(update_kernel, out_shape=jax.ShapeDtypeStruct((own_rows, m...  3.72 us
  transfers between devices with their start and end apart: 2, of which 2 were waited for; matrix products, arithmetic and copies ran while one was open for 0% of the time, Pallas kernels for 0%

profile of v9, /device:TPU:1, one launch (start us, length us, event | category | flops | bytes accessed | tf_op | source)
XLA Modules:
  0.0 94.1 jit_solution(9524529306419494731)
XLA Ops:
  0.0 5.2 %term.1 = (f32[8,64,256]{2,1,0:T(8,128)}, f32[8,64,256]{2,1,0:T(8,128)}) custom-call(s32[1]{0:T(128)} %bitcast.place_ref, s32[12,1,16]{2,1,0:T(1,128)} %bitcast.7, s32[12,1,16]{2,1,0:T(1,128)} %bitcast.8, s32[16]{0:T(128)} %live_hbm.3, bf16[2048,256]{1,0:T(8,128)(2,1)} %states_hbm.3, bf16[32,128,128]{2,1,0:T(8,128)(2,1)} %bitcast.6), custom_call_target="tpu_custom_call" | custom-call | tf_op jit(solution)/shard_map/term/pallas_call | solution.py:152
  5.2 8.8 %collective-permute-start = (f32[8,64,256]{2,1,0:T(8,128)}, f32[8,64,256]{2,1,0:T(8,128)S(1)}, u32[]{:S(2)}, u32[]{:S(2)}) collective-permute-start(f32[8,64,256]{2,1,0:T(8,128)} %get-tuple-element.10), channel_id=1, source_target_pairs={{0,4},{4,0},{1,5},{5,1},{2,6},{6,2},{3,7},{7,3},{8,12},{12,8},{9,1... | collective-permute-start | bytes 1572872 | tf_op jit(solution)/shard_map/ppermute | solution.py:309
  14.0 0.0 copy-start.1
  14.0 1.0 %copy-done.1 = f32[8,64,256]{2,1,0:T(8,128)S(1)} copy-done((f32[8,64,256]{2,1,0:T(8,128)S(1)}, f32[8,64,256]{2,1,0:T(8,128)}, u32[]{:S(2)}) %copy-start.1) | copy-done | bytes 524312
  15.1 0.6 collective-permute-done.b_ref
  15.8 0.1 add_kernel.1
  15.8 0.0 copy-start.3
  15.8 0.0 copy-start.4
  15.8 12.2 %all_to_all.15.parts_ref = f32[8,64,256]{2,1,0:T(8,128)S(1)} all-to-all(f32[8,64,256]{2,1,0:T(8,128)S(1)} %add_kernel.1), channel_id=1, replica_groups=mesh['y'=4,'zq'=4,'zp'=2,'zl'=2,'c'=2,'x'=4] {'y','zl'}, dimensions={0} | all-to-all | bytes 1048576 | tf_op jit(solution)/shard_map/all_to_all | solution.py:290
  28.1 0.0 copy-done.3
  28.1 0.0 copy-done.4
  28.1 0.1 rows.1
  28.2 7.2 %collective-permute-start.1 = (f32[72,128]{1,0:T(8,128)S(1)}, f32[72,128]{1,0:T(8,128)S(1)}, u32[]{:S(2)}, u32[]{:S(2)}) collective-permute-start(f32[72,128]{1,0:T(8,128)S(1)} %get-tuple-element.12), channel_id=1, source_target_pairs={{0,120},{8,16},{16,8},{24,32},{32,24},{40,48},{48,40},{56,64},{64,... | collective-permute-start | bytes 110600 | tf_op jit(solution)/shard_map/ppermute | solution.py:320
  35.4 1.3 %collective-permute-done.1 = f32[72,128]{1,0:T(8,128)S(1)} collective-permute-done((f32[72,128]{1,0:T(8,128)S(1)}, f32[72,128]{1,0:T(8,128)S(1)}, u32[]{:S(2)}, u32[]{:S(2)}) %collective-permute-start.1) | collective-permute-done | bytes 36896 | tf_op jit(solution)/shard_map/ppermute | solution.py:320
  36.8 23.2 %all-gather = f32[1152,128]{1,0:T(8,128)S(1)} all-gather(f32[72,128]{1,0:T(8,128)S(1)} %add.15), channel_id=2, replica_groups=mesh['y'=4,'zq'=4,'zp'=2,'zl'=2,'c'=2,'x'=4] {'zq','zp','c'}, dimensions={0}, use_global_device_ids=true | all-gather | bytes 626688 | tf_op jit(solution)/shard_map/all_gather | solution.py:321
  60.0 0.0 copy-start
  60.0 0.4 gram_kernel.1
  60.4 14.7 %all_to_all.16.parts_ref = f32[32,8,128]{2,1,0:T(8,128)S(1)} all-to-all(f32[32,8,128]{2,1,0:T(8,128)S(1)} %gram_kernel.1), channel_id=1, replica_groups=mesh['y'=4,'zq'=4,'zp'=2,'zl'=2,'c'=2,'x'=4] {'x','y','zl'}, dimensions={0} | all-to-all | bytes 262144 | tf_op jit(solution)/shard_map/all_to_all | solution.py:290
  75.1 0.1 share_kernel.1
  75.1 0.0 copy-start.2
  75.1 15.2 %all_to_all.17.pieces_ref = f32[64,8,128]{2,1,0:T(8,128)S(1)} all-to-all(f32[64,8,128]{2,1,0:T(8,128)S(1)} %share_kernel.1), channel_id=1, replica_groups=mesh['y'=4,'zq'=4,'zp'=2,'zl'=2,'c'=2,'x'=4] {'x','y','zl','c'}, dimensions={0} | all-to-all | bytes 524288 | tf_op jit(solution)/shard_map/all_to_all | solution.py:290
  90.3 0.0 copy-done
  90.3 0.0 copy-done.2
  90.3 3.7 %update.1 = bf16[512,256]{1,0:T(8,128)(2,1)} custom-call(s32[1]{0:T(128)} %bitcast.place_ref, s32[16]{0:T(128)S(1)} %copy-done.2, f32[64,8,128]{2,1,0:T(8,128)S(1)} %all_to_all.17.pieces_ref, bf16[2048,256]{1,0:T(8,128)(2,1)S(1)} %copy-done), custom_call_target="tpu_custom_call" | custom-call | tf_op jit(solution)/shard_map/update/pallas_call | solution.py:326
  (2 shorter events, 0.0 us)
Async XLA Ops:
  5.2 10.5 %collective-permute-start = (f32[8,64,256]{2,1,0:T(8,128)}, f32[8,64,256]{2,1,0:T(8,128)S(1)}, u32[]{:S(2)}, u32[]{:S(2)}) collective-permute-start(f32[8,64,256]{2,1,0:T(8,128)} %get-tuple-element.10), channel_id=1, source_target_pairs={{0,4},{4,0},{1,5},{5,1},{2,6},{6,2},{3,7},{7,3},{8,12},{12,8},{9,1... | collective-permute-start | bytes 1572872 | tf_op jit(solution)/shard_map/ppermute | solution.py:309
  14.0 1.0 %copy-start.1 = (f32[8,64,256]{2,1,0:T(8,128)S(1)}, f32[8,64,256]{2,1,0:T(8,128)}, u32[]{:S(2)}) copy-start(f32[8,64,256]{2,1,0:T(8,128)} %get-tuple-element.9.a_ref) | copy-start | bytes 1572868
  15.8 12.3 %copy-start.3 = (f32[1,8]{1,0:T(1,128)S(1)}, f32[1,8]{1,0:T(1,128)}, u32[]{:S(2)}) copy-start(f32[1,8]{1,0:T(1,128)} %counts_ref.1) | copy-start | bytes 100
  15.8 12.3 %copy-start.4 = (f32[1,8]{1,0:T(1,128)S(1)}, f32[1,8]{1,0:T(1,128)}, u32[]{:S(2)}) copy-start(f32[1,8]{1,0:T(1,128)} %var_ref.1) | copy-start | bytes 100
  28.2 8.6 %collective-permute-start.1 = (f32[72,128]{1,0:T(8,128)S(1)}, f32[72,128]{1,0:T(8,128)S(1)}, u32[]{:S(2)}, u32[]{:S(2)}) collective-permute-start(f32[72,128]{1,0:T(8,128)S(1)} %get-tuple-element.12), channel_id=1, source_target_pairs={{0,120},{8,16},{16,8},{24,32},{32,24},{40,48},{48,40},{56,64},{64,... | collective-permute-start | bytes 110600 | tf_op jit(solution)/shard_map/ppermute | solution.py:320
  60.0 30.3 %copy-start = (bf16[2048,256]{1,0:T(8,128)(2,1)S(1)}, bf16[2048,256]{1,0:T(8,128)(2,1)}, u32[]{:S(2)}) copy-start(bf16[2048,256]{1,0:T(8,128)(2,1)} %states_hbm.3) | copy-start | bytes 3145732
  75.1 15.2 %copy-start.2 = (s32[16]{0:T(128)S(1)}, s32[16]{0:T(128)}, u32[]{:S(2)}) copy-start(s32[16]{0:T(128)} %live_hbm.3) | copy-start | bytes 196

commit v10 on v9

--- a/solution.py
+++ b/solution.py
@@ -15,7 +15,7 @@
 VMEM = pl.BlockSpec(memory_space=pltpu.VMEM)
 SMEM = pl.BlockSpec(memory_space=pltpu.SMEM)
 HBM = pl.BlockSpec(memory_space=pltpu.HBM)
-DEPTH = 8
+DEPTH = 4
 WHOLE = pltpu.CompilerParams(vmem_limit_bytes=58 * 2**20)
 PARAMS = pltpu.CompilerParams(vmem_limit_bytes=40 * 2**20)
 

time: 94.4 us -> 94.7 us (level)
  no operation moved by 1% of the time
where the time goes in v10:
time: 94.7 us; the launch traced here: 94.3 us
  blocking collectives  65.3 us (69%)
  starting transfers between devices  16 us (17%)
  Pallas kernels  9.85 us (10%)
  waiting for transfers between devices  1.98 us (2%)
  local copies, waits for them, and re-layouts  1.06 us (1%)
    all_to_all x3, blocking collectives, all_to_all(): return lax.all_to_all(x, axes, split_axis=0, concat_axis=0, tiled=True)  42.1 us
    all_gather x1, blocking collectives, per_device(): column = lax.all_gather(own, ('zq', 'zp', 'c'))  23.2 us
    ppermute x1, starting transfers between devices, per_device(): received = lax.ppermute(send, 'c', [(0, 1), (1, 0)])  8.79 us
    ppermute x1, starting transfers between devices, per_device(): lax.ppermute(other, ('zq', 'zp', 'zl'), [(z, (z + (1 if z % 2 else -1)) %...  7.25 us
    pallas_call x1, Pallas kernels, term(): pl.pallas_call(term_kernel, out_shape=(half, half), in_specs=[SMEM] + [HB...  5.51 us
    pallas_call x1, Pallas kernels, per_device(): pl.pallas_call(update_kernel, out_shape=jax.ShapeDtypeStruct((own_rows, m...  3.72 us
  transfers between devices with their start and end apart: 2, of which 2 were waited for; matrix products, arithmetic and copies ran while one was open for 0% of the time, Pallas kernels for 0%

profile of v10, /device:TPU:1, one launch (start us, length us, event | category | flops | bytes accessed | tf_op | source)
XLA Modules:
  0.0 94.3 jit_solution(5105816376220077989)
XLA Ops:
  0.0 5.5 %term.1 = (f32[8,64,256]{2,1,0:T(8,128)}, f32[8,64,256]{2,1,0:T(8,128)}) custom-call(s32[1]{0:T(128)} %bitcast.place_ref, s32[12,1,16]{2,1,0:T(1,128)} %bitcast.7, s32[12,1,16]{2,1,0:T(1,128)} %bitcast.8, s32[16]{0:T(128)} %live_hbm.3, bf16[2048,256]{1,0:T(8,128)(2,1)} %states_hbm.3, bf16[32,128,128]{2,1,0:T(8,128)(2,1)} %bitcast.6), custom_call_target="tpu_custom_call" | custom-call | tf_op jit(solution)/shard_map/term/pallas_call | solution.py:152
  5.5 8.8 %collective-permute-start = (f32[8,64,256]{2,1,0:T(8,128)}, f32[8,64,256]{2,1,0:T(8,128)S(1)}, u32[]{:S(2)}, u32[]{:S(2)}) collective-permute-start(f32[8,64,256]{2,1,0:T(8,128)} %get-tuple-element.10), channel_id=1, source_target_pairs={{0,4},{4,0},{1,5},{5,1},{2,6},{6,2},{3,7},{7,3},{8,12},{12,8},{9,1... | collective-permute-start | bytes 1572872 | tf_op jit(solution)/shard_map/ppermute | solution.py:309
  14.3 0.0 copy-start.1
  14.3 1.0 %copy-done.1 = f32[8,64,256]{2,1,0:T(8,128)S(1)} copy-done((f32[8,64,256]{2,1,0:T(8,128)S(1)}, f32[8,64,256]{2,1,0:T(8,128)}, u32[]{:S(2)}) %copy-start.1) | copy-done | bytes 524312
  15.4 0.6 collective-permute-done.b_ref
  16.0 0.1 add_kernel.1
  16.1 0.0 copy-start.3
  16.1 0.0 copy-start.4
  16.1 12.2 %all_to_all.15.parts_ref = f32[8,64,256]{2,1,0:T(8,128)S(1)} all-to-all(f32[8,64,256]{2,1,0:T(8,128)S(1)} %add_kernel.1), channel_id=1, replica_groups=mesh['y'=4,'zq'=4,'zp'=2,'zl'=2,'c'=2,'x'=4] {'y','zl'}, dimensions={0} | all-to-all | bytes 1048576 | tf_op jit(solution)/shard_map/all_to_all | solution.py:290
  28.4 0.0 copy-done.3
  28.4 0.0 copy-done.4
  28.4 0.1 rows.1
  28.5 7.2 %collective-permute-start.1 = (f32[72,128]{1,0:T(8,128)S(1)}, f32[72,128]{1,0:T(8,128)S(1)}, u32[]{:S(2)}, u32[]{:S(2)}) collective-permute-start(f32[72,128]{1,0:T(8,128)S(1)} %get-tuple-element.12), channel_id=1, source_target_pairs={{0,120},{8,16},{16,8},{24,32},{32,24},{40,48},{48,40},{56,64},{64,... | collective-permute-start | bytes 110600 | tf_op jit(solution)/shard_map/ppermute | solution.py:320
  35.7 1.3 %collective-permute-done.1 = f32[72,128]{1,0:T(8,128)S(1)} collective-permute-done((f32[72,128]{1,0:T(8,128)S(1)}, f32[72,128]{1,0:T(8,128)S(1)}, u32[]{:S(2)}, u32[]{:S(2)}) %collective-permute-start.1) | collective-permute-done | bytes 36896 | tf_op jit(solution)/shard_map/ppermute | solution.py:320
  37.1 23.2 %all-gather = f32[1152,128]{1,0:T(8,128)S(1)} all-gather(f32[72,128]{1,0:T(8,128)S(1)} %add.15), channel_id=2, replica_groups=mesh['y'=4,'zq'=4,'zp'=2,'zl'=2,'c'=2,'x'=4] {'zq','zp','c'}, dimensions={0}, use_global_device_ids=true | all-gather | bytes 626688 | tf_op jit(solution)/shard_map/all_gather | solution.py:321
  60.3 0.0 copy-start
  60.3 0.4 gram_kernel.1
  60.7 14.7 %all_to_all.16.parts_ref = f32[32,8,128]{2,1,0:T(8,128)S(1)} all-to-all(f32[32,8,128]{2,1,0:T(8,128)S(1)} %gram_kernel.1), channel_id=1, replica_groups=mesh['y'=4,'zq'=4,'zp'=2,'zl'=2,'c'=2,'x'=4] {'x','y','zl'}, dimensions={0} | all-to-all | bytes 262144 | tf_op jit(solution)/shard_map/all_to_all | solution.py:290
  75.3 0.1 share_kernel.1
  75.4 0.0 copy-start.2
  75.4 15.2 %all_to_all.17.pieces_ref = f32[64,8,128]{2,1,0:T(8,128)S(1)} all-to-all(f32[64,8,128]{2,1,0:T(8,128)S(1)} %share_kernel.1), channel_id=1, replica_groups=mesh['y'=4,'zq'=4,'zp'=2,'zl'=2,'c'=2,'x'=4] {'x','y','zl','c'}, dimensions={0} | all-to-all | bytes 524288 | tf_op jit(solution)/shard_map/all_to_all | solution.py:290
  90.6 0.0 copy-done
  90.6 0.0 copy-done.2
  90.6 3.7 %update.1 = bf16[512,256]{1,0:T(8,128)(2,1)} custom-call(s32[1]{0:T(128)} %bitcast.place_ref, s32[16]{0:T(128)S(1)} %copy-done.2, f32[64,8,128]{2,1,0:T(8,128)S(1)} %all_to_all.17.pieces_ref, bf16[2048,256]{1,0:T(8,128)(2,1)S(1)} %copy-done), custom_call_target="tpu_custom_call" | custom-call | tf_op jit(solution)/shard_map/update/pallas_call | solution.py:326
  (2 shorter events, 0.0 us)
Async XLA Ops:
  5.5 10.5 %collective-permute-start = (f32[8,64,256]{2,1,0:T(8,128)}, f32[8,64,256]{2,1,0:T(8,128)S(1)}, u32[]{:S(2)}, u32[]{:S(2)}) collective-permute-start(f32[8,64,256]{2,1,0:T(8,128)} %get-tuple-element.10), channel_id=1, source_target_pairs={{0,4},{4,0},{1,5},{5,1},{2,6},{6,2},{3,7},{7,3},{8,12},{12,8},{9,1... | collective-permute-start | bytes 1572872 | tf_op jit(solution)/shard_map/ppermute | solution.py:309
  14.3 1.0 %copy-start.1 = (f32[8,64,256]{2,1,0:T(8,128)S(1)}, f32[8,64,256]{2,1,0:T(8,128)}, u32[]{:S(2)}) copy-start(f32[8,64,256]{2,1,0:T(8,128)} %get-tuple-element.9.a_ref) | copy-start | bytes 1572868
  16.1 12.3 %copy-start.3 = (f32[1,8]{1,0:T(1,128)S(1)}, f32[1,8]{1,0:T(1,128)}, u32[]{:S(2)}) copy-start(f32[1,8]{1,0:T(1,128)} %counts_ref.1) | copy-start | bytes 100
  16.1 12.3 %copy-start.4 = (f32[1,8]{1,0:T(1,128)S(1)}, f32[1,8]{1,0:T(1,128)}, u32[]{:S(2)}) copy-start(f32[1,8]{1,0:T(1,128)} %var_ref.1) | copy-start | bytes 100
  28.5 8.6 %collective-permute-start.1 = (f32[72,128]{1,0:T(8,128)S(1)}, f32[72,128]{1,0:T(8,128)S(1)}, u32[]{:S(2)}, u32[]{:S(2)}) collective-permute-start(f32[72,128]{1,0:T(8,128)S(1)} %get-tuple-element.12), channel_id=1, source_target_pairs={{0,120},{8,16},{16,8},{24,32},{32,24},{40,48},{48,40},{56,64},{64,... | collective-permute-start | bytes 110600 | tf_op jit(solution)/shard_map/ppermute | solution.py:320
  60.3 30.3 %copy-start = (bf16[2048,256]{1,0:T(8,128)(2,1)S(1)}, bf16[2048,256]{1,0:T(8,128)(2,1)}, u32[]{:S(2)}) copy-start(bf16[2048,256]{1,0:T(8,128)(2,1)} %states_hbm.3) | copy-start | bytes 3145732
  75.4 15.2 %copy-start.2 = (s32[16]{0:T(128)S(1)}, s32[16]{0:T(128)}, u32[]{:S(2)}) copy-start(s32[16]{0:T(128)} %live_hbm.3) | copy-start | bytes 196
